TPU v7x, 128 devices: a whole 4x4x4 slice. The times are simulated.
128 devices in a mesh: energy: 32 (over z, y, x_lo), mom: 4 (over x_hi, core).
Axes of the slice: x: 4 (x_hi: 2, x_lo: 2; x = x_hi * 2 + x_lo), y: 4, z: 4, core: 2. Of those that a mesh axis runs over, the one named last changes fastest.
Arguments:
- green_ret: bfloat16 [16, 64, 2, 512, 512], P('mom', 'energy'), may hold values from -0.25 to 0.25
- broadening: float32 [16, 64, 512], P('mom', 'energy'), may hold values from 0.2 to 2
- coupling: bfloat16 [16, 512, 512], P(None, 'mom'), may hold values from -1.5 to 1.5
- shift_steps: int32 [4], replicated, may hold values from 1 to 2, as said below
- mode_weight: float32 [4], replicated, may hold values from 0.05 to 0.25
- occupation: float32 [4], replicated, may hold values from 0.1 to 2
- momentum_map: int32 [16, 16], replicated, may hold values from 0 to 15, as said below
Outputs:
- self_energy: bfloat16 [16, 64, 2, 512, 512], P(None, 'energy', None, 'mom')
- density: float32 [512, 16, 2, 512], P('energy', 'mom')
Inputs may be any that keep to these rules, and one draw needn't show every extreme that they name: `shift_steps`: some entry equals 2. `momentum_map`: every row and every column holds each of the 16 momentum indices once.
All inputs are finite; a program needn't handle non-finite values.
Results may differ from a plain program's by a relative error of at most 0.02.
Values may be sent and summed in bfloat16 or wider, within the bound.
A program may use at most 192 MiB of HBM per device.

v0:
```python
import math

import jax
import jax.numpy as jnp
from jax import lax
from jax.sharding import PartitionSpec as P

SHIFT_MAX = 2


def with_halo(cells, sides, width):
    for axis, dim in sides:
        count = lax.axis_size(axis)
        ends = count - 1
        head = lax.slice_in_dim(cells, 0, width, axis=dim)
        tail = lax.slice_in_dim(cells, cells.shape[dim] - width, cells.shape[dim], axis=dim)
        cells = jnp.concatenate(
            [
                lax.ppermute(tail, axis, [(i, (i + 1) % count) for i in range(ends)]),
                cells,
                lax.ppermute(head, axis, [((i + 1) % count, i) for i in range(ends)]),
            ],
            axis=dim,
        )
    return cells


def split_up(x, dim, devices):
    before, after = (x.shape[:dim], x.shape[dim + 1 :])
    return jnp.moveaxis(x.reshape(*before, devices, -1, *after), dim, 0)


def cut_rows(length, count):
    unit = 8 if length >= 8 * count else 1
    return [length // unit * k // count * unit for k in range(1, count)]


def laid_out(parts, dim):
    shape = list(parts.shape[1:])
    shape[dim] *= parts.shape[0]
    return jnp.moveaxis(parts, 0, dim).reshape(shape)


def several_exchanges(x, axis, pieces, split_dim, concat_dim):
    parts = split_up(x, split_dim, lax.axis_size(axis))
    widest = max(range(1, max(2, parts.ndim - 1)), key=lambda d: parts.shape[d])
    finished = []
    for share in jnp.split(parts, cut_rows(parts.shape[widest], pieces), axis=widest):
        if share.size:
            finished.append(lax.all_to_all(share, axis, split_axis=0, concat_axis=0, tiled=True))
    return laid_out(jnp.concatenate(finished, axis=widest), concat_dim)


def sum_at_owner(x, axis, dim):
    devices = lax.axis_size(axis)
    parts = lax.all_to_all(split_up(x, dim, devices), axis, 0, 0, tiled=True)
    return jnp.sum(parts.astype(jnp.float32), axis=0)


def scale_columns(green, gamma):
    return (green.astype(jnp.float32) * gamma[:, :, None, None, :]).astype(jnp.bfloat16)


def outer_pair(left, right):
    real_part = jnp.einsum("kecij,kecmj->keim", left, right, preferred_element_type=jnp.float32)
    imag_part = jnp.einsum(
        "keij,kemj->keim", left[:, :, 1], right[:, :, 0], preferred_element_type=jnp.float32
    ) - jnp.einsum(
        "keij,kemj->keim", left[:, :, 0], right[:, :, 1], preferred_element_type=jnp.float32
    )
    return jnp.stack([real_part, imag_part], axis=2)


def complex_product(left, right):
    real_part = jnp.einsum(
        "keij,kejm->keim", left[:, :, 0], right[:, :, 0], preferred_element_type=jnp.float32
    ) - jnp.einsum(
        "keij,kejm->keim", left[:, :, 1], right[:, :, 1], preferred_element_type=jnp.float32
    )
    imag_part = jnp.einsum(
        "keij,kejm->keim", left[:, :, 0], right[:, :, 1], preferred_element_type=jnp.float32
    ) + jnp.einsum(
        "keij,kejm->keim", left[:, :, 1], right[:, :, 0], preferred_element_type=jnp.float32
    )
    return jnp.stack([real_part, imag_part], axis=2)


def shifted_sum(padded, shift_steps, mode_weight, occupation):
    count_energy = padded.shape[1] - 2 * SHIFT_MAX
    total = jnp.zeros((padded.shape[0], count_energy) + padded.shape[2:], jnp.float32)
    for branch in range(shift_steps.shape[0]):
        offset = shift_steps[branch]
        above = lax.dynamic_slice_in_dim(padded, SHIFT_MAX + offset, count_energy, 1).astype(
            jnp.float32
        )
        below = lax.dynamic_slice_in_dim(padded, SHIFT_MAX - offset, count_energy, 1).astype(
            jnp.float32
        )
        total = total + mode_weight[branch] * (
            (occupation[branch] + 1.0) * above + occupation[branch] * below
        )
    return total.astype(jnp.bfloat16)


def convolve_blocks(make_block, coupling, momentum_map, shape):
    rows_tile = shape[3]
    block_rows = math.gcd(16, rows_tile)
    block_count = rows_tile // block_rows

    def one_block(position, result):
        start = position * block_rows
        source = make_block(start, block_rows)
        weights = lax.dynamic_slice_in_dim(coupling, start, block_rows, 1).astype(jnp.float32)
        total = jnp.zeros(source.shape, jnp.float32)
        for qpoint in range(source.shape[0]):
            donor = jnp.take(source, momentum_map[:, qpoint], axis=0).astype(jnp.float32)
            total = total + weights[qpoint][None, None, None] * donor
        return lax.dynamic_update_slice_in_dim(result, total.astype(jnp.bfloat16), start, 3)

    return lax.fori_loop(0, block_count, one_block, jnp.zeros(shape, jnp.bfloat16))


def on_device(green_ret, broadening, coupling, shift_steps, mode_weight, occupation, momentum_map):
    scaled = scale_columns(green_ret, broadening)
    lesser = outer_pair(scaled, green_ret).astype(jnp.bfloat16)
    local_k = green_ret.shape[0]
    norb = green_ret.shape[-1]
    all_k = local_k * lax.axis_size("mom")
    tile_shape = (all_k, green_ret.shape[1], 2, norb // lax.axis_size("mom"), norb)
    padded = with_halo(lesser, (("energy", 1),), SHIFT_MAX)
    source = shifted_sum(padded, shift_steps, mode_weight, occupation)
    tiles = several_exchanges(source, "mom", 2, 3, 0)

    def make_block(start, count):
        return lax.dynamic_slice_in_dim(tiles, start, count, 3)

    self_energy = convolve_blocks(make_block, coupling, momentum_map, tile_shape)
    home = several_exchanges(self_energy, "mom", 2, 0, 3)
    total_energies = green_ret.shape[1] * lax.axis_size("energy")
    mixed = (complex_product(green_ret, home) + scaled.astype(jnp.float32)).astype(jnp.bfloat16)
    real_part = jnp.einsum("kecij,kecmj->ikm", mixed, green_ret, preferred_element_type=jnp.float32)
    imag_part = jnp.einsum(
        "keij,kemj->ikm", mixed[:, :, 1], green_ret[:, :, 0], preferred_element_type=jnp.float32
    ) - jnp.einsum(
        "keij,kemj->ikm", mixed[:, :, 0], green_ret[:, :, 1], preferred_element_type=jnp.float32
    )
    density = sum_at_owner(
        (jnp.stack([real_part, imag_part], axis=2) / total_energies).astype(jnp.bfloat16),
        "energy",
        0,
    )
    return (self_energy, density)


def solution(mesh):
    return jax.shard_map(
        on_device,
        mesh=mesh,
        in_specs=(
            P("mom", "energy", None, None, None),
            P("mom", "energy", None),
            P(None, "mom", None),
            P(),
            P(),
            P(),
            P(),
        ),
        out_specs=(P(None, "energy", None, "mom", None), P("energy", "mom", None, None)),
        check_vma=False,
    )
```

profile of v0, /device:TPU:0, one launch (start us, length us, event | category | flops | bytes accessed | tf_op | source)
XLA Modules:
  0.0 1179.4 jit_solution(12209074839195449831)
XLA Ops:
  9.3 11.0 fusion.21
  75.9 160.5 %collective-permute-done = bf16[4,2,2,512,512]{4,3,0,1,2:T(8,128)(2,1)} collective-permute-done((bf16[4,2,2,512,512]{4,3,0,1,2:T(8,128)(2,1)}, bf16[4,2,2,512,512]{4,3,0,1,2:T(8,128)(2,1)}, u32[]{:S(2)}, u32[]{:S(2)}) %collective-permute-start) | collective-permute-done | bytes 8388640 | tf_op jit(solution)/shard_map/ppermute | solution.py:19
  236.4 181.8 %collective-permute-done.1 = bf16[4,2,2,512,512]{4,3,0,1,2:T(8,128)(2,1)} collective-permute-done((bf16[4,2,2,512,512]{4,3,0,1,2:T(8,128)(2,1)}, bf16[4,2,2,512,512]{4,3,0,1,2:T(8,128)(2,1)}, u32[]{:S(2)}, u32[]{:S(2)}) %collective-permute-start.1) | collective-permute-done | bytes 8388640 | tf_op jit(solution)/shard_map/ppermute | solution.py:21
  418.2 17.5 %pad_maximum_fusion = bf16[4,6,2,512,512]{4,3,0,1,2:T(8,128)(2,1)} fusion(bf16[4,2,2,512,512]{4,3,0,1,2:T(8,128)(2,1)} %collective-permute-done.1, bf16[4,2,1,512,512]{4,3,0,1,2:T(8,128)(2,1)} %copy-done.1, bf16[4,2,1,512,512]{4,3,0,1,2:T(8,128)(2,1)} %bitcast.190, bf16[4,2,2,512,512]{4,3,0,1,2:T(8,128)(2,1)} %collective-permute-done), kind=kLoop, calls=%fused_computation.84 | loop fusion | flops 37748736 | bytes 50331648 | tf_op jit(solution)/shard_map/concatenate | solution.py:17
  435.7 39.3 %add_convert_fusion.1 = bf16[4,2,2,512,512]{4,3,0,1,2:T(8,128)(2,1)} fusion(bf16[4,6,2,512,512]{4,3,0,1,2:T(8,128)(2,1)} %pad_maximum_fusion, s32[]{:T(128)S(6)} %select_n.47, f32[]{:T(128)} %bitcast.58, s32[]{:T(128)S(6)} %select_n.46, f32[]{:T(128)S(6)} %add.281, f32[]{:T(128)} %bitcast.57, s32[]{:T(128)S(6)} %select_n.45, f32[]{:T(128)} %bitcast.52, ...), kind=kLoop, calls=%fused_computation.87 | loop fusion | flops 117440512 | bytes 75497552 | tf_op jit(solution)/shard_map/convert_element_type | solution.py:102
  487.8 54.0 %all_to_all.25 = bf16[4,4,2,2,64,512]{5,4,2,1,3,0:T(8,128)(2,1)} all-to-all(bf16[4,4,2,2,64,512]{5,4,2,1,3,0:T(8,128)(2,1)S(1)} %get-tuple-element.223), channel_id=1, replica_groups=mesh['energy'=32,'mom'=4] {'mom'}, dimensions={0} | all-to-all | bytes 8388608 | tf_op jit(solution)/shard_map/all_to_all | solution.py:50
  546.7 49.7 %all-to-all-done.1 = bf16[4,4,2,2,64,512]{5,4,2,1,3,0:T(8,128)(2,1)} async-done(((bf16[4,4,2,2,64,512]{5,4,2,1,3,0:T(8,128)(2,1)}), bf16[4,4,2,2,64,512]{5,4,2,1,3,0:T(8,128)(2,1)}, u32[]{:S(2)}, u32[]{:S(2)}) %all-to-all-start.1) | async-done | bytes 4194336 | tf_op jit(solution)/shard_map/all_to_all | solution.py:50
  616.3 285.5 %while.13 = (s32[]{:T(128)}, bf16[16,2,2,128,512]{4,3,2,1,0:T(8,128)(2,1)}, bf16[16,128,512]{2,1,0:T(8,128)(2,1)}, bf16[16,2,2,128,512]{4,3,2,1,0:T(8,128)(2,1)}...) while((s32[]{:T(128)}, bf16[16,2,2,128,512]{4,3,2,1,0:T(8,128)(2,1)}, ...), condition=%wide.region_1.3_spmd, body=%wide.region_0.2_spmd.sunk | while | flops 33703428 | bytes 55906968 | solution.py:120
  642.4 9.5 fusion.39
  678.1 9.5 fusion.39
  713.8 9.5 fusion.39
  749.5 9.5 fusion.39
  785.2 9.5 fusion.39
  820.9 9.5 fusion.39
  856.6 9.5 fusion.39
  892.3 9.5 fusion.39
  905.7 53.1 %all_to_all.26 = bf16[4,4,2,2,64,512]{5,4,3,2,1,0:T(8,128)(2,1)} all-to-all(bf16[4,4,2,2,64,512]{5,4,3,2,1,0:T(8,128)(2,1)S(1)} %get-tuple-element.221), channel_id=1, replica_groups=mesh['energy'=32,'mom'=4] {'mom'}, dimensions={0} | all-to-all | bytes 8388608 | tf_op jit(solution)/shard_map/all_to_all | solution.py:50
  958.8 53.3 %all_to_all.27 = bf16[4,4,2,2,64,512]{5,4,3,2,1,0:T(8,128)(2,1)} all-to-all(bf16[4,4,2,2,64,512]{5,4,3,2,1,0:T(8,128)(2,1)S(1)} %get-tuple-element.222), channel_id=1, replica_groups=mesh['energy'=32,'mom'=4] {'mom'}, dimensions={0} | all-to-all | bytes 8388608 | tf_op jit(solution)/shard_map/all_to_all | solution.py:50
  1019.8 13.7 %copy.51 = bf16[4,2,2,4,128,512]{4,3,5,1,0,2:T(4,128)(2,1)} copy(bf16[4,2,2,4,128,512]{5,4,2,1,0,3:T(8,128)(2,1)} %maximum_bitcast_fusion) | data formatting | bytes 16777216 | tf_op jit(solution)/shard_map/transpose | solution.py:41
  1033.5 13.1 %reshape.78 = bf16[4,2,2,512,512]{3,4,1,0,2:T(8,128)(2,1)} reshape(bf16[4,2,2,4,128,512]{4,3,5,1,0,2:T(4,128)(2,1)} %copy.51) | data formatting | bytes 16777216 | tf_op jit(solution)/shard_map/reshape | solution.py:41
  1063.8 10.4 subtract_bitcast_fusion
  1074.3 10.4 add_bitcast_fusion
  1100.0 9.6 fusion.22
  1118.1 59.3 %all_to_all.28 = bf16[32,16,4,2,512]{4,1,2,3,0:T(8,128)(2,1)S(1)} all-to-all(bf16[32,16,4,2,512]{4,1,2,3,0:T(8,128)(2,1)S(1)} %fusion.2), channel_id=1, replica_groups=mesh['energy'=32,'mom'=4] {'energy'}, dimensions={0} | all-to-all | bytes 8388608 | tf_op jit(solution)/shard_map/all_to_all | solution.py:56
  (280 shorter events, 352.4 us)
Async XLA Ops:
  0.6 8.7 copy-start.3
  0.6 19.7 %slice-start = ((s8[8388608]{0:T(1024)(128)(4,1)}), s8[4194304]{0:T(1024)(128)(4,1)S(1)}, s32[]{:S(2)}) async-start(s8[8388608]{0:T(1024)(128)(4,1)} %bitcast.185), calls=%async_computation.5 | async-start | bytes 8388608
  9.3 11.0 slice-start.1
  45.0 7.9 copy-start.1
  45.0 16.4 %copy-start.6 = (s32[4]{0:T(128)S(1)}, s32[4]{0:T(128)}, u32[]{:S(2)}) copy-start(s32[4]{0:T(128)} %param.14) | copy-start | bytes 52
  45.0 26.9 %copy-start.7 = (f32[4]{0:T(128)S(1)}, f32[4]{0:T(128)}, u32[]{:S(2)}) copy-start(f32[4]{0:T(128)} %param.16) | copy-start | bytes 52
  45.0 30.2 %copy-start.8 = (f32[4]{0:T(128)S(1)}, f32[4]{0:T(128)}, u32[]{:S(2)}) copy-start(f32[4]{0:T(128)} %param.15) | copy-start | bytes 52
  52.9 183.5 %collective-permute-start = (bf16[4,2,2,512,512]{4,3,0,1,2:T(8,128)(2,1)}, bf16[4,2,2,512,512]{4,3,0,1,2:T(8,128)(2,1)}, u32[]{:S(2)}, u32[]{:S(2)}) collective-permute-start(bf16[4,2,2,512,512]{4,3,0,1,2:T(8,128)(2,1)} %pad_maximum_fusion.1), channel_id=1, source_target_pairs={{0,4},{4,8},{8,12},{12,16},{16,20},{20,24},{24,28},{28,32},{32,36}... | collective-permute-start | bytes 25165832 | tf_op jit(solution)/shard_map/ppermute | solution.py:19
  59.7 358.5 %collective-permute-start.1 = (bf16[4,2,2,512,512]{4,3,0,1,2:T(8,128)(2,1)}, bf16[4,2,2,512,512]{4,3,0,1,2:T(8,128)(2,1)}, u32[]{:S(2)}, u32[]{:S(2)}) collective-permute-start(bf16[4,2,2,512,512]{4,3,0,1,2:T(8,128)(2,1)} %pad_maximum_fusion.1), channel_id=1, source_target_pairs={{4,0},{8,4},{12,8},{16,12},{20,16},{24,20},{28,24},{32,28},{36,32}... | collective-permute-start | bytes 25165832 | tf_op jit(solution)/shard_map/ppermute | solution.py:21
  487.8 58.8 %copy-start.5 = (s32[16,16]{1,0:T(8,128)S(1)}, s32[16,16]{1,0:T(8,128)}, u32[]{:S(2)}) copy-start(s32[16,16]{1,0:T(8,128)} %param.17) | copy-start | bytes 3076
  541.8 54.6 %all-to-all-start.1 = ((bf16[4,4,2,2,64,512]{5,4,2,1,3,0:T(8,128)(2,1)}), bf16[4,4,2,2,64,512]{5,4,2,1,3,0:T(8,128)(2,1)}, u32[]{:S(2)}, u32[]{:S(2)}) async-start(bf16[4,4,2,2,64,512]{5,4,2,1,3,0:T(8,128)(2,1)} %get-tuple-element.224), calls=%async_computation.1 | async-start | bytes 8388608 | tf_op jit(solution)/shard_map/all_to_all | solution.py:50
  1046.6 9.2 copy-start
  1046.6 17.2 %slice-start.2 = ((s8[8388608]{0:T(1024)(128)(4,1)}), s8[4194304]{0:T(1024)(128)(4,1)S(1)}, s32[]{:S(2)}) async-start(s8[8388608]{0:T(1024)(128)(4,1)} %bitcast.187), calls=%async_computation.7 | async-start | bytes 8388608
  1055.9 8.0 slice-start.3
  1074.3 10.4 copy-start.4
  1092.4 3.3 copy-start.2
where the time goes:
time: 1190 us; the launch traced here: 1180 us
  waiting for transfers between devices  392 us (33%)
  local copies, waits for them, and re-layouts  272 us (23%)
  blocking collectives  220 us (18%)
  other arithmetic  184 us (15%)
  matrix products  84 us (7%)
  between operations  13.5 us (1%)
  starting transfers between devices  13.3 us (1%)
    gather x128, local copies, waits for them, and re-layouts, one_block(): jnp.take(source, momentum_map[:, qpoint], axis=0).astype(jnp.float32)  189 us
    ppermute x1, waiting for transfers between devices, with_halo(): lax.ppermute(head, axis, [((i + 1) % count, i) for i in range(ends)])  182 us
    ppermute x1, waiting for transfers between devices, with_halo(): lax.ppermute(tail, axis, [(i, (i + 1) % count) for i in range(ends)])  161 us
    all_to_all x3, blocking collectives, several_exchanges(): lax.all_to_all(share, axis, split_axis=0, concat_axis=0, tiled=True)  160 us
    dynamic_update_slice x8, other arithmetic, one_block(): lax.dynamic_update_slice_in_dim(result, total.astype(jnp.bfloat16), start...  76 us
    all_to_all x1, blocking collectives, sum_at_owner(): parts = lax.all_to_all(split_up(x, dim, devices), axis, 0, 0, tiled=True)  59.3 us
    all_to_all x1, waiting for transfers between devices, several_exchanges(): lax.all_to_all(share, axis, split_axis=0, concat_axis=0, tiled=True)  49.7 us
    convert_element_type x1, other arithmetic, shifted_sum(): return total.astype(jnp.bfloat16)  39.3 us
  transfers between devices with their start and end apart: 3, of which 3 were waited for; matrix products, arithmetic and copies ran while one was open for 0% of the time, Pallas kernels for 0%

commit v1 on v0

v1 whole, which is shorter than its diff:
```python
import functools

import jax
import jax.numpy as jnp
from jax import lax
from jax.experimental import pallas as pl
from jax.experimental.pallas import tpu as pltpu
from jax.sharding import PartitionSpec as P

SHIFT_MAX = 2
BOTH = ("energy", "mom")
MIB = 1 << 20
NT = (((1,), (1,)), ((), ()))


def dot_nt(left, right):
    return lax.dot_general(left, right, NT, preferred_element_type=jnp.float32)


def dot_nn(left, right):
    return jnp.dot(left, right, preferred_element_type=jnp.float32)


def scale(block, gamma):
    return (block.astype(jnp.float32) * gamma).astype(jnp.bfloat16)


def lesser_kernel(half, green, gamma, out):
    g_re = green[0, 0, 0]
    g_im = green[0, 0, 1]
    gam = gamma[0, 0]
    wide_re = g_re.astype(jnp.float32)
    wide_im = g_im.astype(jnp.float32)
    less = (wide_re - wide_im).astype(jnp.bfloat16)
    more = (wide_re + wide_im).astype(jnp.bfloat16)
    total = dot_nt(scale(g_re, gam), less) + dot_nt(scale(g_im, gam), more)
    out[0, 0] = total.astype(jnp.bfloat16)


def packed_lesser(half, green, gamma):
    energies, norb = green.shape[1], green.shape[-1]
    count = green.shape[0] // 2
    return pl.pallas_call(
        lesser_kernel,
        grid_spec=pltpu.PrefetchScalarGridSpec(
            num_scalar_prefetch=1,
            grid=(count, energies),
            in_specs=[
                pl.BlockSpec((1, 1, 2, norb, norb), lambda k, e, h: (h[0] * count + k, e, 0, 0, 0)),
                pl.BlockSpec((1, 1, 1, norb), lambda k, e, h: (h[0] * count + k, e, 0, 0)),
            ],
            out_specs=pl.BlockSpec((1, 1, norb, norb), lambda k, e, h: (k, e, 0, 0)),
        ),
        out_shape=jax.ShapeDtypeStruct((count, energies, norb, norb), jnp.bfloat16),
        compiler_params=pltpu.CompilerParams(vmem_limit_bytes=32 * MIB),
        cost_estimate=pl.CostEstimate(
            flops=4 * count * energies * norb**3,
            bytes_accessed=6 * count * energies * norb**2,
            transcendentals=0,
        ),
        name="lesser",
    )(half, green, gamma)


def shift_kernel(place, weights, own, got, own_halo, got_halo, out_own, out_other):
    rows = own.shape[2]
    step = 16

    def run(first, second, third, fourth, outs):
        def slab(i, carry):
            at = pl.ds(pl.multiple_of(i * step, step), step)
            levels = [
                ref[0, e, at, :].astype(jnp.float32)
                for ref in (first, second, third, fourth)
                for e in range(2)
            ]
            for o in range(4):
                total = weights[0] * levels[o + 3] + weights[1] * levels[o + 4]
                total = total + weights[2] * levels[o + 1] + weights[3] * levels[o]
                outs[o // 2][0, o % 2, at, :] = total.astype(jnp.bfloat16)
            return carry

        lax.fori_loop(0, rows // step, slab, 0)

    @pl.when(place[0] == 0)
    def _():
        run(got_halo, own, got, own_halo, (out_own, out_other))

    @pl.when(place[0] != 0)
    def _():
        run(own_halo, got, own, got_halo, (out_other, out_own))


def shifted(place, weights, own, got, own_halo, got_halo):
    count, energies, norb, _ = own.shape
    rows = norb // 4
    block = pl.BlockSpec((1, energies, rows, norb), lambda k, i, p, w: (k, 0, i, 0))
    out = jax.ShapeDtypeStruct(own.shape, jnp.bfloat16)
    return pl.pallas_call(
        shift_kernel,
        grid_spec=pltpu.PrefetchScalarGridSpec(
            num_scalar_prefetch=2,
            grid=(count, norb // rows),
            in_specs=[block] * 4,
            out_specs=[block] * 2,
        ),
        out_shape=[out, out],
        compiler_params=pltpu.CompilerParams(vmem_limit_bytes=32 * MIB),
        cost_estimate=pl.CostEstimate(
            flops=32 * count * norb**2, bytes_accessed=24 * count * norb**2, transcendentals=0
        ),
        name="shifted",
    )(place, weights, own, got, own_halo, got_halo)


def convolve_kernel(tiles, table, *refs):
    n = 8
    rows_of, cols_of = refs[:n], refs[n : 2 * n]
    coup, coup_t, out, along, across = refs[2 * n :]
    targets, _, _, height, norb = out.shape
    group = pl.program_id(0) * targets

    def spread(sources, factor, at, store):
        acc = [[None, None] for _ in range(targets)]
        for quad in range(n // 2):
            donors = [(s, kk) for s in (2 * quad, 2 * quad + 1) for kk in range(2)]
            held = [[sources[s][kk, e, at[0], at[1]] for e in range(2)] for s, kk in donors]
            for t in range(targets):
                pick = [table[(group + t) * 2 * n + 4 * quad + d] for d in range(4)]
                c = [factor[0, q, at[0], at[1]] for q in pick]
                for e in range(2):
                    part = (c[0] * held[0][e] + c[1] * held[1][e]) + (
                        c[2] * held[2][e] + c[3] * held[3][e]
                    )
                    part = part.astype(jnp.float32)
                    acc[t][e] = part if acc[t][e] is None else acc[t][e] + part
        for t in range(targets):
            for e in range(2):
                store[t, e, at[0], at[1]] = acc[t][e]

    def over_rows(i, carry):
        r, l = i // 2, i % 2
        at = (
            pl.ds(pl.multiple_of(r * 16, 16), 16),
            pl.ds(pl.multiple_of(l * (norb // 2), norb // 2), norb // 2),
        )
        spread(rows_of, coup, at, along)
        return carry

    def over_cols(i, carry):
        at = (pl.ds(pl.multiple_of(i * 32, 32), 32), slice(None))
        spread(cols_of, coup_t, at, across)
        return carry

    lax.fori_loop(0, height // 16 * 2, over_rows, 0)
    lax.fori_loop(0, norb // 32, over_cols, 0)

    def finish(i, carry):
        t, e = i // 2, i % 2
        for b in range(norb // height):
            span = slice(b * height, (b + 1) * height)
            u = along[t, e, :, span]
            v = across[t, e, span, :].T
            out[t, e, 0, :, span] = (u + v).astype(jnp.bfloat16)
            out[t, e, 1, :, span] = (u - v).astype(jnp.bfloat16)
        return carry

    lax.fori_loop(0, targets * 2, finish, 0)


def convolved(tiles, table, sources, coup, coup_t, groups, steps, targets, name):
    norb = sources[0].shape[-1]
    height = coup.shape[2]
    points = coup.shape[1]
    row_block = pl.BlockSpec((2, 2, height, norb), lambda g, i, t, q: (0, 0, t[i], 0))
    col_block = pl.BlockSpec((2, 2, norb, height), lambda g, i, t, q: (0, 0, 0, t[i]))
    slot = lambda g, i, t, q: (t[steps + i], 0, 0, 0)
    return pl.pallas_call(
        convolve_kernel,
        grid_spec=pltpu.PrefetchScalarGridSpec(
            num_scalar_prefetch=2,
            grid=(groups, steps),
            in_specs=[row_block] * 8
            + [col_block] * 8
            + [
                pl.BlockSpec((1, points, height, norb), slot),
                pl.BlockSpec((1, points, norb, height), slot),
            ],
            out_specs=pl.BlockSpec((targets, 2, 2, height, norb), lambda g, i, t, q: (g, 0, 0, i, 0)),
            scratch_shapes=[
                pltpu.VMEM((targets, 2, height, norb), jnp.float32),
                pltpu.VMEM((targets, 2, norb, height), jnp.float32),
            ],
        ),
        out_shape=jax.ShapeDtypeStruct(
            (groups * targets, 2, 2, steps * height, norb), jnp.bfloat16
        ),
        compiler_params=pltpu.CompilerParams(vmem_limit_bytes=56 * MIB),
        cost_estimate=pl.CostEstimate(
            flops=8 * groups * steps * targets * points * height * norb,
            bytes_accessed=12 * MIB * steps + 2 * MIB * steps * groups,
            transcendentals=0,
        ),
        name=name,
    )(tiles, table, *sources, *sources, coup, coup_t)


def density_kernel(inverse, green, gamma, sigma, out):
    d_re = d_im = None
    for e in range(green.shape[1]):
        g_re, g_im = green[0, e, 0], green[0, e, 1]
        s_re, s_im = sigma[0, e, 0], sigma[0, e, 1]
        gam = gamma[0, e]
        m_re = dot_nn(g_re, s_re) - dot_nn(g_im, s_im) + scale(g_re, gam).astype(jnp.float32)
        m_im = dot_nn(g_re, s_im) + dot_nn(g_im, s_re) + scale(g_im, gam).astype(jnp.float32)
        m_re, m_im = m_re.astype(jnp.bfloat16), m_im.astype(jnp.bfloat16)
        one = dot_nt(m_re, g_re) + dot_nt(m_im, g_im)
        two = dot_nt(m_im, g_re) - dot_nt(m_re, g_im)
        d_re = one if d_re is None else d_re + one
        d_im = two if d_im is None else d_im + two
    out[0, 0] = (d_re * inverse).astype(jnp.bfloat16)
    out[0, 1] = (d_im * inverse).astype(jnp.bfloat16)


def partial_density(green, gamma, sigma, inverse):
    count, energies, _, norb, _ = green.shape
    whole = pl.BlockSpec((1, energies, 2, norb, norb), lambda k: (k, 0, 0, 0, 0))
    return pl.pallas_call(
        functools.partial(density_kernel, inverse),
        grid=(count,),
        in_specs=[
            whole,
            pl.BlockSpec((1, energies, 1, norb), lambda k: (k, 0, 0, 0)),
            whole,
        ],
        out_specs=pl.BlockSpec((1, 2, norb, norb), lambda k: (k, 0, 0, 0)),
        out_shape=jax.ShapeDtypeStruct((count, 2, norb, norb), jnp.bfloat16),
        compiler_params=pltpu.CompilerParams(vmem_limit_bytes=48 * MIB),
        cost_estimate=pl.CostEstimate(
            flops=16 * count * energies * norb**3,
            bytes_accessed=(8 * energies + 4) * count * norb**2,
            transcendentals=0,
        ),
        name="density",
    )(green, gamma, sigma)


def on_device(green, broadening, coupling, shift_steps, mode_weight, occupation, momentum_map):
    n_energy, n_mom = lax.axis_size("energy"), lax.axis_size("mom")
    pairs = n_energy // 2
    local_k = green.shape[0]
    half = local_k // 2
    points = momentum_map.shape[1]
    energy, mom = lax.axis_index("energy"), lax.axis_index("mom")
    x_lo = energy % 2

    def flip(x, lo, mo):
        perm = [
            (e * n_mom + m, (e ^ lo) * n_mom + (m ^ mo))
            for e in range(n_energy)
            for m in range(n_mom)
        ]
        return lax.ppermute(x, BOTH, perm)

    def along_pairs(x, step_of_low):
        moves = []
        for j in range(pairs):
            for lo in range(2):
                to = j + (step_of_low if lo == 0 else -step_of_low)
                if 0 <= to < pairs:
                    moves.append((2 * j + lo, 2 * to + lo))
        return lax.ppermute(x, "energy", moves)

    gamma = broadening[:, :, None, :]
    place = x_lo.astype(jnp.int32)[None]

    sent = packed_lesser(1 - place, green, gamma)
    got = flip(sent, 1, 0)
    coup_b = flip(coupling, 1, 2)
    coup_c = flip(coupling, 0, 1)
    own = packed_lesser(place, green, gamma)
    own_halo = along_pairs(own, -1)
    got_halo = along_pairs(got, 1)
    coup_bc = flip(coup_b, 0, 1)

    def weight_of(step, factor):
        return 0.5 * jnp.sum(jnp.where(shift_steps == step, mode_weight * factor, 0.0))

    weights = jnp.stack(
        [weight_of(s, occupation + 1.0) for s in (1, 2)] + [weight_of(s, occupation) for s in (1, 2)]
    ).astype(jnp.float32)

    source_own, source_other = shifted(place, weights, own, got, own_halo, got_halo)
    near = [
        source_own,
        flip(source_other, 1, 0),
        flip(source_other, 1, 2),
        flip(source_own, 0, 2),
    ]
    moves = [(0, 0), (1, 0), (1, 2), (0, 2)]
    sources = near + [flip(x, 0, 1) for x in near]
    moves = moves + [(lo, mo ^ 1) for lo, mo in moves]

    coup = jnp.stack([coupling, coup_c, coup_b, coup_bc])
    coup_t = jnp.swapaxes(coup, 2, 3)

    donors = jnp.stack(
        [(mom ^ mo) * local_k + (x_lo ^ lo) * half + kk for lo, mo in moves for kk in range(half)]
    ).astype(jnp.int32)
    table = jnp.sum(
        jnp.where(
            momentum_map[:, :, None] == donors[None, None, :],
            jnp.arange(points, dtype=jnp.int32)[None, :, None],
            0,
        ),
        axis=1,
    ).astype(jnp.int32)
    table_home = lax.dynamic_slice_in_dim(table, mom * local_k, local_k, 0)

    every = jnp.arange(n_mom, dtype=jnp.int32)
    tiles_home = jnp.concatenate([every, every ^ mom.astype(jnp.int32)])
    tiles_out = jnp.stack([mom.astype(jnp.int32), jnp.zeros((), jnp.int32)])

    sigma_home = convolved(
        tiles_home, table_home.reshape(-1), sources, coup, coup_t, 1, n_mom, local_k, "home"
    )
    part = partial_density(green, gamma, sigma_home, 1.0 / (green.shape[1] * n_energy))
    summed = lax.psum_scatter(part, "energy", scatter_dimension=2, tiled=True)
    density = jnp.transpose(summed, (2, 0, 1, 3)).astype(jnp.float32)
    self_energy = convolved(
        tiles_out, table.reshape(-1), sources, coup, coup_t, n_mom, 1, local_k, "rows"
    )
    return (self_energy, density)


def solution(mesh):
    return jax.shard_map(
        on_device,
        mesh=mesh,
        in_specs=(
            P("mom", "energy", None, None, None),
            P("mom", "energy", None),
            P(None, "mom", None),
            P(),
            P(),
            P(),
            P(),
        ),
        out_specs=(P(None, "energy", None, "mom", None), P("energy", "mom", None, None)),
        check_vma=False,
    )
```

time: 1190 us -> 483 us (0.41)
  local copies, waits for them, and re-layouts: 272 us -> 25.3 us
  blocking collectives: 220 us -> 0 us
  other arithmetic: 184 us -> 12.4 us
  Pallas kernels: 0 us -> 107 us
  waiting for transfers between devices: 392 us -> 306 us
  matrix products: 84 us -> 0 us
    all_to_all x4 -> x0, blocking collectives: 220 us -> none  [the longest x3 160 us: several_exchanges(): lax.all_to_all(share, axis, split_axis=0, concat_axis=0, tiled=True)]
    gather x128 -> x0, local copies, waits for them, and re-layouts: 189 us -> none  [one_block(): jnp.take(source, momentum_map[:, qpoint], axis=0).astype(jnp.float32)]
    ppermute x2 -> x13, waiting for transfers between devices: 342 us -> 165 us  [the longest x11 129 us: flip(): return lax.ppermute(x, BOTH, perm)]
    reduce_scatter x0 -> x1, waiting for transfers between devices: none -> 140 us  [on_device(): summed = lax.psum_scatter(part, 'energy', scatter_dimension=2, tiled=True)]
    pallas_call x0 -> x6, Pallas kernels: none -> 107 us  [the longest x2 73.1 us: convolved(): pl.pallas_call(convolve_kernel, grid_spec=pltpu.PrefetchScalarGridSpec(nu...]
    dot_general x10 -> x0, matrix products: 84 us -> none  [the longest x1 11 us: outer_pair(): jnp.einsum('kecij,kecmj->keim', left, right, preferred_element_type=jnp.f...]
    dynamic_update_slice x8 -> x0, other arithmetic: 76 us -> none  [one_block(): lax.dynamic_update_slice_in_dim(result, total.astype(jnp.bfloat16), start...]
    convert_element_type x12 -> x1, other arithmetic: 65 us -> 0.92 us  [on_device(): density = jnp.transpose(summed, (2, 0, 1, 3)).astype(jnp.float32)]
  transfers between devices with their start and end apart: 3 -> 14, of which waited for: 3 -> 5; matrix products, arithmetic and copies ran while one was open for 0% -> 6% of each run, Pallas kernels for 0% -> 10%
where the time goes in v1:
time: 483 us; the launch traced here: 482 us
  waiting for transfers between devices  306 us (63%)
  Pallas kernels  107 us (22%)
  local copies, waits for them, and re-layouts  25.3 us (5%)
  between operations  16.8 us (3%)
  starting transfers between devices  14.4 us (3%)
  other arithmetic  12.4 us (3%)
    reduce_scatter x1, waiting for transfers between devices, on_device(): summed = lax.psum_scatter(part, 'energy', scatter_dimension=2, tiled=True)  140 us
    ppermute x11, waiting for transfers between devices, flip(): return lax.ppermute(x, BOTH, perm)  129 us
    pallas_call x2, Pallas kernels, convolved(): pl.pallas_call(convolve_kernel, grid_spec=pltpu.PrefetchScalarGridSpec(nu...  73.1 us
    ppermute x2, waiting for transfers between devices, along_pairs(): return lax.ppermute(x, 'energy', moves)  35.8 us
    pallas_call x1, Pallas kernels, partial_density(): pl.pallas_call(functools.partial(density_kernel, inverse), grid=(count,),...  20.7 us
    unnamed x22, local copies, waits for them, and re-layouts  11.8 us
    another operation x1, local copies, waits for them, and re-layouts, on_device(): coup = jnp.stack([coupling, coup_c, coup_b, coup_bc])  11.4 us
  transfers between devices with their start and end apart: 14, of which 5 were waited for; matrix products, arithmetic and copies ran while one was open for 6% of the time, Pallas kernels for 10%

profile of v1, /device:TPU:0, one launch (start us, length us, event | category | flops | bytes accessed | tf_op | source)
XLA Modules:
  0.0 481.8 jit_solution(10058632884360556047)
XLA Ops:
  8.0 3.4 copy-done.1
  11.3 3.1 lesser.3
  14.4 1.7 collective-permute-start
  16.1 3.1 lesser.2.own
  19.2 1.4 collective-permute-start.1
  20.7 41.2 %collective-permute-done.got = bf16[2,2,512,512]{3,2,1,0:T(8,128)(2,1)} collective-permute-done((bf16[2,2,512,512]{3,2,1,0:T(8,128)(2,1)S(1)}, bf16[2,2,512,512]{3,2,1,0:T(8,128)(2,1)}, u32[]{:S(2)}, u32[]{:S(2)}) %collective-permute-start) | collective-permute-done | bytes 2097184 | tf_op jit(solution)/shard_map/ppermute | solution.py:263
  61.8 5.1 %collective-permute-start.2 = (bf16[2,2,512,512]{3,2,1,0:T(8,128)(2,1)}, bf16[2,2,512,512]{3,2,1,0:T(8,128)(2,1)}, u32[]{:S(2)}, u32[]{:S(2)}) collective-permute-start(bf16[2,2,512,512]{3,2,1,0:T(8,128)(2,1)} %collective-permute-done.got), channel_id=1, source_target_pairs={{0,8},{8,16},{12,4},{16,24},{20,12},{24,32},{28,20},{32,40},{36,28... | collective-permute-start | bytes 6291464 | tf_op jit(solution)/shard_map/ppermute | solution.py:272
  66.9 3.9 copy.15
  74.1 35.8 %collective-permute-done.2.got_halo = bf16[2,2,512,512]{3,2,1,0:T(8,128)(2,1)} collective-permute-done((bf16[2,2,512,512]{3,2,1,0:T(8,128)(2,1)}, bf16[2,2,512,512]{3,2,1,0:T(8,128)(2,1)}, u32[]{:S(2)}, u32[]{:S(2)}) %collective-permute-start.2) | collective-permute-done | bytes 2097184 | tf_op jit(solution)/shard_map/ppermute | solution.py:272
  109.9 1.6 copy-done.4
  111.5 7.6 %shifted.1 = (bf16[2,2,512,512]{3,2,1,0:T(8,128)(2,1)S(1)}, bf16[2,2,512,512]{3,2,1,0:T(8,128)(2,1)S(1)}) custom-call(s32[1]{0:T(128)} %bitcast.17.half.place, f32[4]{0:T(128)S(1)} %pad_maximum_fusion.1.weights, bf16[2,2,512,512]{3,2,1,0:T(8,128)(2,1)S(1)} %copy-done.4, bf16[2,2,512,512]{3,2,1,0:T(8,128)(2,1)} %collective-permute-done.got, ...), custom_call_target="tpu_custom_call" | custom-call | flops 16777216 | bytes 12582912 | tf_op jit(solution)/shard_map/shifted/pallas_call | solution.py:99
  119.0 2.4 collective-permute-start.3
  121.5 1.4 collective-permute-start.4
  122.8 1.4 collective-permute-start.5
  124.7 43.4 %collective-permute-done.3.refs_1_.refs_9_ = bf16[2,2,512,512]{3,2,1,0:T(8,128)(2,1)} collective-permute-done((bf16[2,2,512,512]{3,2,1,0:T(8,128)(2,1)S(1)}, bf16[2,2,512,512]{3,2,1,0:T(8,128)(2,1)}, u32[]{:S(2)}, u32[]{:S(2)}) %collective-permute-start.3) | collective-permute-done | bytes 2097184 | tf_op jit(solution)/shard_map/ppermute | solution.py:263
  168.1 44.9 %collective-permute-done.4.refs_2_.refs_10_ = bf16[2,2,512,512]{3,2,1,0:T(8,128)(2,1)} collective-permute-done((bf16[2,2,512,512]{3,2,1,0:T(8,128)(2,1)S(1)}, bf16[2,2,512,512]{3,2,1,0:T(8,128)(2,1)}, u32[]{:S(2)}, u32[]{:S(2)}) %collective-permute-start.4) | collective-permute-done | bytes 2097184 | tf_op jit(solution)/shard_map/ppermute | solution.py:263
  215.0 9.4 %fusion.4 = (bf16[4,16,512,128]{3,2,1,0:T(8,128)(2,1)}, bf16[4,16,128,512]{2,3,1,0:T(8,128)(2,1)}) fusion(bf16[1,16,128,512]{2,3,1,0:T(8,128)(2,1)} %bitcast.25, bf16[1,16,128,512]{2,3,1,0:T(8,128)(2,1)} %bitcast.24, bf16[1,16,128,512]{2,3,1,0:T(8,128)(2,1)} %bitcast.23, bf16[1,16,128,512]{2,3,1,0:T(8,128)(2,1)} %bitcast.30), kind=kLoop, calls=%fused_computation.17 | loop fusion | flops 12582912 | bytes 25165824 | tf_op jit(solution)/shard_map/transpose | solution.py:305
  224.4 11.4 %copy.18.refs_16_ = bf16[4,16,128,512]{3,2,1,0:T(8,128)(2,1)} copy(bf16[4,16,128,512]{2,3,1,0:T(8,128)(2,1)} %get-tuple-element.15) | data formatting | bytes 16777216 | tf_op jit(solution)/shard_map/stack | solution.py:304
  235.9 37.1 %home.1.sigma = bf16[4,2,2,512,512]{4,3,2,1,0:T(8,128)(2,1)} custom-call(s32[8]{0:T(128)} %pad_add_fusion.1.tiles, s32[64]{0:T(128)} %reshape.13.table, bf16[2,2,512,512]{3,2,1,0:T(8,128)(2,1)} %copy-done, bf16[2,2,512,512]{3,2,1,0:T(8,128)(2,1)} %collective-permute-done.3.refs_1_.refs_9_, bf16[2,2,512,512]{3,2,1,0:T(8,128)(2,1)} %collective-permute-done.4.refs_2_.refs_10_, ...), custom_call_target="tpu_custom_call" | custom-call | flops 134217728 | bytes 58720256 | tf_op jit(solution)/shard_map/home/pallas_call | solution.py:178
  272.9 20.7 %density.1 = bf16[4,2,512,512]{3,2,1,0:T(8,128)(2,1)S(1)} custom-call(bf16[4,2,2,512,512]{4,3,2,1,0:T(8,128)(2,1)} %green.5, f32[4,2,1,512]{3,2,1,0:T(1,128)S(1)} %broadcast_in_dim.32.gamma, bf16[4,2,2,512,512]{4,3,2,1,0:T(8,128)(2,1)} %home.1.sigma), custom_call_target="tpu_custom_call" | custom-call | flops 17179869184 | bytes 20971520 | tf_op jit(solution)/shard_map/density/pallas_call | solution.py:228
  293.6 1.9 copy-done.5
  296.8 36.0 %rows.1 = bf16[16,2,2,128,512]{4,3,2,1,0:T(8,128)(2,1)} custom-call(s32[2]{0:T(128)} %pad_add_fusion.tiles, s32[256]{0:T(256)} %reshape.12.table, bf16[2,2,512,512]{3,2,1,0:T(8,128)(2,1)} %copy-done, bf16[2,2,512,512]{3,2,1,0:T(8,128)(2,1)} %collective-permute-done.3.refs_1_.refs_9_, bf16[2,2,512,512]{3,2,1,0:T(8,128)(2,1)} %collective-permute-done.4.refs_2_.refs_10_, ...), custom_call_target="tpu_custom_call" | custom-call | flops 134217728 | bytes 20971520 | tf_op jit(solution)/shard_map/rows/pallas_call | solution.py:178
  332.8 140.3 %reduce-scatter.2.cloned.1.call-done = bf16[4,2,16,512]{3,2,1,0:T(8,128)(2,1)} async-done(((bf16[4,2,512,512]{3,2,1,0:T(8,128)(2,1)}), bf16[4,2,16,512]{3,2,1,0:T(8,128)(2,1)}) %reduce-scatter.2.cloned.1.call-update) | async-done | bytes 131088 | tf_op jit(solution)/shard_map/reduce_scatter | solution.py:328
  473.1 0.9 convert_bitcast_fusion
  (48 shorter events, 6.3 us)
Async XLA Ops:
  7.2 466.0 %reduce-scatter.2.cloned.1.call-start = ((), (), s32[]{:S(2)}) async-start(), calls=%async_computation.1 | async-start | bytes 4325376 | tf_op jit(solution)/shard_map/reduce_scatter | solution.py:328
  8.0 3.4 copy-start.1
  11.3 4.8 copy-start.2
  14.4 47.4 %collective-permute-start = (bf16[2,2,512,512]{3,2,1,0:T(8,128)(2,1)S(1)}, bf16[2,2,512,512]{3,2,1,0:T(8,128)(2,1)}, u32[]{:S(2)}, u32[]{:S(2)}) collective-permute-start(bf16[2,2,512,512]{3,2,1,0:T(8,128)(2,1)S(1)} %lesser.3), channel_id=1, source_target_pairs={{0,4},{1,5},{2,6},{3,7},{4,0},{5,1},{6,2},{7,3},{8,12},{9,13},{10,... | collective-permute-start | bytes 6291464 | tf_op jit(solution)/shard_map/ppermute | solution.py:263
  19.2 52.3 %copy-start.3 = (bf16[2,2,512,512]{3,2,1,0:T(8,128)(2,1)}, bf16[2,2,512,512]{3,2,1,0:T(8,128)(2,1)S(1)}, u32[]{:S(2)}) copy-start(bf16[2,2,512,512]{3,2,1,0:T(8,128)(2,1)S(1)} %lesser.2.own) | copy-start | bytes 6291460
  19.2 51.6 %copy-start.7 = (s32[4]{0:T(128)S(1)}, s32[4]{0:T(128)}, u32[]{:S(2)}) copy-start(s32[4]{0:T(128)} %param.10) | copy-start | bytes 52
  19.2 51.6 %copy-start.8 = (f32[4]{0:T(128)S(1)}, f32[4]{0:T(128)}, u32[]{:S(2)}) copy-start(f32[4]{0:T(128)} %param.11) | copy-start | bytes 52
  19.2 51.6 %copy-start.9 = (f32[4]{0:T(128)S(1)}, f32[4]{0:T(128)}, u32[]{:S(2)}) copy-start(f32[4]{0:T(128)} %param.12) | copy-start | bytes 52
  19.2 54.9 %collective-permute-start.1 = (bf16[2,2,512,512]{3,2,1,0:T(8,128)(2,1)S(1)}, bf16[2,2,512,512]{3,2,1,0:T(8,128)(2,1)}, u32[]{:S(2)}, u32[]{:S(2)}) collective-permute-start(bf16[2,2,512,512]{3,2,1,0:T(8,128)(2,1)S(1)} %lesser.2.own), channel_id=1, source_target_pairs={{4,12},{8,0},{12,20},{16,8},{20,28},{24,16},{28,36},{32,24},{36,44... | collective-permute-start | bytes 6291464 | tf_op jit(solution)/shard_map/ppermute | solution.py:272
  61.8 48.0 %collective-permute-start.2 = (bf16[2,2,512,512]{3,2,1,0:T(8,128)(2,1)}, bf16[2,2,512,512]{3,2,1,0:T(8,128)(2,1)}, u32[]{:S(2)}, u32[]{:S(2)}) collective-permute-start(bf16[2,2,512,512]{3,2,1,0:T(8,128)(2,1)} %collective-permute-done.got), channel_id=1, source_target_pairs={{0,8},{8,16},{12,4},{16,24},{20,12},{24,32},{28,20},{32,40},{36,28... | collective-permute-start | bytes 6291464 | tf_op jit(solution)/shard_map/ppermute | solution.py:272
  70.8 53.4 %collective-permute-start.11 = (bf16[16,128,512]{1,2,0:T(8,128)(2,1)}, bf16[16,128,512]{1,2,0:T(8,128)(2,1)}, u32[]{:S(2)}, u32[]{:S(2)}) collective-permute-start(bf16[16,128,512]{1,2,0:T(8,128)(2,1)} %copy.15), channel_id=1, source_target_pairs={{0,6},{1,7},{2,4},{3,5},{4,2},{5,3},{6,0},{7,1},{8,14},{9,15},{10,... | collective-permute-start | bytes 6291464 | tf_op jit(solution)/shard_map/ppermute | solution.py:263
  70.8 53.4 %collective-permute-start.10 = (bf16[16,128,512]{1,2,0:T(8,128)(2,1)}, bf16[16,128,512]{1,2,0:T(8,128)(2,1)}, u32[]{:S(2)}, u32[]{:S(2)}) collective-permute-start(bf16[16,128,512]{1,2,0:T(8,128)(2,1)} %copy.15), channel_id=1, source_target_pairs={{0,1},{1,0},{2,3},{3,2},{4,5},{5,4},{6,7},{7,6},{8,9},{9,8},{10,11... | collective-permute-start | bytes 6291464 | tf_op jit(solution)/shard_map/ppermute | solution.py:263
  109.9 1.6 copy-start.4
  111.5 102.2 %copy-start.6 = (s32[16,16]{1,0:T(8,128)S(1)}, s32[16,16]{1,0:T(8,128)}, u32[]{:S(2)}) copy-start(s32[16,16]{1,0:T(8,128)} %param.13) | copy-start | bytes 3076
  119.0 105.4 %copy-start = (bf16[2,2,512,512]{3,2,1,0:T(8,128)(2,1)}, bf16[2,2,512,512]{3,2,1,0:T(8,128)(2,1)S(1)}, u32[]{:S(2)}) copy-start(bf16[2,2,512,512]{3,2,1,0:T(8,128)(2,1)S(1)} %get-tuple-element.4.refs_0_.refs_8_) | copy-start | bytes 6291460
  119.0 49.1 %collective-permute-start.3 = (bf16[2,2,512,512]{3,2,1,0:T(8,128)(2,1)S(1)}, bf16[2,2,512,512]{3,2,1,0:T(8,128)(2,1)}, u32[]{:S(2)}, u32[]{:S(2)}) collective-permute-start(bf16[2,2,512,512]{3,2,1,0:T(8,128)(2,1)S(1)} %get-tuple-element.5), channel_id=1, source_target_pairs={{0,4},{1,5},{2,6},{3,7},{4,0},{5,1},{6,2},{7,3},{8,12},{9,13},{10,... | collective-permute-start | bytes 6291464 | tf_op jit(solution)/shard_map/ppermute | solution.py:263
  121.5 91.5 %collective-permute-start.4 = (bf16[2,2,512,512]{3,2,1,0:T(8,128)(2,1)S(1)}, bf16[2,2,512,512]{3,2,1,0:T(8,128)(2,1)}, u32[]{:S(2)}, u32[]{:S(2)}) collective-permute-start(bf16[2,2,512,512]{3,2,1,0:T(8,128)(2,1)S(1)} %get-tuple-element.5), channel_id=1, source_target_pairs={{0,6},{1,7},{2,4},{3,5},{4,2},{5,3},{6,0},{7,1},{8,14},{9,15},{10,... | collective-permute-start | bytes 6291464 | tf_op jit(solution)/shard_map/ppermute | solution.py:263
  122.8 90.2 %collective-permute-start.5 = (bf16[2,2,512,512]{3,2,1,0:T(8,128)(2,1)S(1)}, bf16[2,2,512,512]{3,2,1,0:T(8,128)(2,1)}, u32[]{:S(2)}, u32[]{:S(2)}) collective-permute-start(bf16[2,2,512,512]{3,2,1,0:T(8,128)(2,1)S(1)} %get-tuple-element.4.refs_0_.refs_8_), channel_id=1, source_target_pairs={{0,2},{1,3},{2,0},{3,1},{4,6},{5,7},{6,4},{7,5},{8,10},{9,11},{10,... | collective-permute-start | bytes 6291464 | tf_op jit(solution)/shard_map/ppermute | solution.py:263
  124.2 90.8 %collective-permute-start.12 = (bf16[16,128,512]{1,2,0:T(8,128)(2,1)}, bf16[16,128,512]{1,2,0:T(8,128)(2,1)}, u32[]{:S(2)}, u32[]{:S(2)}) collective-permute-start(bf16[16,128,512]{1,2,0:T(8,128)(2,1)} %collective-permute-done.11), channel_id=1, source_target_pairs={{0,1},{1,0},{2,3},{3,2},{4,5},{5,4},{6,7},{7,6},{8,9},{9,8},{10,11... | collective-permute-start | bytes 6291464 | tf_op jit(solution)/shard_map/ppermute | solution.py:263
  124.2 111.6 %collective-permute-start.6 = (bf16[2,2,512,512]{3,2,1,0:T(8,128)(2,1)S(1)}, bf16[2,2,512,512]{3,2,1,0:T(8,128)(2,1)}, u32[]{:S(2)}, u32[]{:S(2)}) collective-permute-start(bf16[2,2,512,512]{3,2,1,0:T(8,128)(2,1)S(1)} %get-tuple-element.4.refs_0_.refs_8_), channel_id=1, source_target_pairs={{0,1},{1,0},{2,3},{3,2},{4,5},{5,4},{6,7},{7,6},{8,9},{9,8},{10,11... | collective-permute-start | bytes 6291464 | tf_op jit(solution)/shard_map/ppermute | solution.py:263
  168.1 67.7 %collective-permute-start.7 = (bf16[2,2,512,512]{3,2,1,0:T(8,128)(2,1)}, bf16[2,2,512,512]{3,2,1,0:T(8,128)(2,1)}, u32[]{:S(2)}, u32[]{:S(2)}) collective-permute-start(bf16[2,2,512,512]{3,2,1,0:T(8,128)(2,1)} %collective-permute-done.3.refs_1_.refs_9_), channel_id=1, source_target_pairs={{0,1},{1,0},{2,3},{3,2},{4,5},{5,4},{6,7},{7,6},{8,9},{9,8},{10,11... | collective-permute-start | bytes 6291464 | tf_op jit(solution)/shard_map/ppermute | solution.py:263
  213.0 22.8 %collective-permute-start.8 = (bf16[2,2,512,512]{3,2,1,0:T(8,128)(2,1)}, bf16[2,2,512,512]{3,2,1,0:T(8,128)(2,1)}, u32[]{:S(2)}, u32[]{:S(2)}) collective-permute-start(bf16[2,2,512,512]{3,2,1,0:T(8,128)(2,1)} %collective-permute-done.4.refs_2_.refs_10_), channel_id=1, source_target_pairs={{0,1},{1,0},{2,3},{3,2},{4,5},{5,4},{6,7},{7,6},{8,9},{9,8},{10,11... | collective-permute-start | bytes 6291464 | tf_op jit(solution)/shard_map/ppermute | solution.py:263
  213.0 22.8 %collective-permute-start.9 = (bf16[2,2,512,512]{3,2,1,0:T(8,128)(2,1)}, bf16[2,2,512,512]{3,2,1,0:T(8,128)(2,1)}, u32[]{:S(2)}, u32[]{:S(2)}) collective-permute-start(bf16[2,2,512,512]{3,2,1,0:T(8,128)(2,1)} %collective-permute-done.5.refs_3_.refs_11_), channel_id=1, source_target_pairs={{0,1},{1,0},{2,3},{3,2},{4,5},{5,4},{6,7},{7,6},{8,9},{9,8},{10,11... | collective-permute-start | bytes 6291464 | tf_op jit(solution)/shard_map/ppermute | solution.py:263
  293.6 1.9 copy-start.5
Sparse Core Ops, SparseCore 0:
  295.7 177.3 reduce-scatter.1

commit v2 on v1

v2 whole, which is shorter than its diff:
```python
import functools

import jax
import jax.numpy as jnp
from jax import lax
from jax.experimental import pallas as pl
from jax.experimental.pallas import tpu as pltpu
from jax.sharding import PartitionSpec as P

CHUNKS = 2
BOTH = ("energy", "mom")
MIB = 1 << 20
NT = (((1,), (1,)), ((), ()))


def dot_nt(left, right):
    return lax.dot_general(left, right, NT, preferred_element_type=jnp.float32)


def dot_nn(left, right):
    return jnp.dot(left, right, preferred_element_type=jnp.float32)


def scale(block, gamma):
    return (block.astype(jnp.float32) * gamma).astype(jnp.bfloat16)


def lesser_kernel(chunk, half, green, gamma, out):
    rows = out.shape[2]
    span = slice(chunk * rows, (chunk + 1) * rows)
    gam = gamma[0, 0]
    wide_re = green[0, 0, 0].astype(jnp.float32)
    wide_im = green[0, 0, 1].astype(jnp.float32)
    less = (wide_re - wide_im).astype(jnp.bfloat16)
    more = (wide_re + wide_im).astype(jnp.bfloat16)
    total = dot_nt(scale(green[0, 0, 0, span], gam), less) + dot_nt(
        scale(green[0, 0, 1, span], gam), more
    )
    out[0, 0] = total.astype(jnp.bfloat16)


def packed_lesser(half, green, gamma, chunk):
    energies, norb = green.shape[1], green.shape[-1]
    count = green.shape[0] // 2
    rows = norb // CHUNKS
    return pl.pallas_call(
        functools.partial(lesser_kernel, chunk),
        grid_spec=pltpu.PrefetchScalarGridSpec(
            num_scalar_prefetch=1,
            grid=(count, energies),
            in_specs=[
                pl.BlockSpec((1, 1, 2, norb, norb), lambda k, e, h: (h[0] * count + k, e, 0, 0, 0)),
                pl.BlockSpec((1, 1, 1, norb), lambda k, e, h: (h[0] * count + k, e, 0, 0)),
            ],
            out_specs=pl.BlockSpec((1, 1, rows, norb), lambda k, e, h: (k, e, 0, 0)),
        ),
        out_shape=jax.ShapeDtypeStruct((count, energies, rows, norb), jnp.bfloat16),
        compiler_params=pltpu.CompilerParams(vmem_limit_bytes=32 * MIB),
        cost_estimate=pl.CostEstimate(
            flops=4 * count * energies * rows * norb**2,
            bytes_accessed=6 * count * energies * norb**2,
            transcendentals=0,
        ),
        name="lesser",
    )(half, green, gamma)


def shift_kernel(place, weights, own, got, own_halo, got_halo, early, out_own, out_other):
    rows = own.shape[2]
    step = 16

    def run(first, second, third, fourth, outs):
        def slab(i, carry):
            at = pl.ds(pl.multiple_of(i * step, step), step)
            levels = [
                ref[0, e, at, :].astype(jnp.float32)
                for ref in (first, second, third, fourth)
                for e in range(2)
            ]
            for o in range(4):
                total = weights[0] * levels[o + 3] + weights[1] * levels[o + 4]
                total = total + weights[2] * levels[o + 1] + weights[3] * levels[o]
                outs[o // 2][0, o % 2, at, :] = total.astype(jnp.bfloat16)
            return carry

        lax.fori_loop(0, rows // step, slab, 0)

    @pl.when(place[0] == 0)
    def _():
        run(got_halo, own, got, own_halo, (out_own, out_other))

    @pl.when(place[0] != 0)
    def _():
        run(own_halo, got, own, got_halo, (out_other, out_own))


def shifted(place, weights, own, got, own_halo, got_halo, early):
    count, energies, height, norb = own.shape
    rows = height // 2
    block = pl.BlockSpec((1, energies, rows, norb), lambda k, i, p, w: (k, 0, i, 0))
    out = jax.ShapeDtypeStruct(own.shape, jnp.bfloat16)
    return pl.pallas_call(
        shift_kernel,
        grid_spec=pltpu.PrefetchScalarGridSpec(
            num_scalar_prefetch=2,
            grid=(count, height // rows),
            in_specs=[block] * 4 + [pl.BlockSpec(memory_space=pl.ANY)],
            out_specs=[block] * 2,
        ),
        out_shape=[out, out],
        compiler_params=pltpu.CompilerParams(vmem_limit_bytes=32 * MIB),
        cost_estimate=pl.CostEstimate(
            flops=32 * count * height * norb,
            bytes_accessed=24 * count * height * norb,
            transcendentals=0,
        ),
        name="shifted",
    )(place, weights, own, got, own_halo, got_halo, early)


def identity(n):
    rows = lax.broadcasted_iota(jnp.int32, (n, n), 0)
    cols = lax.broadcasted_iota(jnp.int32, (n, n), 1)
    return (rows == cols).astype(jnp.float32).astype(jnp.bfloat16)


def fold_kernel(tiles, *refs):
    parts, (out, out_t) = refs[:4], refs[4:]
    points, height, norb = parts[0].shape
    turn = identity(norb // 2)
    for s in range(4):

        @pl.when(pl.program_id(0) == s)
        def _(part=parts[s]):
            for q in range(points):
                out[q] = part[q]
                for b in range(2):
                    span = slice(b * (norb // 2), (b + 1) * (norb // 2))
                    out_t[q, span, :] = dot_nt(turn, part[q, :, span]).astype(jnp.bfloat16)


def folded(tiles, parts):
    points, height, norb = parts[0].shape
    some = points // 4
    given = pl.BlockSpec((some, height, norb), lambda s, q, t: (q, 0, 0))
    whole = jax.ShapeDtypeStruct((points, norb, norb), jnp.bfloat16)
    return pl.pallas_call(
        fold_kernel,
        grid_spec=pltpu.PrefetchScalarGridSpec(
            num_scalar_prefetch=1,
            grid=(4, points // some),
            in_specs=[given] * 4,
            out_specs=[
                pl.BlockSpec((some, height, norb), lambda s, q, t: (q, t[s], 0)),
                pl.BlockSpec((some, norb, height), lambda s, q, t: (q, 0, t[s])),
            ],
        ),
        out_shape=[whole, whole],
        compiler_params=pltpu.CompilerParams(vmem_limit_bytes=48 * MIB),
        cost_estimate=pl.CostEstimate(
            flops=4 * points * norb**3 // 2, bytes_accessed=14 * points * norb**2, transcendentals=0
        ),
        name="fold",
    )(tiles, *parts)


def add_products(targets, picks, sources, factor, at, store):
    acc = [[None, None] for _ in range(targets)]
    for quad in range(4):
        donors = [(s, kk) for s in (2 * quad, 2 * quad + 1) for kk in range(2)]
        held = [[sources[s][kk, e, at[0], at[1]] for e in range(2)] for s, kk in donors]
        for t in range(targets):
            c = [factor[picks(t, 4 * quad + d), at[0], at[1]] for d in range(4)]
            for e in range(2):
                part = (c[0] * held[0][e] + c[1] * held[1][e]) + (
                    c[2] * held[2][e] + c[3] * held[3][e]
                )
                part = part.astype(jnp.float32)
                acc[t][e] = part if acc[t][e] is None else acc[t][e] + part
    for t in range(targets):
        for e in range(2):
            store[t, e, at[0], at[1]] = acc[t][e].astype(store.dtype)


def home_kernel(table, *refs):
    sources, (coup, coup_t, out, out_t) = refs[:8], refs[8:]
    targets, _, height, norb = out.shape

    def picks(t, d):
        return table[t * 16 + d]

    def slab(i, carry):
        at = (
            pl.ds(pl.multiple_of(i // 2 * 16, 16), 16),
            pl.ds(pl.multiple_of(i % 2 * (norb // 2), norb // 2), norb // 2),
        )
        add_products(targets, picks, sources, coup, at, out)
        add_products(targets, picks, sources, coup_t, at, out_t)
        return carry

    lax.fori_loop(0, height // 16 * 2, slab, 0)


def home_sums(table, sources, coup, coup_t, chunk, targets):
    _, _, rows, norb = sources[0].shape
    points = coup.shape[0]
    height = 128
    steps = rows // height
    given = pl.BlockSpec((2, 2, height, norb), lambda i, q: (0, 0, i, 0))
    factor = pl.BlockSpec((points, height, norb), lambda i, q: (0, chunk * steps + i, 0))
    result = pl.BlockSpec((targets, 2, height, norb), lambda i, q: (0, 0, i, 0))
    out = jax.ShapeDtypeStruct((targets, 2, rows, norb), jnp.bfloat16)
    return pl.pallas_call(
        home_kernel,
        grid_spec=pltpu.PrefetchScalarGridSpec(
            num_scalar_prefetch=1,
            grid=(steps,),
            in_specs=[given] * 8 + [factor] * 2,
            out_specs=[result] * 2,
        ),
        out_shape=[out, out],
        compiler_params=pltpu.CompilerParams(vmem_limit_bytes=48 * MIB),
        cost_estimate=pl.CostEstimate(
            flops=40 * targets * points * rows * norb,
            bytes_accessed=10 * MIB * steps,
            transcendentals=0,
        ),
        name="home",
    )(table, *sources, coup, coup_t)


def rows_kernel(tile, table, *refs):
    rows_of, cols_of = refs[:16], refs[16:32]
    coup, coup_t, out, picked, along, across = refs[32:]
    targets, _, _, height, norb = out.shape
    group = pl.program_id(0) * targets
    part = norb // CHUNKS

    for c in range(CHUNKS):

        @pl.when((pl.program_id(0) == 0) & (tile[0] // CHUNKS == c))
        def _(held=rows_of[8 * c : 8 * c + 8]):
            for s in range(8):
                picked[s] = held[s][...]

    def picks(t, d):
        return table[(group + t) * 16 + d]

    def over_rows(i, carry):
        at = (
            pl.ds(pl.multiple_of(i // 2 * 16, 16), 16),
            pl.ds(pl.multiple_of(i % 2 * (norb // 2), norb // 2), norb // 2),
        )
        add_products(targets, picks, [picked.at[s] for s in range(8)], coup, at, along)
        return carry

    lax.fori_loop(0, height // 16 * 2, over_rows, 0)
    for c in range(CHUNKS):

        def over_cols(i, carry, c=c):
            at = (pl.ds(pl.multiple_of(i * 32, 32), 32), slice(None))
            add_products(
                targets,
                picks,
                cols_of[8 * c : 8 * c + 8],
                coup_t.at[:, c * part : (c + 1) * part],
                at,
                across.at[:, :, c * part : (c + 1) * part],
            )
            return carry

        lax.fori_loop(0, part // 32, over_cols, 0)

    turn = identity(height)
    for t in range(targets):
        for e in range(2):
            u = along[t, e]
            v = dot_nt(turn, across[t, e])
            out[t, e, 0] = (u + v).astype(jnp.bfloat16)
            out[t, e, 1] = (u - v).astype(jnp.bfloat16)


def row_sums(tile, table, chunks, coup, coup_t, targets):
    _, _, part, norb = chunks[0][0].shape
    points = coup.shape[0]
    height = 128
    steps = part // height
    groups = points // targets
    row_block = pl.BlockSpec((2, 2, height, norb), lambda g, t, q: (0, 0, t[0] % steps, 0))
    col_block = pl.BlockSpec((2, 2, part, height), lambda g, t, q: (0, 0, 0, t[0]))
    sources = [x for chunk in chunks for x in chunk]
    return pl.pallas_call(
        rows_kernel,
        grid_spec=pltpu.PrefetchScalarGridSpec(
            num_scalar_prefetch=2,
            grid=(groups,),
            in_specs=[row_block] * 16
            + [col_block] * 16
            + [
                pl.BlockSpec((points, height, norb), lambda g, t, q: (0, t[0], 0)),
                pl.BlockSpec((points, norb, height), lambda g, t, q: (0, 0, t[0])),
            ],
            out_specs=pl.BlockSpec((targets, 2, 2, height, norb), lambda g, t, q: (g, 0, 0, 0, 0)),
            scratch_shapes=[
                pltpu.VMEM((8, 2, 2, height, norb), jnp.bfloat16),
                pltpu.VMEM((targets, 2, height, norb), jnp.float32),
                pltpu.VMEM((targets, 2, norb, height), jnp.bfloat16),
            ],
        ),
        out_shape=jax.ShapeDtypeStruct((points, 2, 2, height, norb), jnp.bfloat16),
        compiler_params=pltpu.CompilerParams(vmem_limit_bytes=56 * MIB),
        cost_estimate=pl.CostEstimate(
            flops=40 * points * points * height * norb,
            bytes_accessed=24 * MIB,
            transcendentals=0,
        ),
        name="rows",
    )(tile, table, *sources, *sources, coup, coup_t)


def density_kernel(inverse, green, gamma, *refs):
    us, vs, out = refs[:CHUNKS], refs[CHUNKS : 2 * CHUNKS], refs[-1]
    norb = green.shape[-1]
    part = norb // CHUNKS
    d_re = d_im = None
    for e in range(green.shape[1]):
        g_re, g_im = green[0, e, 0], green[0, e, 1]
        gam = gamma[0, e]
        wide_re, wide_im = g_re.astype(jnp.float32), g_im.astype(jnp.float32)
        less = (wide_re - wide_im).astype(jnp.bfloat16)
        more = (wide_re + wide_im).astype(jnp.bfloat16)
        u = jnp.concatenate([ref[0, e] for ref in us], axis=0)
        v = jnp.concatenate([ref[0, e] for ref in vs], axis=0)
        m_re = dot_nn(less, u) + dot_nt(more, v) + scale(g_re, gam).astype(jnp.float32)
        m_im = dot_nn(more, u) - dot_nt(less, v) + scale(g_im, gam).astype(jnp.float32)
        m_re, m_im = m_re.astype(jnp.bfloat16), m_im.astype(jnp.bfloat16)
        one = dot_nt(m_re, g_re) + dot_nt(m_im, g_im)
        two = dot_nt(m_im, g_re) - dot_nt(m_re, g_im)
        d_re = one if d_re is None else d_re + one
        d_im = two if d_im is None else d_im + two
    out[0, 0] = (d_re * inverse).astype(jnp.bfloat16)
    out[0, 1] = (d_im * inverse).astype(jnp.bfloat16)


def partial_density(green, gamma, sums, sums_t, inverse, first, count):
    _, energies, _, norb, _ = green.shape
    part = pl.BlockSpec((1, energies, norb // CHUNKS, norb), lambda k: (first + k, 0, 0, 0))
    return pl.pallas_call(
        functools.partial(density_kernel, inverse),
        grid=(count,),
        in_specs=[
            pl.BlockSpec((1, energies, 2, norb, norb), lambda k: (first + k, 0, 0, 0, 0)),
            pl.BlockSpec((1, energies, 1, norb), lambda k: (first + k, 0, 0, 0)),
        ]
        + [part] * (2 * CHUNKS),
        out_specs=pl.BlockSpec((1, 2, norb, norb), lambda k: (k, 0, 0, 0)),
        out_shape=jax.ShapeDtypeStruct((count, 2, norb, norb), jnp.bfloat16),
        compiler_params=pltpu.CompilerParams(vmem_limit_bytes=48 * MIB),
        cost_estimate=pl.CostEstimate(
            flops=16 * count * energies * norb**3,
            bytes_accessed=(8 * energies + 4) * count * norb**2,
            transcendentals=0,
        ),
        name="density",
    )(green, gamma, *sums, *sums_t)


def on_device(green, broadening, coupling, shift_steps, mode_weight, occupation, momentum_map):
    n_energy, n_mom = lax.axis_size("energy"), lax.axis_size("mom")
    pairs = n_energy // 2
    local_k = green.shape[0]
    norb = green.shape[-1]
    half = local_k // 2
    points = momentum_map.shape[1]
    energy, mom = lax.axis_index("energy"), lax.axis_index("mom")
    x_lo = energy % 2

    def flip(x, lo, mo):
        perm = [
            (e * n_mom + m, (e ^ lo) * n_mom + (m ^ mo))
            for e in range(n_energy)
            for m in range(n_mom)
        ]
        return lax.ppermute(x, BOTH, perm)

    def along_pairs(x, step_of_low):
        moves = []
        for j in range(pairs):
            for lo in range(2):
                to = j + (step_of_low if lo == 0 else -step_of_low)
                if 0 <= to < pairs:
                    moves.append((2 * j + lo, 2 * to + lo))
        return lax.ppermute(x, "energy", moves)

    def weight_of(step, factor):
        return 0.5 * jnp.sum(jnp.where(shift_steps == step, mode_weight * factor, 0.0))

    weights = jnp.stack(
        [weight_of(s, occupation + 1.0) for s in (1, 2)] + [weight_of(s, occupation) for s in (1, 2)]
    ).astype(jnp.float32)

    gamma = broadening[:, :, None, :]
    place = x_lo.astype(jnp.int32)[None]

    coup_b = flip(coupling, 1, 2)
    coup_c = flip(coupling, 0, 1)
    coup_bc = flip(coup_b, 0, 1)
    early = (coup_b, coup_bc)

    sent = [packed_lesser(1 - place, green, gamma, c) for c in range(CHUNKS)]
    got = [flip(x, 1, 0) for x in sent]
    own = [packed_lesser(place, green, gamma, c) for c in range(CHUNKS)]
    own_halo = [along_pairs(x, -1) for x in own]
    got_halo = [along_pairs(x, 1) for x in got]

    moves = [(0, 0), (1, 0), (1, 2), (0, 2)]
    moves = moves + [(lo, mo ^ 1) for lo, mo in moves]
    chunks = []
    for c in range(CHUNKS):
        mine, other = shifted(place, weights, own[c], got[c], own_halo[c], got_halo[c], early[c])
        near = [mine, flip(other, 1, 0), flip(other, 1, 2), flip(mine, 0, 2)]
        chunks.append(near + [flip(x, 0, 1) for x in near])

    tile = mom.astype(jnp.int32)
    coup, coup_t = folded(
        jnp.arange(4, dtype=jnp.int32) ^ tile, [coupling, coup_c, coup_b, coup_bc]
    )

    donors = jnp.stack(
        [(mom ^ mo) * local_k + (x_lo ^ lo) * half + kk for lo, mo in moves for kk in range(half)]
    ).astype(jnp.int32)
    table = jnp.sum(
        jnp.where(
            momentum_map[:, :, None] == donors[None, None, :],
            jnp.arange(points, dtype=jnp.int32)[None, :, None],
            0,
        ),
        axis=1,
    ).astype(jnp.int32)
    table_home = lax.dynamic_slice_in_dim(table, mom * local_k, local_k, 0).reshape(-1)

    sums = [home_sums(table_home, chunks[c], coup, coup_t, c, local_k) for c in range(CHUNKS)]
    us, vs = [s[0] for s in sums], [s[1] for s in sums]
    inverse = 1.0 / (green.shape[1] * n_energy)
    received = []
    for first in range(0, local_k, half):
        part = partial_density(green, gamma, us, vs, inverse, first, half)
        part = part.reshape(half, 2, n_energy, norb // n_energy, norb)
        received.append(lax.all_to_all(part, "energy", split_axis=2, concat_axis=2, tiled=True))
    self_energy = row_sums(tile[None], table.reshape(-1), chunks, coup, coup_t, local_k)
    summed = jnp.concatenate(
        [jnp.sum(x.astype(jnp.float32), axis=2) for x in received], axis=0
    )
    density = jnp.transpose(summed, (2, 0, 1, 3))
    return (self_energy, density)


def solution(mesh):
    return jax.shard_map(
        on_device,
        mesh=mesh,
        in_specs=(
            P("mom", "energy", None, None, None),
            P("mom", "energy", None),
            P(None, "mom", None),
            P(),
            P(),
            P(),
            P(),
        ),
        out_specs=(P(None, "energy", None, "mom", None), P("energy", "mom", None, None)),
        check_vma=False,
    )
```

time: 483 us -> 320 us (0.66)
  waiting for transfers between devices: 306 us -> 132 us
  starting transfers between devices: 14.4 us -> 38.6 us
  Pallas kernels: 107 us -> 124 us
  between operations: 16.8 us -> 3.52 us
  other arithmetic: 12.4 us -> 3.23 us
  local copies, waits for them, and re-layouts: 25.3 us -> 17.4 us
    reduce_scatter x1 -> x0, waiting for transfers between devices: 140 us -> none  [on_device(): summed = lax.psum_scatter(part, 'energy', scatter_dimension=2, tiled=True)]
    ppermute x11 -> x19, waiting for transfers between devices: 129 us -> 97.9 us  [flip(): return lax.ppermute(x, BOTH, perm)]
    ppermute x2 -> x4, waiting for transfers between devices: 35.8 us -> 16.8 us  [along_pairs(): return lax.ppermute(x, 'energy', moves)]
    all_to_all x0 -> x2, waiting for transfers between devices: none -> 16.9 us  [on_device(): lax.all_to_all(part, 'energy', split_axis=2, concat_axis=2, tiled=True)]
    all_to_all x0 -> x2, starting transfers between devices: none -> 13.7 us  [on_device(): lax.all_to_all(part, 'energy', split_axis=2, concat_axis=2, tiled=True)]
    pallas_call x4 -> x8, Pallas kernels: 79.2 us -> 92.3 us  [the longest x1 36.3 us: row_sums(): pl.pallas_call(rows_kernel, grid_spec=pltpu.PrefetchScalarGridSpec(num_sc...]
    another operation x1 -> x0, local copies, waits for them, and re-layouts: 11.4 us -> none  [on_device(): coup = jnp.stack([coupling, coup_c, coup_b, coup_bc])]
    transpose x1, other arithmetic: 9.41 us -> 0.02 us  [on_device(): density = jnp.transpose(summed, (2, 0, 1, 3))]
  transfers between devices with their start and end apart: 14 -> 25, of which waited for: 5 -> 10; matrix products, arithmetic and copies ran while one was open for 6% -> 2% of each run, Pallas kernels for 10% -> 31%
where the time goes in v2:
time: 320 us; the launch traced here: 319 us
  waiting for transfers between devices  132 us (41%)
  Pallas kernels  124 us (39%)
  starting transfers between devices  38.6 us (12%)
  local copies, waits for them, and re-layouts  17.4 us (5%)
  between operations  3.52 us (1%)
  other arithmetic  3.23 us (1%)
    ppermute x19, waiting for transfers between devices, flip(): return lax.ppermute(x, BOTH, perm)  97.9 us
    pallas_call x1, Pallas kernels, row_sums(): pl.pallas_call(rows_kernel, grid_spec=pltpu.PrefetchScalarGridSpec(num_sc...  36.3 us
    pallas_call x2, Pallas kernels, home_sums(): pl.pallas_call(home_kernel, grid_spec=pltpu.PrefetchScalarGridSpec(num_sc...  27.1 us
    pallas_call x2, Pallas kernels, partial_density(): pl.pallas_call(functools.partial(density_kernel, inverse), grid=(count,),...  22.6 us
    pallas_call x1, Pallas kernels, folded(): pl.pallas_call(fold_kernel, grid_spec=pltpu.PrefetchScalarGridSpec(num_sc...  20.9 us
    all_to_all x2, waiting for transfers between devices, on_device(): lax.all_to_all(part, 'energy', split_axis=2, concat_axis=2, tiled=True)  16.9 us
    ppermute x4, waiting for transfers between devices, along_pairs(): return lax.ppermute(x, 'energy', moves)  16.8 us
    ppermute x19, starting transfers between devices, flip(): return lax.ppermute(x, BOTH, perm)  14.4 us
  transfers between devices with their start and end apart: 25, of which 10 were waited for; matrix products, arithmetic and copies ran while one was open for 2% of the time, Pallas kernels for 31%

profile of v2, /device:TPU:0, one launch (start us, length us, event | category | flops | bytes accessed | tf_op | source)
XLA Modules:
  0.0 318.6 jit_solution(14212174642225236841)
XLA Ops:
  0.6 2.9 collective-permute-start.3
  4.3 3.4 %copy-done = bf16[4,2,2,512,512]{4,3,2,1,0:T(8,128)(2,1)S(1)} copy-done((bf16[4,2,2,512,512]{4,3,2,1,0:T(8,128)(2,1)S(1)}, bf16[4,2,2,512,512]{4,3,2,1,0:T(8,128)(2,1)}, u32[]{:S(2)}) %copy-start) | copy-done | bytes 8388632
  16.4 4.0 %collective-permute-start.11 = (bf16[2,2,256,512]{3,2,1,0:T(8,128)(2,1)S(1)}, bf16[2,2,256,512]{3,2,1,0:T(8,128)(2,1)}, u32[]{:S(2)}, u32[]{:S(2)}) collective-permute-start(bf16[2,2,256,512]{3,2,1,0:T(8,128)(2,1)S(1)} %lesser.7), channel_id=1, source_target_pairs={{0,4},{1,5},{2,6},{3,7},{4,0},{5,1},{6,2},{7,3},{8,12},{9,13},{10,... | collective-permute-start | bytes 3145736 | tf_op jit(solution)/shard_map/ppermute | solution.py:384
  20.4 15.6 %collective-permute-done.got = bf16[2,2,256,512]{3,2,1,0:T(8,128)(2,1)} collective-permute-done((bf16[2,2,256,512]{3,2,1,0:T(8,128)(2,1)S(1)}, bf16[2,2,256,512]{3,2,1,0:T(8,128)(2,1)}, u32[]{:S(2)}, u32[]{:S(2)}) %collective-permute-start) | collective-permute-done | bytes 1048608 | tf_op jit(solution)/shard_map/ppermute | solution.py:384
  36.0 4.5 %collective-permute-start.2 = (bf16[2,2,256,512]{3,2,1,0:T(8,128)(2,1)}, bf16[2,2,256,512]{3,2,1,0:T(8,128)(2,1)}, u32[]{:S(2)}, u32[]{:S(2)}) collective-permute-start(bf16[2,2,256,512]{3,2,1,0:T(8,128)(2,1)} %collective-permute-done.got), channel_id=1, source_target_pairs={{0,8},{8,16},{12,4},{16,24},{20,12},{24,32},{28,20},{32,40},{36,28... | collective-permute-start | bytes 3145736 | tf_op jit(solution)/shard_map/ppermute | solution.py:393
  50.0 7.0 %collective-permute-done.11.got = bf16[2,2,256,512]{3,2,1,0:T(8,128)(2,1)} collective-permute-done((bf16[2,2,256,512]{3,2,1,0:T(8,128)(2,1)S(1)}, bf16[2,2,256,512]{3,2,1,0:T(8,128)(2,1)}, u32[]{:S(2)}, u32[]{:S(2)}) %collective-permute-start.11) | collective-permute-done | bytes 1048608 | tf_op jit(solution)/shard_map/ppermute | solution.py:384
  57.0 3.5 %collective-permute-start.13 = (bf16[2,2,256,512]{3,2,1,0:T(8,128)(2,1)}, bf16[2,2,256,512]{3,2,1,0:T(8,128)(2,1)S(1)}, u32[]{:S(2)}, u32[]{:S(2)}) collective-permute-start(bf16[2,2,256,512]{3,2,1,0:T(8,128)(2,1)} %collective-permute-done.11.got), channel_id=1, source_target_pairs={{0,8},{8,16},{12,4},{16,24},{20,12},{24,32},{28,20},{32,40},{36,28... | collective-permute-start | bytes 3145736 | tf_op jit(solution)/shard_map/ppermute | solution.py:393
  60.5 4.3 %shifted.2 = (bf16[2,2,256,512]{3,2,1,0:T(8,128)(2,1)S(1)}, bf16[2,2,256,512]{3,2,1,0:T(8,128)(2,1)S(1)}) custom-call(s32[1]{0:T(128)} %bitcast.17.half.place, f32[4]{0:T(128)S(1)} %pad_maximum_fusion.weights, bf16[2,2,256,512]{3,2,1,0:T(8,128)(2,1)S(1)} %lesser.4.own, bf16[2,2,256,512]{3,2,1,0:T(8,128)(2,1)} %collective-permute-done.got, ...), custom_call_target="tpu_custom_call" | custom-call | flops 8388608 | bytes 6291456 | tf_op jit(solution)/shard_map/shifted/pallas_call | solution.py:102
  66.4 15.6 %collective-permute-done.13.got_halo = bf16[2,2,256,512]{3,2,1,0:T(8,128)(2,1)S(1)} collective-permute-done((bf16[2,2,256,512]{3,2,1,0:T(8,128)(2,1)}, bf16[2,2,256,512]{3,2,1,0:T(8,128)(2,1)S(1)}, u32[]{:S(2)}, u32[]{:S(2)}) %collective-permute-start.13) | collective-permute-done | bytes 1048608 | tf_op jit(solution)/shard_map/ppermute | solution.py:393
  82.8 8.2 %collective-permute-done.4.refs_1_.refs_17_ = bf16[2,2,256,512]{3,2,1,0:T(8,128)(2,1)S(1)} collective-permute-done((bf16[2,2,256,512]{3,2,1,0:T(8,128)(2,1)S(1)}, bf16[2,2,256,512]{3,2,1,0:T(8,128)(2,1)S(1)}, u32[]{:S(2)}, u32[]{:S(2)}) %collective-permute-start.4) | collective-permute-done | bytes 1048608 | tf_op jit(solution)/shard_map/ppermute | solution.py:384
  91.0 21.1 %collective-permute-done.5.refs_2_.refs_18_ = bf16[2,2,256,512]{3,2,1,0:T(8,128)(2,1)S(1)} collective-permute-done((bf16[2,2,256,512]{3,2,1,0:T(8,128)(2,1)S(1)}, bf16[2,2,256,512]{3,2,1,0:T(8,128)(2,1)S(1)}, u32[]{:S(2)}, u32[]{:S(2)}) %collective-permute-start.5) | collective-permute-done | bytes 1048608 | tf_op jit(solution)/shard_map/ppermute | solution.py:384
  114.5 4.9 %shifted.3 = (bf16[2,2,256,512]{3,2,1,0:T(8,128)(2,1)}, bf16[2,2,256,512]{3,2,1,0:T(8,128)(2,1)S(1)}) custom-call(s32[1]{0:T(128)} %bitcast.17.half.place, f32[4]{0:T(128)S(1)} %pad_maximum_fusion.weights, bf16[2,2,256,512]{3,2,1,0:T(8,128)(2,1)S(1)} %copy-done.8, bf16[2,2,256,512]{3,2,1,0:T(8,128)(2,1)} %collective-permute-done.11.got, ...), custom_call_target="tpu_custom_call" | custom-call | flops 8388608 | bytes 6291456 | tf_op jit(solution)/shard_map/shifted/pallas_call | solution.py:102
  123.0 2.8 collective-permute-start.17
  126.3 20.5 %collective-permute-done.15.refs_9_.refs_25_.refs_1_ = bf16[2,2,256,512]{3,2,1,0:T(8,128)(2,1)} collective-permute-done((bf16[2,2,256,512]{3,2,1,0:T(8,128)(2,1)S(1)}, bf16[2,2,256,512]{3,2,1,0:T(8,128)(2,1)}, u32[]{:S(2)}, u32[]{:S(2)}) %collective-permute-start.15) | collective-permute-done | bytes 1048608 | tf_op jit(solution)/shard_map/ppermute | solution.py:384
  146.8 23.1 %collective-permute-done.16.refs_10_.refs_26_.refs_2_ = bf16[2,2,256,512]{3,2,1,0:T(8,128)(2,1)} collective-permute-done((bf16[2,2,256,512]{3,2,1,0:T(8,128)(2,1)S(1)}, bf16[2,2,256,512]{3,2,1,0:T(8,128)(2,1)}, u32[]{:S(2)}, u32[]{:S(2)}) %collective-permute-start.16) | collective-permute-done | bytes 1048608 | tf_op jit(solution)/shard_map/ppermute | solution.py:384
  173.9 20.9 %fold.1 = (bf16[16,512,512]{2,1,0:T(8,128)(2,1)}, bf16[16,512,512]{2,1,0:T(8,128)(2,1)}) custom-call(s32[4]{0:T(128)S(1)} %iota_xor_fusion.tiles, bf16[16,128,512]{2,1,0:T(8,128)(2,1)S(1)} %copy-done.10, bf16[16,128,512]{2,1,0:T(8,128)(2,1)S(1)} %copy-done.12, bf16[16,128,512]{2,1,0:T(8,128)(2,1)} %collective-permute-done.3.early.refs_2_, ...), custom_call_target="tpu_custom_call" | custom-call | flops 4294967296 | bytes 58720256 | tf_op jit(solution)/shard_map/fold/pallas_call | solution.py:147
  194.9 13.3 %home.2 = (bf16[4,2,256,512]{3,2,1,0:T(8,128)(2,1)}, bf16[4,2,256,512]{3,2,1,0:T(8,128)(2,1)}) custom-call(s32[64]{0:T(128)S(1)} %reshape.19.table, bf16[2,2,256,512]{3,2,1,0:T(8,128)(2,1)S(1)} %get-tuple-element.12.refs_0_.refs_16_, bf16[2,2,256,512]{3,2,1,0:T(8,128)(2,1)S(1)} %collective-permute-done.4.refs_1_.refs_17_, ...), custom_call_target="tpu_custom_call" | custom-call | flops 335544320 | bytes 20971520 | tf_op jit(solution)/shard_map/home/pallas_call | solution.py:213
  208.2 13.8 %home.3 = (bf16[4,2,256,512]{3,2,1,0:T(8,128)(2,1)}, bf16[4,2,256,512]{3,2,1,0:T(8,128)(2,1)}) custom-call(s32[64]{0:T(128)S(1)} %reshape.19.table, bf16[2,2,256,512]{3,2,1,0:T(8,128)(2,1)} %get-tuple-element.14.refs_8_.refs_24_.refs_0_, bf16[2,2,256,512]{3,2,1,0:T(8,128)(2,1)} %collective-permute-done.15.refs_9_.refs_25_.refs_1_, ...), custom_call_target="tpu_custom_call" | custom-call | flops 335544320 | bytes 20971520 | tf_op jit(solution)/shard_map/home/pallas_call | solution.py:213
  222.0 11.3 %density.3 = bf16[2,2,512,512]{3,2,1,0:T(8,128)(2,1)S(1)} custom-call(bf16[4,2,2,512,512]{4,3,2,1,0:T(8,128)(2,1)} %green.11, f32[4,2,1,512]{3,2,1,0:T(1,128)S(1)} %broadcast_in_dim.36.gamma, bf16[4,2,256,512]{3,2,1,0:T(8,128)(2,1)S(1)} %copy-done.13, bf16[4,2,256,512]{3,2,1,0:T(8,128)(2,1)} %get-tuple-element.19.refs_1_, ...), custom_call_target="tpu_custom_call" | custom-call | flops 8589934592 | bytes 10485760 | tf_op jit(solution)/shard_map/density/pallas_call | solution.py:348
  234.9 8.1 %all-to-all-start.1 = ((bf16[2,2,32,16,512]{4,3,1,0,2:T(8,128)(2,1)}), bf16[2,2,32,16,512]{4,3,1,0,2:T(8,128)(2,1)}, u32[]{:S(2)}, u32[]{:S(2)}) async-start(bf16[2,2,32,16,512]{4,3,1,0,2:T(8,128)(2,1)} %copy.16), calls=%async_computation.1 | async-start | bytes 4194304 | tf_op jit(solution)/shard_map/all_to_all | solution.py:449
  243.0 11.3 %density.2 = bf16[2,2,512,512]{3,2,1,0:T(8,128)(2,1)S(1)} custom-call(bf16[4,2,2,512,512]{4,3,2,1,0:T(8,128)(2,1)} %green.11, f32[4,2,1,512]{3,2,1,0:T(1,128)S(1)} %broadcast_in_dim.36.gamma, bf16[4,2,256,512]{3,2,1,0:T(8,128)(2,1)S(1)} %copy-done.13, bf16[4,2,256,512]{3,2,1,0:T(8,128)(2,1)} %get-tuple-element.19.refs_1_, ...), custom_call_target="tpu_custom_call" | custom-call | flops 8589934592 | bytes 10485760 | tf_op jit(solution)/shard_map/density/pallas_call | solution.py:348
  255.9 16.9 %all-to-all-done.1 = bf16[2,2,32,16,512]{4,3,1,0,2:T(8,128)(2,1)} async-done(((bf16[2,2,32,16,512]{4,3,1,0,2:T(8,128)(2,1)}), bf16[2,2,32,16,512]{4,3,1,0,2:T(8,128)(2,1)}, u32[]{:S(2)}, u32[]{:S(2)}) %all-to-all-start.1) | async-done | bytes 2097184 | tf_op jit(solution)/shard_map/all_to_all | solution.py:449
  272.8 5.5 %all-to-all-start = ((bf16[2,2,32,16,512]{4,3,1,0,2:T(8,128)(2,1)}), bf16[2,2,32,16,512]{4,3,1,0,2:T(8,128)(2,1)S(1)}, u32[]{:S(2)}, u32[]{:S(2)}) async-start(bf16[2,2,32,16,512]{4,3,1,0,2:T(8,128)(2,1)} %copy.14), calls=%async_computation | async-start | bytes 4194304 | tf_op jit(solution)/shard_map/all_to_all | solution.py:449
  279.0 36.3 %rows.1 = bf16[16,2,2,128,512]{4,3,2,1,0:T(8,128)(2,1)} custom-call(s32[1]{0:T(128)} %bitcast.tile, s32[256]{0:T(256)} %reshape.18.table, bf16[2,2,256,512]{3,2,1,0:T(8,128)(2,1)} %copy-done.2, bf16[2,2,256,512]{3,2,1,0:T(8,128)(2,1)} %copy-done.3, bf16[2,2,256,512]{3,2,1,0:T(8,128)(2,1)} %copy-done.4, ...), custom_call_target="tpu_custom_call" | custom-call | flops 671088640 | bytes 25165824 | tf_op jit(solution)/shard_map/rows/pallas_call | solution.py:292
  (93 shorter events, 36.4 us)
Async XLA Ops:
  0.6 48.9 %collective-permute-start.3 = (bf16[16,128,512]{2,1,0:T(8,128)(2,1)}, bf16[16,128,512]{2,1,0:T(8,128)(2,1)}, u32[]{:S(2)}, u32[]{:S(2)}) collective-permute-start(bf16[16,128,512]{2,1,0:T(8,128)(2,1)} %refs_0_.1), channel_id=1, source_target_pairs={{0,6},{1,7},{2,4},{3,5},{4,2},{5,3},{6,0},{7,1},{8,14},{9,15},{10,... | collective-permute-start | bytes 6291464 | tf_op jit(solution)/shard_map/ppermute | solution.py:384
  9.7 26.3 %collective-permute-start = (bf16[2,2,256,512]{3,2,1,0:T(8,128)(2,1)S(1)}, bf16[2,2,256,512]{3,2,1,0:T(8,128)(2,1)}, u32[]{:S(2)}, u32[]{:S(2)}) collective-permute-start(bf16[2,2,256,512]{3,2,1,0:T(8,128)(2,1)S(1)} %lesser.5), channel_id=1, source_target_pairs={{0,4},{1,5},{2,6},{3,7},{4,0},{5,1},{6,2},{7,3},{8,12},{9,13},{10,... | collective-permute-start | bytes 3145736 | tf_op jit(solution)/shard_map/ppermute | solution.py:384
  13.1 36.4 %collective-permute-start.1 = (bf16[2,2,256,512]{3,2,1,0:T(8,128)(2,1)S(1)}, bf16[2,2,256,512]{3,2,1,0:T(8,128)(2,1)}, u32[]{:S(2)}, u32[]{:S(2)}) collective-permute-start(bf16[2,2,256,512]{3,2,1,0:T(8,128)(2,1)S(1)} %lesser.4.own), channel_id=1, source_target_pairs={{4,12},{8,0},{12,20},{16,8},{20,28},{24,16},{28,36},{32,24},{36,44... | collective-permute-start | bytes 3145736 | tf_op jit(solution)/shard_map/ppermute | solution.py:393
  16.4 40.5 %collective-permute-start.11 = (bf16[2,2,256,512]{3,2,1,0:T(8,128)(2,1)S(1)}, bf16[2,2,256,512]{3,2,1,0:T(8,128)(2,1)}, u32[]{:S(2)}, u32[]{:S(2)}) collective-permute-start(bf16[2,2,256,512]{3,2,1,0:T(8,128)(2,1)S(1)} %lesser.7), channel_id=1, source_target_pairs={{0,4},{1,5},{2,6},{3,7},{4,0},{5,1},{6,2},{7,3},{8,12},{9,13},{10,... | collective-permute-start | bytes 3145736 | tf_op jit(solution)/shard_map/ppermute | solution.py:384
  36.0 24.5 %collective-permute-start.2 = (bf16[2,2,256,512]{3,2,1,0:T(8,128)(2,1)}, bf16[2,2,256,512]{3,2,1,0:T(8,128)(2,1)}, u32[]{:S(2)}, u32[]{:S(2)}) collective-permute-start(bf16[2,2,256,512]{3,2,1,0:T(8,128)(2,1)} %collective-permute-done.got), channel_id=1, source_target_pairs={{0,8},{8,16},{12,4},{16,24},{20,12},{24,32},{28,20},{32,40},{36,28... | collective-permute-start | bytes 3145736 | tf_op jit(solution)/shard_map/ppermute | solution.py:393
  42.5 24.0 %collective-permute-start.12 = (bf16[2,2,256,512]{3,2,1,0:T(8,128)(2,1)S(1)}, bf16[2,2,256,512]{3,2,1,0:T(8,128)(2,1)}, u32[]{:S(2)}, u32[]{:S(2)}) collective-permute-start(bf16[2,2,256,512]{3,2,1,0:T(8,128)(2,1)S(1)} %lesser.6.own), channel_id=1, source_target_pairs={{4,12},{8,0},{12,20},{16,8},{20,28},{24,16},{28,36},{32,24},{36,44... | collective-permute-start | bytes 3145736 | tf_op jit(solution)/shard_map/ppermute | solution.py:393
  49.5 62.6 %collective-permute-start.14 = (bf16[16,128,512]{2,1,0:T(8,128)(2,1)}, bf16[16,128,512]{2,1,0:T(8,128)(2,1)S(1)}, u32[]{:S(2)}, u32[]{:S(2)}) collective-permute-start(bf16[16,128,512]{2,1,0:T(8,128)(2,1)} %collective-permute-done.3.early.refs_2_), channel_id=1, source_target_pairs={{0,1},{1,0},{2,3},{3,2},{4,5},{5,4},{6,7},{7,6},{8,9},{9,8},{10,11... | collective-permute-start | bytes 6291464 | tf_op jit(solution)/shard_map/ppermute | solution.py:384
  49.5 69.9 %collective-permute-start.22 = (bf16[16,128,512]{2,1,0:T(8,128)(2,1)}, bf16[16,128,512]{2,1,0:T(8,128)(2,1)S(1)}, u32[]{:S(2)}, u32[]{:S(2)}) collective-permute-start(bf16[16,128,512]{2,1,0:T(8,128)(2,1)} %refs_0_.1), channel_id=1, source_target_pairs={{0,1},{1,0},{2,3},{3,2},{4,5},{5,4},{6,7},{7,6},{8,9},{9,8},{10,11... | collective-permute-start | bytes 6291464 | tf_op jit(solution)/shard_map/ppermute | solution.py:384
  57.0 25.0 %collective-permute-start.13 = (bf16[2,2,256,512]{3,2,1,0:T(8,128)(2,1)}, bf16[2,2,256,512]{3,2,1,0:T(8,128)(2,1)S(1)}, u32[]{:S(2)}, u32[]{:S(2)}) collective-permute-start(bf16[2,2,256,512]{3,2,1,0:T(8,128)(2,1)} %collective-permute-done.11.got), channel_id=1, source_target_pairs={{0,8},{8,16},{12,4},{16,24},{20,12},{24,32},{28,20},{32,40},{36,28... | collective-permute-start | bytes 3145736 | tf_op jit(solution)/shard_map/ppermute | solution.py:393
  64.8 26.2 %collective-permute-start.4 = (bf16[2,2,256,512]{3,2,1,0:T(8,128)(2,1)S(1)}, bf16[2,2,256,512]{3,2,1,0:T(8,128)(2,1)S(1)}, u32[]{:S(2)}, u32[]{:S(2)}) collective-permute-start(bf16[2,2,256,512]{3,2,1,0:T(8,128)(2,1)S(1)} %get-tuple-element.13), channel_id=1, source_target_pairs={{0,4},{1,5},{2,6},{3,7},{4,0},{5,1},{6,2},{7,3},{8,12},{9,13},{10,... | collective-permute-start | bytes 3145736 | tf_op jit(solution)/shard_map/ppermute | solution.py:384
  66.4 45.7 %collective-permute-start.5 = (bf16[2,2,256,512]{3,2,1,0:T(8,128)(2,1)S(1)}, bf16[2,2,256,512]{3,2,1,0:T(8,128)(2,1)S(1)}, u32[]{:S(2)}, u32[]{:S(2)}) collective-permute-start(bf16[2,2,256,512]{3,2,1,0:T(8,128)(2,1)S(1)} %get-tuple-element.13), channel_id=1, source_target_pairs={{0,6},{1,7},{2,4},{3,5},{4,2},{5,3},{6,0},{7,1},{8,14},{9,15},{10,... | collective-permute-start | bytes 3145736 | tf_op jit(solution)/shard_map/ppermute | solution.py:384
  82.0 39.2 %collective-permute-start.6 = (bf16[2,2,256,512]{3,2,1,0:T(8,128)(2,1)S(1)}, bf16[2,2,256,512]{3,2,1,0:T(8,128)(2,1)}, u32[]{:S(2)}, u32[]{:S(2)}) collective-permute-start(bf16[2,2,256,512]{3,2,1,0:T(8,128)(2,1)S(1)} %get-tuple-element.12.refs_0_.refs_16_), channel_id=1, source_target_pairs={{0,2},{1,3},{2,0},{3,1},{4,6},{5,7},{6,4},{7,5},{8,10},{9,11},{10,... | collective-permute-start | bytes 3145736 | tf_op jit(solution)/shard_map/ppermute | solution.py:384
  91.0 31.0 %collective-permute-start.7 = (bf16[2,2,256,512]{3,2,1,0:T(8,128)(2,1)S(1)}, bf16[2,2,256,512]{3,2,1,0:T(8,128)(2,1)S(1)}, u32[]{:S(2)}, u32[]{:S(2)}) collective-permute-start(bf16[2,2,256,512]{3,2,1,0:T(8,128)(2,1)S(1)} %get-tuple-element.12.refs_0_.refs_16_), channel_id=1, source_target_pairs={{0,1},{1,0},{2,3},{3,2},{4,5},{5,4},{6,7},{7,6},{8,9},{9,8},{10,11... | collective-permute-start | bytes 3145736 | tf_op jit(solution)/shard_map/ppermute | solution.py:384
  112.1 13.7 %collective-permute-start.8 = (bf16[2,2,256,512]{3,2,1,0:T(8,128)(2,1)S(1)}, bf16[2,2,256,512]{3,2,1,0:T(8,128)(2,1)S(1)}, u32[]{:S(2)}, u32[]{:S(2)}) collective-permute-start(bf16[2,2,256,512]{3,2,1,0:T(8,128)(2,1)S(1)} %collective-permute-done.4.refs_1_.refs_17_), channel_id=1, source_target_pairs={{0,1},{1,0},{2,3},{3,2},{4,5},{5,4},{6,7},{7,6},{8,9},{9,8},{10,11... | collective-permute-start | bytes 3145736 | tf_op jit(solution)/shard_map/ppermute | solution.py:384
  120.7 26.1 %collective-permute-start.15 = (bf16[2,2,256,512]{3,2,1,0:T(8,128)(2,1)S(1)}, bf16[2,2,256,512]{3,2,1,0:T(8,128)(2,1)}, u32[]{:S(2)}, u32[]{:S(2)}) collective-permute-start(bf16[2,2,256,512]{3,2,1,0:T(8,128)(2,1)S(1)} %get-tuple-element.15), channel_id=1, source_target_pairs={{0,4},{1,5},{2,6},{3,7},{4,0},{5,1},{6,2},{7,3},{8,12},{9,13},{10,... | collective-permute-start | bytes 3145736 | tf_op jit(solution)/shard_map/ppermute | solution.py:384
  121.1 48.8 %collective-permute-start.16 = (bf16[2,2,256,512]{3,2,1,0:T(8,128)(2,1)S(1)}, bf16[2,2,256,512]{3,2,1,0:T(8,128)(2,1)}, u32[]{:S(2)}, u32[]{:S(2)}) collective-permute-start(bf16[2,2,256,512]{3,2,1,0:T(8,128)(2,1)S(1)} %get-tuple-element.15), channel_id=1, source_target_pairs={{0,6},{1,7},{2,4},{3,5},{4,2},{5,3},{6,0},{7,1},{8,14},{9,15},{10,... | collective-permute-start | bytes 3145736 | tf_op jit(solution)/shard_map/ppermute | solution.py:384
  123.0 46.9 %collective-permute-start.17 = (bf16[2,2,256,512]{3,2,1,0:T(8,128)(2,1)}, bf16[2,2,256,512]{3,2,1,0:T(8,128)(2,1)}, u32[]{:S(2)}, u32[]{:S(2)}) collective-permute-start(bf16[2,2,256,512]{3,2,1,0:T(8,128)(2,1)} %get-tuple-element.14.refs_8_.refs_24_.refs_0_), channel_id=1, source_target_pairs={{0,2},{1,3},{2,0},{3,1},{4,6},{5,7},{6,4},{7,5},{8,10},{9,11},{10,... | collective-permute-start | bytes 3145736 | tf_op jit(solution)/shard_map/ppermute | solution.py:384
  125.8 69.0 %collective-permute-start.10 = (bf16[2,2,256,512]{3,2,1,0:T(8,128)(2,1)}, bf16[2,2,256,512]{3,2,1,0:T(8,128)(2,1)}, u32[]{:S(2)}, u32[]{:S(2)}) collective-permute-start(bf16[2,2,256,512]{3,2,1,0:T(8,128)(2,1)} %collective-permute-done.6.refs_3_.refs_19_), channel_id=1, source_target_pairs={{0,1},{1,0},{2,3},{3,2},{4,5},{5,4},{6,7},{7,6},{8,9},{9,8},{10,11... | collective-permute-start | bytes 3145736 | tf_op jit(solution)/shard_map/ppermute | solution.py:384
  125.8 82.3 %collective-permute-start.18 = (bf16[2,2,256,512]{3,2,1,0:T(8,128)(2,1)}, bf16[2,2,256,512]{3,2,1,0:T(8,128)(2,1)}, u32[]{:S(2)}, u32[]{:S(2)}) collective-permute-start(bf16[2,2,256,512]{3,2,1,0:T(8,128)(2,1)} %get-tuple-element.14.refs_8_.refs_24_.refs_0_), channel_id=1, source_target_pairs={{0,1},{1,0},{2,3},{3,2},{4,5},{5,4},{6,7},{7,6},{8,9},{9,8},{10,11... | collective-permute-start | bytes 3145736 | tf_op jit(solution)/shard_map/ppermute | solution.py:384
  146.8 61.3 %collective-permute-start.19 = (bf16[2,2,256,512]{3,2,1,0:T(8,128)(2,1)}, bf16[2,2,256,512]{3,2,1,0:T(8,128)(2,1)}, u32[]{:S(2)}, u32[]{:S(2)}) collective-permute-start(bf16[2,2,256,512]{3,2,1,0:T(8,128)(2,1)} %collective-permute-done.15.refs_9_.refs_25_.refs_1_), channel_id=1, source_target_pairs={{0,1},{1,0},{2,3},{3,2},{4,5},{5,4},{6,7},{7,6},{8,9},{9,8},{10,11... | collective-permute-start | bytes 3145736 | tf_op jit(solution)/shard_map/ppermute | solution.py:384
  169.9 38.3 %collective-permute-start.20 = (bf16[2,2,256,512]{3,2,1,0:T(8,128)(2,1)}, bf16[2,2,256,512]{3,2,1,0:T(8,128)(2,1)}, u32[]{:S(2)}, u32[]{:S(2)}) collective-permute-start(bf16[2,2,256,512]{3,2,1,0:T(8,128)(2,1)} %collective-permute-done.16.refs_10_.refs_26_.refs_2_), channel_id=1, source_target_pairs={{0,1},{1,0},{2,3},{3,2},{4,5},{5,4},{6,7},{7,6},{8,9},{9,8},{10,11... | collective-permute-start | bytes 3145736 | tf_op jit(solution)/shard_map/ppermute | solution.py:384
  169.9 38.3 %collective-permute-start.21 = (bf16[2,2,256,512]{3,2,1,0:T(8,128)(2,1)}, bf16[2,2,256,512]{3,2,1,0:T(8,128)(2,1)}, u32[]{:S(2)}, u32[]{:S(2)}) collective-permute-start(bf16[2,2,256,512]{3,2,1,0:T(8,128)(2,1)} %collective-permute-done.17.refs_11_.refs_27_.refs_3_), channel_id=1, source_target_pairs={{0,1},{1,0},{2,3},{3,2},{4,5},{5,4},{6,7},{7,6},{8,9},{9,8},{10,11... | collective-permute-start | bytes 3145736 | tf_op jit(solution)/shard_map/ppermute | solution.py:384
  234.9 37.9 %all-to-all-start.1 = ((bf16[2,2,32,16,512]{4,3,1,0,2:T(8,128)(2,1)}), bf16[2,2,32,16,512]{4,3,1,0,2:T(8,128)(2,1)}, u32[]{:S(2)}, u32[]{:S(2)}) async-start(bf16[2,2,32,16,512]{4,3,1,0,2:T(8,128)(2,1)} %copy.16), calls=%async_computation.1 | async-start | bytes 4194304 | tf_op jit(solution)/shard_map/all_to_all | solution.py:449
  272.8 44.4 %all-to-all-start = ((bf16[2,2,32,16,512]{4,3,1,0,2:T(8,128)(2,1)}), bf16[2,2,32,16,512]{4,3,1,0,2:T(8,128)(2,1)S(1)}, u32[]{:S(2)}, u32[]{:S(2)}) async-start(bf16[2,2,32,16,512]{4,3,1,0,2:T(8,128)(2,1)} %copy.14), calls=%async_computation | async-start | bytes 4194304 | tf_op jit(solution)/shard_map/all_to_all | solution.py:449
  (21 other events, 635.0 us)

commit v3 on v2

v3 whole, which is shorter than its diff:
```python
import functools

import jax
import jax.numpy as jnp
from jax import lax
from jax.experimental import pallas as pl
from jax.experimental.pallas import tpu as pltpu
from jax.sharding import PartitionSpec as P

CHUNKS = 2
BOTH = ("energy", "mom")
MIB = 1 << 20
LIGHT = pl.CostEstimate(flops=1, bytes_accessed=1, transcendentals=0)
NT = (((1,), (1,)), ((), ()))


def dot_nt(left, right):
    return lax.dot_general(left, right, NT, preferred_element_type=jnp.float32)


def dot_nn(left, right):
    return jnp.dot(left, right, preferred_element_type=jnp.float32)


def scale(block, gamma):
    return (block.astype(jnp.float32) * gamma).astype(jnp.bfloat16)


def lesser_kernel(chunk, half, green, gamma, out):
    rows = out.shape[2]
    span = slice(chunk * rows, (chunk + 1) * rows)
    gam = gamma[0, 0]
    wide_re = green[0, 0, 0].astype(jnp.float32)
    wide_im = green[0, 0, 1].astype(jnp.float32)
    less = (wide_re - wide_im).astype(jnp.bfloat16)
    more = (wide_re + wide_im).astype(jnp.bfloat16)
    total = dot_nt(scale(green[0, 0, 0, span], gam), less) + dot_nt(
        scale(green[0, 0, 1, span], gam), more
    )
    out[0, 0] = total.astype(jnp.bfloat16)


def packed_lesser(half, green, gamma, chunk):
    energies, norb = green.shape[1], green.shape[-1]
    count = green.shape[0] // 2
    rows = norb // CHUNKS
    return pl.pallas_call(
        functools.partial(lesser_kernel, chunk),
        grid_spec=pltpu.PrefetchScalarGridSpec(
            num_scalar_prefetch=1,
            grid=(count, energies),
            in_specs=[
                pl.BlockSpec((1, 1, 2, norb, norb), lambda k, e, h: (h[0] * count + k, e, 0, 0, 0)),
                pl.BlockSpec((1, 1, 1, norb), lambda k, e, h: (h[0] * count + k, e, 0, 0)),
            ],
            out_specs=pl.BlockSpec((1, 1, rows, norb), lambda k, e, h: (k, e, 0, 0)),
        ),
        out_shape=jax.ShapeDtypeStruct((count, energies, rows, norb), jnp.bfloat16),
        compiler_params=pltpu.CompilerParams(vmem_limit_bytes=32 * MIB),
        cost_estimate=LIGHT,
        name="lesser",
    )(half, green, gamma)


def shift_kernel(place, weights, own, got, own_halo, got_halo, early, *outs):
    rows = own.shape[2]
    step = 16

    def run(first, second, third, fourth, outs):
        def slab(i, carry):
            at = pl.ds(pl.multiple_of(i * step, step), step)
            levels = [
                ref[0, e, at, :].astype(jnp.float32)
                for ref in (first, second, third, fourth)
                for e in range(2)
            ]
            for o in range(4):
                total = weights[0] * levels[o + 3] + weights[1] * levels[o + 4]
                total = total + weights[2] * levels[o + 1] + weights[3] * levels[o]
                outs[o][0, at, :] = total.astype(jnp.bfloat16)
            return carry

        lax.fori_loop(0, rows // step, slab, 0)

    @pl.when(place[0] == 0)
    def _():
        run(got_halo, own, got, own_halo, outs)

    @pl.when(place[0] != 0)
    def _():
        run(own_halo, got, own, got_halo, outs[2:] + outs[:2])


def shifted(place, weights, own, got, own_halo, got_halo, early):
    count, energies, height, norb = own.shape
    rows = height // 2
    block = pl.BlockSpec((1, energies, rows, norb), lambda k, i, p, w: (k, 0, i, 0))
    result = pl.BlockSpec((1, rows, norb), lambda k, i, p, w: (k, i, 0))
    out = jax.ShapeDtypeStruct((count, height, norb), own.dtype)
    return pl.pallas_call(
        shift_kernel,
        grid_spec=pltpu.PrefetchScalarGridSpec(
            num_scalar_prefetch=2,
            grid=(count, height // rows),
            in_specs=[block] * 4 + [pl.BlockSpec(memory_space=pl.ANY)],
            out_specs=[result] * 4,
        ),
        out_shape=[out] * 4,
        compiler_params=pltpu.CompilerParams(vmem_limit_bytes=32 * MIB),
        cost_estimate=LIGHT,
        name="shifted",
    )(place, weights, own, got, own_halo, got_halo, early)


def held_back(arrays, waited):
    return pl.pallas_call(
        lambda *refs: None,
        in_specs=[pl.BlockSpec(memory_space=pl.ANY)] * (len(arrays) + len(waited)),
        out_specs=[pl.BlockSpec(memory_space=pl.ANY)] * len(arrays),
        out_shape=[jax.ShapeDtypeStruct(x.shape, x.dtype) for x in arrays],
        input_output_aliases={i: i for i in range(len(arrays))},
        cost_estimate=LIGHT,
        name="held_back",
    )(*arrays, *waited)


def identity(n):
    rows = lax.broadcasted_iota(jnp.int32, (n, n), 0)
    cols = lax.broadcasted_iota(jnp.int32, (n, n), 1)
    return (rows == cols).astype(jnp.float32).astype(jnp.bfloat16)


def fold_kernel(tiles, *refs):
    parts, (out, out_t) = refs[:4], refs[4:]
    points, height, norb = parts[0].shape
    turn = identity(norb // 2)
    for s in range(4):

        @pl.when(pl.program_id(0) == s)
        def _(part=parts[s]):
            for q in range(points):
                out[q] = part[q]
                for b in range(2):
                    span = slice(b * (norb // 2), (b + 1) * (norb // 2))
                    out_t[q, span, :] = dot_nt(turn, part[q, :, span]).astype(jnp.bfloat16)


def folded(tiles, parts):
    points, height, norb = parts[0].shape
    some = points // 4
    given = pl.BlockSpec((some, height, norb), lambda s, q, t: (q, 0, 0))
    whole = jax.ShapeDtypeStruct((points, norb, norb), jnp.bfloat16)
    return pl.pallas_call(
        fold_kernel,
        grid_spec=pltpu.PrefetchScalarGridSpec(
            num_scalar_prefetch=1,
            grid=(4, points // some),
            in_specs=[given] * 4,
            out_specs=[
                pl.BlockSpec((some, height, norb), lambda s, q, t: (q, t[s], 0)),
                pl.BlockSpec((some, norb, height), lambda s, q, t: (q, 0, t[s])),
            ],
        ),
        out_shape=[whole, whole],
        compiler_params=pltpu.CompilerParams(vmem_limit_bytes=48 * MIB),
        cost_estimate=LIGHT,
        name="fold",
    )(tiles, *parts)


def add_products(targets, streams, picks, donor, factor, at, store):
    acc = [[None] * streams for _ in range(targets)]
    kept = {}
    for quad in range(4):
        held = [[donor(4 * quad + d, n, at) for n in range(streams)] for d in range(4)]
        for t in range(targets):
            c = [factor[picks(t, 4 * quad + d), at[0], at[1]] for d in range(4)]
            for n in range(streams):
                part = (c[0] * held[0][n] + c[1] * held[1][n]) + (
                    c[2] * held[2][n] + c[3] * held[3][n]
                )
                if quad % 2 == 0:
                    kept[t, n] = part
                    continue
                part = (kept.pop((t, n)) + part).astype(jnp.float32)
                acc[t][n] = part if acc[t][n] is None else acc[t][n] + part
    for t in range(targets):
        for n in range(streams):
            store(t, n, at, acc[t][n])


def home_kernel(table, *refs):
    sources, (coup, coup_t, out, out_t) = refs[:8], refs[8:]
    targets, height, norb = out.shape

    def picks(t, d):
        return table[t * 16 + d]

    def donor(d, n, at):
        return sources[d // 2][d % 2, at[0], at[1]]

    def into(ref):
        def store(t, n, at, value):
            ref[t, at[0], at[1]] = value.astype(jnp.bfloat16)

        return store

    def slab(i, carry):
        at = (pl.ds(pl.multiple_of(i * 16, 16), 16), slice(None))
        add_products(targets, 1, picks, donor, coup, at, into(out))
        add_products(targets, 1, picks, donor, coup_t, at, into(out_t))
        return carry

    lax.fori_loop(0, height // 16, slab, 0)


def home_sums(table, sources, coup, coup_t, chunk, targets):
    _, rows, norb = sources[0].shape
    points = coup.shape[0]
    height = 64
    steps = rows // height
    given = pl.BlockSpec((2, height, norb), lambda i, q: (0, i, 0))
    factor = pl.BlockSpec((points, height, norb), lambda i, q: (0, chunk * steps + i, 0))
    result = pl.BlockSpec((targets, height, norb), lambda i, q: (0, i, 0))
    out = jax.ShapeDtypeStruct((targets, rows, norb), jnp.bfloat16)
    return pl.pallas_call(
        home_kernel,
        grid_spec=pltpu.PrefetchScalarGridSpec(
            num_scalar_prefetch=1,
            grid=(steps,),
            in_specs=[given] * 8 + [factor] * 2,
            out_specs=[result] * 2,
        ),
        out_shape=[out, out],
        compiler_params=pltpu.CompilerParams(vmem_limit_bytes=32 * MIB),
        cost_estimate=LIGHT,
        name="home",
    )(table, *sources, coup, coup_t)


def rows_kernel(tile, table, *refs):
    rows_of, cols_of = refs[:16], refs[16:32]
    coup, out, source = refs[32], refs[-2], refs[-1]
    targets, _, _, height, norb = out.shape
    group = pl.program_id(0) * targets
    part = norb // CHUNKS

    for c in range(CHUNKS):

        @pl.when((pl.program_id(0) == 0) & (tile[0] // CHUNKS == c))
        def _(held=rows_of[8 * c : 8 * c + 8]):
            turn = identity(height)

            for d in range(16):
                for b in range(CHUNKS):
                    span = slice(b * part, (b + 1) * part)
                    straight = held[d // 2][d % 2, :, span].astype(jnp.float32)
                    turned = turn_over(turn, cols_of[8 * b + d // 2][d % 2])
                    source[d, 0, :, span] = (straight + turned).astype(jnp.bfloat16)
                    source[d, 1, :, span] = (straight - turned).astype(jnp.bfloat16)

    def picks(t, d):
        return table[(group + t) * 16 + d]

    def donor(d, n, at):
        return source[d, n, at[0], at[1]]

    def store(t, n, at, value):
        out[t, 0, n, at[0], at[1]] = value.astype(jnp.bfloat16)

    def slab(i, carry):
        at = (
            pl.ds(pl.multiple_of(i // 2 * 16, 16), 16),
            pl.ds(pl.multiple_of(i % 2 * (norb // 2), norb // 2), norb // 2),
        )
        add_products(targets, 2, picks, donor, coup, at, store)
        return carry

    lax.fori_loop(0, height // 16 * 2, slab, 0)


def turn_over(turn, block):
    return dot_nt(turn, block)


def row_sums(tile, table, chunks, coupling, targets, energy, before):
    _, part, norb = chunks[0][0].shape
    points, height, _ = coupling.shape
    steps = part // height
    row_block = pl.BlockSpec((2, height, norb), lambda g, t, q: (0, t[0] % steps, 0))
    col_block = pl.BlockSpec((2, part, height), lambda g, t, q: (0, 0, t[0]))
    sources = [x for chunk in chunks for x in chunk]
    out = jax.ShapeDtypeStruct((points, 2, 2, height, norb), jnp.bfloat16)
    given = [tile, table, *sources, *sources, coupling] + ([] if before is None else [before])
    return pl.pallas_call(
        rows_kernel,
        grid_spec=pltpu.PrefetchScalarGridSpec(
            num_scalar_prefetch=2,
            grid=(points // targets,),
            in_specs=[row_block] * 16
            + [col_block] * 16
            + [pl.BlockSpec((points, height, norb), lambda g, t, q: (0, 0, 0))]
            + ([] if before is None else [pl.BlockSpec(memory_space=pl.ANY)]),
            out_specs=pl.BlockSpec(
                (targets, 1, 2, height, norb), lambda g, t, q: (g, energy, 0, 0, 0)
            ),
            scratch_shapes=[pltpu.VMEM((16, 2, height, norb), jnp.bfloat16)],
        ),
        out_shape=out,
        input_output_aliases={} if before is None else {len(given) - 1: 0},
        compiler_params=pltpu.CompilerParams(vmem_limit_bytes=40 * MIB),
        cost_estimate=LIGHT,
        name="rows",
    )(*given)


def density_kernel(inverse, green, gamma, *refs):
    us, vs, rest = refs[:CHUNKS], refs[CHUNKS : 2 * CHUNKS], refs[2 * CHUNKS :]
    g_re, g_im = green[0, 0, 0], green[0, 0, 1]
    gam = gamma[0, 0]
    wide_re, wide_im = g_re.astype(jnp.float32), g_im.astype(jnp.float32)
    less = (wide_re - wide_im).astype(jnp.bfloat16)
    more = (wide_re + wide_im).astype(jnp.bfloat16)
    u = jnp.concatenate([ref[0] for ref in us], axis=0)
    v = jnp.concatenate([ref[0] for ref in vs], axis=0)
    m_re = dot_nn(less, u) + dot_nt(more, v) + scale(g_re, gam).astype(jnp.float32)
    m_im = dot_nn(more, u) - dot_nt(less, v) + scale(g_im, gam).astype(jnp.float32)
    m_re, m_im = m_re.astype(jnp.bfloat16), m_im.astype(jnp.bfloat16)
    d_re = dot_nt(m_re, g_re) + dot_nt(m_im, g_im)
    d_im = dot_nt(m_im, g_re) - dot_nt(m_re, g_im)
    out = rest[-1]
    if len(rest) == 1:
        out[0, 0] = d_re
        out[0, 1] = d_im
    else:
        shape = out.shape[2:]
        out[0, 0] = ((d_re + rest[0][0, 0]) * inverse).astype(jnp.bfloat16).reshape(shape)
        out[0, 1] = ((d_im + rest[0][0, 1]) * inverse).astype(jnp.bfloat16).reshape(shape)


def partial_density(green, gamma, sums, sums_t, energy, before, inverse, owners):
    count, _, _, norb, _ = green.shape
    part = pl.BlockSpec((1, norb // CHUNKS, norb), lambda k: (k, 0, 0))
    whole = pl.BlockSpec((1, 2, norb, norb), lambda k: (k, 0, 0, 0))
    if before is None:
        out_spec = whole
        out = jax.ShapeDtypeStruct((count, 2, norb, norb), jnp.float32)
    else:
        rows = norb // owners
        out_spec = pl.BlockSpec((1, 2, owners, rows, norb), lambda k: (k, 0, 0, 0, 0))
        out = jax.ShapeDtypeStruct((count, 2, owners, rows, norb), jnp.bfloat16)
    return pl.pallas_call(
        functools.partial(density_kernel, inverse),
        grid=(count,),
        in_specs=[
            pl.BlockSpec((1, 1, 2, norb, norb), lambda k: (k, energy, 0, 0, 0)),
            pl.BlockSpec((1, 1, 1, norb), lambda k: (k, energy, 0, 0)),
        ]
        + [part] * (2 * CHUNKS)
        + ([] if before is None else [whole]),
        out_specs=out_spec,
        out_shape=out,
        compiler_params=pltpu.CompilerParams(vmem_limit_bytes=40 * MIB),
        cost_estimate=LIGHT,
        name="density",
    )(green, gamma, *sums, *sums_t, *([] if before is None else [before]))


def on_device(green, broadening, coupling, shift_steps, mode_weight, occupation, momentum_map):
    n_energy, n_mom = lax.axis_size("energy"), lax.axis_size("mom")
    pairs = n_energy // 2
    local_k, local_e = green.shape[:2]
    half = local_k // 2
    points = momentum_map.shape[1]
    energy, mom = lax.axis_index("energy"), lax.axis_index("mom")
    x_lo = energy % 2

    def flip(x, lo, mo):
        perm = [
            (e * n_mom + m, (e ^ lo) * n_mom + (m ^ mo))
            for e in range(n_energy)
            for m in range(n_mom)
        ]
        return lax.ppermute(x, BOTH, perm)

    def along_pairs(x, step_of_low):
        moves = []
        for j in range(pairs):
            for lo in range(2):
                to = j + (step_of_low if lo == 0 else -step_of_low)
                if 0 <= to < pairs:
                    moves.append((2 * j + lo, 2 * to + lo))
        return lax.ppermute(x, "energy", moves)

    def weight_of(step, factor):
        return 0.5 * jnp.sum(jnp.where(shift_steps == step, mode_weight * factor, 0.0))

    weights = jnp.stack(
        [weight_of(s, occupation + 1.0) for s in (1, 2)] + [weight_of(s, occupation) for s in (1, 2)]
    ).astype(jnp.float32)

    gamma = broadening[:, :, None, :]
    place = x_lo.astype(jnp.int32)[None]
    tile = mom.astype(jnp.int32)

    moves = [(0, 0), (1, 0), (1, 2), (0, 2)]
    moves = moves + [(lo, mo ^ 1) for lo, mo in moves]
    donors = jnp.stack(
        [(mom ^ mo) * local_k + (x_lo ^ lo) * half + kk for lo, mo in moves for kk in range(half)]
    ).astype(jnp.int32)
    table = jnp.sum(
        jnp.where(
            momentum_map[:, :, None] == donors[None, None, :],
            jnp.arange(points, dtype=jnp.int32)[None, :, None],
            0,
        ),
        axis=1,
    ).astype(jnp.int32)
    table_home = lax.dynamic_slice_in_dim(table, mom * local_k, local_k, 0).reshape(-1)

    coup_b = flip(coupling, 1, 2)
    coup_c = flip(coupling, 0, 1)

    sent = [packed_lesser(1 - place, green, gamma, c) for c in range(CHUNKS)]
    got = [flip(x, 1, 0) for x in sent]
    own = [packed_lesser(place, green, gamma, c) for c in range(CHUNKS)]
    own_halo = [along_pairs(x, -1) for x in own]
    got_halo = [along_pairs(x, 1) for x in got]
    (coup_b,) = held_back([coup_b], [got[1], own[1]])
    coup_bc = flip(coup_b, 0, 1)

    coup, coup_t = folded(
        jnp.arange(4, dtype=jnp.int32) ^ tile, [coupling, coup_c, coup_b, coup_bc]
    )
    early = (coup_bc, coup_t)
    near = [[None] * CHUNKS for _ in range(local_e)]
    for c in range(CHUNKS):
        mine_other = shifted(place, weights, own[c], got[c], own_halo[c], got_halo[c], early[c])
        for e in range(local_e):
            mine, other = mine_other[e], mine_other[2 + e]
            near[e][c] = [mine, flip(other, 1, 0), flip(other, 1, 2), flip(mine, 0, 2)]
        last = mine

    def with_other_core(block, waited):
        block = block[:1] + list(held_back(block[1:], waited))
        return block + [flip(x, 0, 1) for x in block]

    def sums_of(block, c):
        return home_sums(table_home, block, coup, coup_t, c, local_k)

    inverse = 1.0 / (local_e * n_energy)

    def density_of(sums, e, before):
        us, vs = [s[0] for s in sums], [s[1] for s in sums]
        return partial_density(green, gamma, us, vs, e, before, inverse, n_energy)

    def rows_at(chunks, e, before):
        return row_sums(tile[None], table.reshape(-1), chunks, coupling, local_k, e, before)

    first = [with_other_core(near[0][c], [last]) for c in range(CHUNKS)]
    sums = [sums_of(first[c], c) for c in range(CHUNKS)]
    density = density_of(sums, 0, None)
    self_energy = rows_at(first, 0, None)

    second, sums = [], []
    waited = [density]
    for c in range(CHUNKS):
        second.append(with_other_core(near[1][c], waited))
        sums.append(sums_of(second[c], c))
        waited = [sums[c][0], self_energy]
    density = density_of(sums, 1, density)
    parts = lax.all_to_all(density, "energy", split_axis=2, concat_axis=2, tiled=True)
    self_energy = rows_at(second, 1, self_energy)
    density = jnp.transpose(jnp.sum(parts.astype(jnp.float32), axis=2), (2, 0, 1, 3))
    return (self_energy, density)


def solution(mesh):
    return jax.shard_map(
        on_device,
        mesh=mesh,
        in_specs=(
            P("mom", "energy", None, None, None),
            P("mom", "energy", None),
            P(None, "mom", None),
            P(),
            P(),
            P(),
            P(),
        ),
        out_specs=(P(None, "energy", None, "mom", None), P("energy", "mom", None, None)),
        check_vma=False,
    )
```

time: 320 us -> 351 us (1.097); the launches traced: 319 us -> 344 us
  local copies, waits for them, and re-layouts: 17.4 us -> 51.8 us
  waiting for transfers between devices: 132 us -> 116 us
  starting transfers between devices: 38.6 us -> 48.6 us
  Pallas kernels: 124 us -> 120 us
    ppermute x19 -> x33, waiting for transfers between devices: 97.9 us -> 57.4 us  [flip(): return lax.ppermute(x, BOTH, perm)]
    unnamed x41 -> x111, local copies, waits for them, and re-layouts: 12.7 us -> 48.1 us
    all_to_all x2 -> x1, waiting for transfers between devices: 16.9 us -> 40.1 us  [on_device(): lax.all_to_all(density, 'energy', split_axis=2, concat_axis=2, tiled=True)]
    ppermute x19 -> x33, starting transfers between devices: 14.4 us -> 26.5 us  [flip(): return lax.ppermute(x, BOTH, perm)]
    pallas_call x1 -> x2, Pallas kernels: 36.3 us -> 28 us  [row_sums(): pl.pallas_call(rows_kernel, grid_spec=pltpu.PrefetchScalarGridSpec(num_sc...]
    all_to_all x2 -> x1, starting transfers between devices: 13.7 us -> 9.26 us  [on_device(): lax.all_to_all(density, 'energy', split_axis=2, concat_axis=2, tiled=True)]
    reshape x3 -> x1, local copies, waits for them, and re-layouts: 3.78 us -> 0.08 us  [rows_at(): table.reshape(-1)]
    pallas_call x2 -> x4, Pallas kernels: 27.1 us -> 28 us  [home_sums(): pl.pallas_call(home_kernel, grid_spec=pltpu.PrefetchScalarGridSpec(num_sc...]
  transfers between devices with their start and end apart: 25 -> 38, of which waited for: 10 -> 12; matrix products, arithmetic and copies ran while one was open for 2% -> 1% of each run, Pallas kernels for 31% -> 29%
where the time goes in v3:
time: 351 us; the launch traced here: 344 us
  Pallas kernels  120 us (34%)
  waiting for transfers between devices  116 us (33%)
  local copies, waits for them, and re-layouts  51.8 us (15%)
  starting transfers between devices  48.6 us (14%)
  other arithmetic  3.98 us (1%)
  between operations  3.68 us (1%)
    ppermute x33, waiting for transfers between devices, flip(): return lax.ppermute(x, BOTH, perm)  57.4 us
    unnamed x111, local copies, waits for them, and re-layouts  48.1 us
    all_to_all x1, waiting for transfers between devices, on_device(): lax.all_to_all(density, 'energy', split_axis=2, concat_axis=2, tiled=True)  40.1 us
    pallas_call x2, Pallas kernels, row_sums(): pl.pallas_call(rows_kernel, grid_spec=pltpu.PrefetchScalarGridSpec(num_sc...  28 us
    pallas_call x4, Pallas kernels, home_sums(): pl.pallas_call(home_kernel, grid_spec=pltpu.PrefetchScalarGridSpec(num_sc...  28 us
    ppermute x33, starting transfers between devices, flip(): return lax.ppermute(x, BOTH, perm)  26.5 us
    pallas_call x2, Pallas kernels, partial_density(): pl.pallas_call(functools.partial(density_kernel, inverse), grid=(count,),...  22.7 us
    pallas_call x1, Pallas kernels, folded(): pl.pallas_call(fold_kernel, grid_spec=pltpu.PrefetchScalarGridSpec(num_sc...  22.2 us
  transfers between devices with their start and end apart: 38, of which 12 were waited for; matrix products, arithmetic and copies ran while one was open for 1% of the time, Pallas kernels for 29%

profile of v3, /device:TPU:0, one launch (start us, length us, event | category | flops | bytes accessed | tf_op | source)
XLA Modules:
  0.0 344.3 jit_solution(9479721305707434649)
XLA Ops:
  17.7 18.3 %collective-permute-done.4.refs_1_.got = bf16[2,2,256,512]{3,2,1,0:T(8,128)(2,1)} collective-permute-done((bf16[2,2,256,512]{3,2,1,0:T(8,128)(2,1)S(1)}, bf16[2,2,256,512]{3,2,1,0:T(8,128)(2,1)}, u32[]{:S(2)}, u32[]{:S(2)}) %collective-permute-start.4) | collective-permute-done | bytes 1048608 | tf_op jit(solution)/shard_map/ppermute | solution.py:384
  36.0 13.5 %collective-permute-done.3.refs_0_ = bf16[16,128,512]{2,1,0:T(8,128)(2,1)} collective-permute-done((bf16[16,128,512]{2,1,0:T(8,128)(2,1)}, bf16[16,128,512]{2,1,0:T(8,128)(2,1)}, u32[]{:S(2)}, u32[]{:S(2)}) %collective-permute-start.3) | collective-permute-done | bytes 2097184 | tf_op jit(solution)/shard_map/ppermute | solution.py:384
  50.1 3.4 copy-done.1
  57.8 5.5 %collective-permute-start.2 = (bf16[2,2,256,512]{3,2,1,0:T(8,128)(2,1)}, bf16[2,2,256,512]{3,2,1,0:T(8,128)(2,1)}, u32[]{:S(2)}, u32[]{:S(2)}) collective-permute-start(bf16[2,2,256,512]{3,2,1,0:T(8,128)(2,1)} %collective-permute-done.got), channel_id=1, source_target_pairs={{0,8},{8,16},{12,4},{16,24},{20,12},{24,32},{28,20},{32,40},{36,28... | collective-permute-start | bytes 3145736 | tf_op jit(solution)/shard_map/ppermute | solution.py:393
  64.6 18.8 %collective-permute-done.1.own_halo = bf16[2,2,256,512]{3,2,1,0:T(8,128)(2,1)S(1)} collective-permute-done((bf16[2,2,256,512]{3,2,1,0:T(8,128)(2,1)S(1)}, bf16[2,2,256,512]{3,2,1,0:T(8,128)(2,1)S(1)}, u32[]{:S(2)}, u32[]{:S(2)}) %collective-permute-start.1) | collective-permute-done | bytes 1048608 | tf_op jit(solution)/shard_map/ppermute | solution.py:393
  84.4 4.7 %collective-permute-start.13 = (bf16[2,2,256,512]{3,2,1,0:T(8,128)(2,1)}, bf16[2,2,256,512]{3,2,1,0:T(8,128)(2,1)}, u32[]{:S(2)}, u32[]{:S(2)}) collective-permute-start(bf16[2,2,256,512]{3,2,1,0:T(8,128)(2,1)} %collective-permute-done.4.refs_1_.got), channel_id=1, source_target_pairs={{0,8},{8,16},{12,4},{16,24},{20,12},{24,32},{28,20},{32,40},{36,28... | collective-permute-start | bytes 3145736 | tf_op jit(solution)/shard_map/ppermute | solution.py:393
  94.8 5.0 %shifted.2 = (bf16[2,256,512]{2,1,0:T(8,128)(2,1)}, bf16[2,256,512]{2,1,0:T(8,128)(2,1)}, bf16[2,256,512]{2,1,0:T(8,128)(2,1)}, bf16[2,256,512]{2,1,0:T(8,128)(2,1)S(1)}) custom-call(s32[1]{0:T(128)} %bitcast.17.half.place, f32[4]{0:T(128)S(1)} %pad_maximum_fusion.weights, bf16[2,2,256,512]{3,2,1,0:T(8,128)(2,1)S(1)} %copy-done.38, ...), custom_call_target="tpu_custom_call" | custom-call | flops 1 | bytes 1 | tf_op jit(solution)/shard_map/shifted/pallas_call | solution.py:100
  105.3 22.2 %fold.1 = (bf16[16,512,512]{2,1,0:T(8,128)(2,1)}, bf16[16,512,512]{2,1,0:T(8,128)(2,1)}) custom-call(s32[4]{0:T(128)S(1)} %iota_xor_fusion.tiles, bf16[16,128,512]{2,1,0:T(8,128)(2,1)S(1)} %copy-done.7, bf16[16,128,512]{2,1,0:T(8,128)(2,1)} %collective-permute-done.14.refs_1_, bf16[16,128,512]{2,1,0:T(8,128)(2,1)} %held_back.5.refs_2_, ...), custom_call_target="tpu_custom_call" | custom-call | flops 1 | bytes 1 | tf_op jit(solution)/shard_map/fold/pallas_call | solution.py:153
  127.6 3.4 copy-done.2
  131.0 5.1 %shifted.3 = (bf16[2,256,512]{2,1,0:T(8,128)(2,1)}, bf16[2,256,512]{2,1,0:T(8,128)(2,1)S(1)}, bf16[2,256,512]{2,1,0:T(8,128)(2,1)}, bf16[2,256,512]{2,1,0:T(8,128)(2,1)S(1)}) custom-call(s32[1]{0:T(128)} %bitcast.17.half.place, f32[4]{0:T(128)S(1)} %pad_maximum_fusion.weights, bf16[2,2,256,512]{3,2,1,0:T(8,128)(2,1)S(1)} %copy-done.11, ...), custom_call_target="tpu_custom_call" | custom-call | flops 1 | bytes 1 | tf_op jit(solution)/shard_map/shifted/pallas_call | solution.py:100
  138.2 4.1 %collective-permute-start.21 = (bf16[2,256,512]{2,1,0:T(8,128)(2,1)}, bf16[2,256,512]{2,1,0:T(8,128)(2,1)}, u32[]{:S(2)}, u32[]{:S(2)}) collective-permute-start(bf16[2,256,512]{2,1,0:T(8,128)(2,1)} %get-tuple-element.43.refs_0_.refs_8_.refs_24_), channel_id=1, source_target_pairs={{0,2},{1,3},{2,0},{3,1},{4,6},{5,7},{6,4},{7,5},{8,10},{9,11},{10,... | collective-permute-start | bytes 1572872 | tf_op jit(solution)/shard_map/ppermute | solution.py:384
  142.9 10.2 %collective-permute-done.20.refs_1_ = bf16[2,256,512]{2,1,0:T(8,128)(2,1)S(1)} collective-permute-done((bf16[2,256,512]{2,1,0:T(8,128)(2,1)}, bf16[2,256,512]{2,1,0:T(8,128)(2,1)S(1)}, u32[]{:S(2)}, u32[]{:S(2)}) %collective-permute-start.20) | collective-permute-done | bytes 524320 | tf_op jit(solution)/shard_map/ppermute | solution.py:384
  153.0 9.8 %collective-permute-done.21.refs_2_ = bf16[2,256,512]{2,1,0:T(8,128)(2,1)} collective-permute-done((bf16[2,256,512]{2,1,0:T(8,128)(2,1)}, bf16[2,256,512]{2,1,0:T(8,128)(2,1)}, u32[]{:S(2)}, u32[]{:S(2)}) %collective-permute-start.21) | collective-permute-done | bytes 524320 | tf_op jit(solution)/shard_map/ppermute | solution.py:384
  171.6 3.4 copy-done.3
  179.2 6.9 %home.5 = (bf16[4,256,512]{2,1,0:T(8,128)(2,1)S(1)}, bf16[4,256,512]{2,1,0:T(8,128)(2,1)S(1)}) custom-call(s32[64]{0:T(128)S(1)} %reshape.14.table, bf16[2,256,512]{2,1,0:T(8,128)(2,1)} %get-tuple-element.43.refs_0_.refs_8_.refs_24_, bf16[2,256,512]{2,1,0:T(8,128)(2,1)S(1)} %copy-done.18, bf16[2,256,512]{2,1,0:T(8,128)(2,1)S(1)} %copy-done.15, ...), custom_call_target="tpu_custom_call" | custom-call | flops 1 | bytes 1 | tf_op jit(solution)/shard_map/home/pallas_call | solution.py:226
  186.4 7.1 %home.4 = (bf16[4,256,512]{2,1,0:T(8,128)(2,1)S(1)}, bf16[4,256,512]{2,1,0:T(8,128)(2,1)S(1)}) custom-call(s32[64]{0:T(128)S(1)} %reshape.14.table, bf16[2,256,512]{2,1,0:T(8,128)(2,1)} %get-tuple-element.34.refs_0_.refs_16_, bf16[2,256,512]{2,1,0:T(8,128)(2,1)} %get-tuple-element.38.refs_1_.refs_17_, ...), custom_call_target="tpu_custom_call" | custom-call | flops 1 | bytes 1 | tf_op jit(solution)/shard_map/home/pallas_call | solution.py:226
  193.5 11.1 %density.2.refs_3_.refs_4_ = f32[4,2,512,512]{3,2,1,0:T(8,128)S(1)} custom-call(bf16[4,2,2,512,512]{4,3,2,1,0:T(8,128)(2,1)} %green.11, f32[4,2,1,512]{3,2,1,0:T(1,128)S(1)} %broadcast_in_dim.37.gamma, bf16[4,256,512]{2,1,0:T(8,128)(2,1)S(1)} %get-tuple-element.42.refs_0_, bf16[4,256,512]{2,1,0:T(8,128)(2,1)S(1)} %get-tuple-element.48.refs_1_, ...), custom_call_target="tpu_custom_call" | custom-call | flops 1 | bytes 1 | tf_op jit(solution)/shard_map/density/pallas_call | solution.py:352
  221.0 14.3 %rows.2.refs_4_.refs_33_ = bf16[16,2,2,128,512]{4,3,2,1,0:T(8,128)(2,1)} custom-call(s32[1]{0:T(128)} %bitcast.tile, s32[256]{0:T(256)S(1)} %reshape.13.table, bf16[2,256,512]{2,1,0:T(8,128)(2,1)} %get-tuple-element.34.refs_0_.refs_16_, bf16[2,256,512]{2,1,0:T(8,128)(2,1)} %get-tuple-element.38.refs_1_.refs_17_, ...), custom_call_target="tpu_custom_call" | custom-call | flops 1 | bytes 1 | tf_op jit(solution)/shard_map/rows/pallas_call | solution.py:295
  235.4 7.0 %home.6 = (bf16[4,256,512]{2,1,0:T(8,128)(2,1)S(1)}, bf16[4,256,512]{2,1,0:T(8,128)(2,1)S(1)}) custom-call(s32[64]{0:T(128)S(1)} %reshape.14.table, bf16[2,256,512]{2,1,0:T(8,128)(2,1)} %get-tuple-element.32.refs_0_.refs_16_, bf16[2,256,512]{2,1,0:T(8,128)(2,1)} %get-tuple-element.51.refs_1_.refs_17_, bf16[2,256,512]{2,1,0:T(8,128)(2,1)S(1)} %copy-done.13, ...), custom_call_target="tpu_custom_call" | custom-call | flops 1 | bytes 1 | tf_op jit(solution)/shard_map/home/pallas_call | solution.py:226
  251.5 7.0 %home.7 = (bf16[4,256,512]{2,1,0:T(8,128)(2,1)S(1)}, bf16[4,256,512]{2,1,0:T(8,128)(2,1)S(1)}) custom-call(s32[64]{0:T(128)S(1)} %reshape.14.table, bf16[2,256,512]{2,1,0:T(8,128)(2,1)S(1)} %copy-done.9, bf16[2,256,512]{2,1,0:T(8,128)(2,1)} %get-tuple-element.56.refs_9_.refs_25_.refs_1_, bf16[2,256,512]{2,1,0:T(8,128)(2,1)} %get-tuple-element.57.refs_10_.refs_26_.refs_2_, ...), custom_call_target="tpu_custom_call" | custom-call | flops 1 | bytes 1 | tf_op jit(solution)/shard_map/home/pallas_call | solution.py:226
  258.6 11.6 %density.3 = bf16[4,2,32,16,512]{4,3,2,1,0:T(8,128)(2,1)S(1)} custom-call(bf16[4,2,2,512,512]{4,3,2,1,0:T(8,128)(2,1)} %green.11, f32[4,2,1,512]{3,2,1,0:T(1,128)S(1)} %broadcast_in_dim.37.gamma, bf16[4,256,512]{2,1,0:T(8,128)(2,1)S(1)} %copy-done.40, bf16[4,256,512]{2,1,0:T(8,128)(2,1)S(1)} %get-tuple-element.59.refs_1_, ...), custom_call_target="tpu_custom_call" | custom-call | flops 1 | bytes 1 | tf_op jit(solution)/shard_map/density/pallas_call | solution.py:352
  272.9 9.3 %all-to-all-start = ((bf16[4,2,32,16,512]{4,3,1,0,2:T(8,128)(2,1)}), bf16[4,2,32,16,512]{4,3,1,0,2:T(8,128)(2,1)}, u32[]{:S(2)}, u32[]{:S(2)}) async-start(bf16[4,2,32,16,512]{4,3,1,0,2:T(8,128)(2,1)} %copy.26), calls=%async_computation | async-start | bytes 8388608 | tf_op jit(solution)/shard_map/all_to_all | solution.py:472
  286.4 13.8 %rows.3 = bf16[16,2,2,128,512]{4,3,2,1,0:T(8,128)(2,1)} custom-call(s32[1]{0:T(128)} %bitcast.tile, s32[256]{0:T(256)S(1)} %reshape.13.table, bf16[2,256,512]{2,1,0:T(8,128)(2,1)} %get-tuple-element.32.refs_0_.refs_16_, bf16[2,256,512]{2,1,0:T(8,128)(2,1)} %get-tuple-element.51.refs_1_.refs_17_, ...), custom_call_target="tpu_custom_call", output_to_operand_aliasing={{}: (35, {})} | custom-call | flops 1 | bytes 1 | tf_op jit(solution)/shard_map/rows/pallas_call | solution.py:295
  300.1 40.1 %all-to-all-done = bf16[4,2,32,16,512]{4,3,1,0,2:T(8,128)(2,1)} async-done(((bf16[4,2,32,16,512]{4,3,1,0,2:T(8,128)(2,1)}), bf16[4,2,32,16,512]{4,3,1,0,2:T(8,128)(2,1)}, u32[]{:S(2)}, u32[]{:S(2)}) %all-to-all-start) | async-done | bytes 4194336 | tf_op jit(solution)/shard_map/all_to_all | solution.py:472
  (196 shorter events, 85.2 us)
Async XLA Ops:
  0.6 48.9 %collective-permute-start.3 = (bf16[16,128,512]{2,1,0:T(8,128)(2,1)}, bf16[16,128,512]{2,1,0:T(8,128)(2,1)}, u32[]{:S(2)}, u32[]{:S(2)}) collective-permute-start(bf16[16,128,512]{2,1,0:T(8,128)(2,1)} %refs_32_.3), channel_id=1, source_target_pairs={{0,6},{1,7},{2,4},{3,5},{4,2},{5,3},{6,0},{7,1},{8,14},{9,15},{10,... | collective-permute-start | bytes 6291464 | tf_op jit(solution)/shard_map/ppermute | solution.py:384
  9.7 26.3 %collective-permute-start.4 = (bf16[2,2,256,512]{3,2,1,0:T(8,128)(2,1)S(1)}, bf16[2,2,256,512]{3,2,1,0:T(8,128)(2,1)}, u32[]{:S(2)}, u32[]{:S(2)}) collective-permute-start(bf16[2,2,256,512]{3,2,1,0:T(8,128)(2,1)S(1)} %lesser.6), channel_id=1, source_target_pairs={{0,4},{1,5},{2,6},{3,7},{4,0},{5,1},{6,2},{7,3},{8,12},{9,13},{10,... | collective-permute-start | bytes 3145736 | tf_op jit(solution)/shard_map/ppermute | solution.py:384
  12.9 44.9 %collective-permute-start = (bf16[2,2,256,512]{3,2,1,0:T(8,128)(2,1)}, bf16[2,2,256,512]{3,2,1,0:T(8,128)(2,1)}, u32[]{:S(2)}, u32[]{:S(2)}) collective-permute-start(bf16[2,2,256,512]{3,2,1,0:T(8,128)(2,1)} %lesser.5), channel_id=1, source_target_pairs={{0,4},{1,5},{2,6},{3,7},{4,0},{5,1},{6,2},{7,3},{8,12},{9,13},{10,... | collective-permute-start | bytes 3145736 | tf_op jit(solution)/shard_map/ppermute | solution.py:384
  49.5 42.8 %collective-permute-start.5 = (bf16[16,128,512]{2,1,0:T(8,128)(2,1)}, bf16[16,128,512]{2,1,0:T(8,128)(2,1)}, u32[]{:S(2)}, u32[]{:S(2)}) collective-permute-start(bf16[16,128,512]{2,1,0:T(8,128)(2,1)} %held_back.5.refs_2_), channel_id=1, source_target_pairs={{0,1},{1,0},{2,3},{3,2},{4,5},{5,4},{6,7},{7,6},{8,9},{9,8},{10,11... | collective-permute-start | bytes 6291464 | tf_op jit(solution)/shard_map/ppermute | solution.py:384
  49.6 52.8 %collective-permute-start.14 = (bf16[16,128,512]{2,1,0:T(8,128)(2,1)S(1)}, bf16[16,128,512]{2,1,0:T(8,128)(2,1)}, u32[]{:S(2)}, u32[]{:S(2)}) collective-permute-start(bf16[16,128,512]{2,1,0:T(8,128)(2,1)S(1)} %copy-done.7), channel_id=1, source_target_pairs={{0,1},{1,0},{2,3},{3,2},{4,5},{5,4},{6,7},{7,6},{8,9},{9,8},{10,11... | collective-permute-start | bytes 6291464 | tf_op jit(solution)/shard_map/ppermute | solution.py:384
  55.5 27.9 %collective-permute-start.1 = (bf16[2,2,256,512]{3,2,1,0:T(8,128)(2,1)S(1)}, bf16[2,2,256,512]{3,2,1,0:T(8,128)(2,1)S(1)}, u32[]{:S(2)}, u32[]{:S(2)}) collective-permute-start(bf16[2,2,256,512]{3,2,1,0:T(8,128)(2,1)S(1)} %lesser.4.own), channel_id=1, source_target_pairs={{4,12},{8,0},{12,20},{16,8},{20,28},{24,16},{28,36},{32,24},{36,44... | collective-permute-start | bytes 3145736 | tf_op jit(solution)/shard_map/ppermute | solution.py:393
  57.8 34.5 %collective-permute-start.2 = (bf16[2,2,256,512]{3,2,1,0:T(8,128)(2,1)}, bf16[2,2,256,512]{3,2,1,0:T(8,128)(2,1)}, u32[]{:S(2)}, u32[]{:S(2)}) collective-permute-start(bf16[2,2,256,512]{3,2,1,0:T(8,128)(2,1)} %collective-permute-done.got), channel_id=1, source_target_pairs={{0,8},{8,16},{12,4},{16,24},{20,12},{24,32},{28,20},{32,40},{36,28... | collective-permute-start | bytes 3145736 | tf_op jit(solution)/shard_map/ppermute | solution.py:393
  63.3 64.2 %collective-permute-start.12 = (bf16[2,2,256,512]{3,2,1,0:T(8,128)(2,1)S(1)}, bf16[2,2,256,512]{3,2,1,0:T(8,128)(2,1)}, u32[]{:S(2)}, u32[]{:S(2)}) collective-permute-start(bf16[2,2,256,512]{3,2,1,0:T(8,128)(2,1)S(1)} %copy-done.11), channel_id=1, source_target_pairs={{4,12},{8,0},{12,20},{16,8},{20,28},{24,16},{28,36},{32,24},{36,44... | collective-permute-start | bytes 3145736 | tf_op jit(solution)/shard_map/ppermute | solution.py:393
  84.4 43.2 %collective-permute-start.13 = (bf16[2,2,256,512]{3,2,1,0:T(8,128)(2,1)}, bf16[2,2,256,512]{3,2,1,0:T(8,128)(2,1)}, u32[]{:S(2)}, u32[]{:S(2)}) collective-permute-start(bf16[2,2,256,512]{3,2,1,0:T(8,128)(2,1)} %collective-permute-done.4.refs_1_.got), channel_id=1, source_target_pairs={{0,8},{8,16},{12,4},{16,24},{20,12},{24,32},{28,20},{32,40},{36,28... | collective-permute-start | bytes 3145736 | tf_op jit(solution)/shard_map/ppermute | solution.py:393
  100.6 37.6 %collective-permute-start.10 = (bf16[2,256,512]{2,1,0:T(8,128)(2,1)}, bf16[2,256,512]{2,1,0:T(8,128)(2,1)}, u32[]{:S(2)}, u32[]{:S(2)}) collective-permute-start(bf16[2,256,512]{2,1,0:T(8,128)(2,1)} %get-tuple-element.35), channel_id=1, source_target_pairs={{0,6},{1,7},{2,4},{3,5},{4,2},{5,3},{6,0},{7,1},{8,14},{9,15},{10,... | collective-permute-start | bytes 1572872 | tf_op jit(solution)/shard_map/ppermute | solution.py:384
  100.6 41.7 %collective-permute-start.9 = (bf16[2,256,512]{2,1,0:T(8,128)(2,1)}, bf16[2,256,512]{2,1,0:T(8,128)(2,1)}, u32[]{:S(2)}, u32[]{:S(2)}) collective-permute-start(bf16[2,256,512]{2,1,0:T(8,128)(2,1)} %get-tuple-element.35), channel_id=1, source_target_pairs={{0,4},{1,5},{2,6},{3,7},{4,0},{5,1},{6,2},{7,3},{8,12},{9,13},{10,... | collective-permute-start | bytes 1572872 | tf_op jit(solution)/shard_map/ppermute | solution.py:384
  102.4 40.0 %collective-permute-start.11 = (bf16[2,256,512]{2,1,0:T(8,128)(2,1)}, bf16[2,256,512]{2,1,0:T(8,128)(2,1)}, u32[]{:S(2)}, u32[]{:S(2)}) collective-permute-start(bf16[2,256,512]{2,1,0:T(8,128)(2,1)} %get-tuple-element.34.refs_0_.refs_16_), channel_id=1, source_target_pairs={{0,2},{1,3},{2,0},{3,1},{4,6},{5,7},{6,4},{7,5},{8,10},{9,11},{10,... | collective-permute-start | bytes 1572872 | tf_op jit(solution)/shard_map/ppermute | solution.py:384
  138.2 24.6 %collective-permute-start.21 = (bf16[2,256,512]{2,1,0:T(8,128)(2,1)}, bf16[2,256,512]{2,1,0:T(8,128)(2,1)}, u32[]{:S(2)}, u32[]{:S(2)}) collective-permute-start(bf16[2,256,512]{2,1,0:T(8,128)(2,1)} %get-tuple-element.43.refs_0_.refs_8_.refs_24_), channel_id=1, source_target_pairs={{0,2},{1,3},{2,0},{3,1},{4,6},{5,7},{6,4},{7,5},{8,10},{9,11},{10,... | collective-permute-start | bytes 1572872 | tf_op jit(solution)/shard_map/ppermute | solution.py:384
  163.5 22.7 %collective-permute-start.17 = (bf16[2,256,512]{2,1,0:T(8,128)(2,1)}, bf16[2,256,512]{2,1,0:T(8,128)(2,1)}, u32[]{:S(2)}, u32[]{:S(2)}) collective-permute-start(bf16[2,256,512]{2,1,0:T(8,128)(2,1)} %get-tuple-element.39.refs_2_.refs_18_), channel_id=1, source_target_pairs={{0,1},{1,0},{2,3},{3,2},{4,5},{5,4},{6,7},{7,6},{8,9},{9,8},{10,11... | collective-permute-start | bytes 1572872 | tf_op jit(solution)/shard_map/ppermute | solution.py:384
  165.0 43.0 %collective-permute-start.7 = (bf16[2,256,512]{2,1,0:T(8,128)(2,1)}, bf16[2,256,512]{2,1,0:T(8,128)(2,1)S(1)}, u32[]{:S(2)}, u32[]{:S(2)}) collective-permute-start(bf16[2,256,512]{2,1,0:T(8,128)(2,1)} %copy-done.46), channel_id=1, source_target_pairs={{0,6},{1,7},{2,4},{3,5},{4,2},{5,3},{6,0},{7,1},{8,14},{9,15},{10,... | collective-permute-start | bytes 1572872 | tf_op jit(solution)/shard_map/ppermute | solution.py:384
  167.3 40.7 %collective-permute-start.6 = (bf16[2,256,512]{2,1,0:T(8,128)(2,1)}, bf16[2,256,512]{2,1,0:T(8,128)(2,1)}, u32[]{:S(2)}, u32[]{:S(2)}) collective-permute-start(bf16[2,256,512]{2,1,0:T(8,128)(2,1)} %copy-done.46), channel_id=1, source_target_pairs={{0,4},{1,5},{2,6},{3,7},{4,0},{5,1},{6,2},{7,3},{8,12},{9,13},{10,... | collective-permute-start | bytes 1572872 | tf_op jit(solution)/shard_map/ppermute | solution.py:384
  168.8 39.2 %collective-permute-start.8 = (bf16[2,256,512]{2,1,0:T(8,128)(2,1)}, bf16[2,256,512]{2,1,0:T(8,128)(2,1)}, u32[]{:S(2)}, u32[]{:S(2)}) collective-permute-start(bf16[2,256,512]{2,1,0:T(8,128)(2,1)} %get-tuple-element.32.refs_0_.refs_16_), channel_id=1, source_target_pairs={{0,2},{1,3},{2,0},{3,1},{4,6},{5,7},{6,4},{7,5},{8,10},{9,11},{10,... | collective-permute-start | bytes 1572872 | tf_op jit(solution)/shard_map/ppermute | solution.py:384
  186.1 25.1 %collective-permute-start.26 = (bf16[2,256,512]{2,1,0:T(8,128)(2,1)}, bf16[2,256,512]{2,1,0:T(8,128)(2,1)}, u32[]{:S(2)}, u32[]{:S(2)}) collective-permute-start(bf16[2,256,512]{2,1,0:T(8,128)(2,1)} %get-tuple-element.32.refs_0_.refs_16_), channel_id=1, source_target_pairs={{0,1},{1,0},{2,3},{3,2},{4,5},{5,4},{6,7},{7,6},{8,9},{9,8},{10,11... | collective-permute-start | bytes 1572872 | tf_op jit(solution)/shard_map/ppermute | solution.py:384
  209.3 35.1 %collective-permute-start.31 = (bf16[2,256,512]{2,1,0:T(8,128)(2,1)}, bf16[2,256,512]{2,1,0:T(8,128)(2,1)}, u32[]{:S(2)}, u32[]{:S(2)}) collective-permute-start(bf16[2,256,512]{2,1,0:T(8,128)(2,1)} %copy-done.45), channel_id=1, source_target_pairs={{0,6},{1,7},{2,4},{3,5},{4,2},{5,3},{6,0},{7,1},{8,14},{9,15},{10,... | collective-permute-start | bytes 1572872 | tf_op jit(solution)/shard_map/ppermute | solution.py:384
  210.8 24.5 %collective-permute-start.28 = (bf16[2,256,512]{2,1,0:T(8,128)(2,1)}, bf16[2,256,512]{2,1,0:T(8,128)(2,1)}, u32[]{:S(2)}, u32[]{:S(2)}) collective-permute-start(bf16[2,256,512]{2,1,0:T(8,128)(2,1)} %get-tuple-element.52.refs_2_.refs_18_), channel_id=1, source_target_pairs={{0,1},{1,0},{2,3},{3,2},{4,5},{5,4},{6,7},{7,6},{8,9},{9,8},{10,11... | collective-permute-start | bytes 1572872 | tf_op jit(solution)/shard_map/ppermute | solution.py:384
  210.8 24.6 %collective-permute-start.29 = (bf16[2,256,512]{2,1,0:T(8,128)(2,1)}, bf16[2,256,512]{2,1,0:T(8,128)(2,1)}, u32[]{:S(2)}, u32[]{:S(2)}) collective-permute-start(bf16[2,256,512]{2,1,0:T(8,128)(2,1)} %get-tuple-element.53.refs_3_.refs_19_), channel_id=1, source_target_pairs={{0,1},{1,0},{2,3},{3,2},{4,5},{5,4},{6,7},{7,6},{8,9},{9,8},{10,11... | collective-permute-start | bytes 1572872 | tf_op jit(solution)/shard_map/ppermute | solution.py:384
  211.3 33.0 %collective-permute-start.30 = (bf16[2,256,512]{2,1,0:T(8,128)(2,1)}, bf16[2,256,512]{2,1,0:T(8,128)(2,1)}, u32[]{:S(2)}, u32[]{:S(2)}) collective-permute-start(bf16[2,256,512]{2,1,0:T(8,128)(2,1)} %copy-done.45), channel_id=1, source_target_pairs={{0,4},{1,5},{2,6},{3,7},{4,0},{5,1},{6,2},{7,3},{8,12},{9,13},{10,... | collective-permute-start | bytes 1572872 | tf_op jit(solution)/shard_map/ppermute | solution.py:384
  212.1 32.2 %collective-permute-start.32 = (bf16[2,256,512]{2,1,0:T(8,128)(2,1)S(1)}, bf16[2,256,512]{2,1,0:T(8,128)(2,1)}, u32[]{:S(2)}, u32[]{:S(2)}) collective-permute-start(bf16[2,256,512]{2,1,0:T(8,128)(2,1)S(1)} %copy-done.9), channel_id=1, source_target_pairs={{0,2},{1,3},{2,0},{3,1},{4,6},{5,7},{6,4},{7,5},{8,10},{9,11},{10,... | collective-permute-start | bytes 1572872 | tf_op jit(solution)/shard_map/ppermute | solution.py:384
  272.9 67.3 %all-to-all-start = ((bf16[4,2,32,16,512]{4,3,1,0,2:T(8,128)(2,1)}), bf16[4,2,32,16,512]{4,3,1,0,2:T(8,128)(2,1)}, u32[]{:S(2)}, u32[]{:S(2)}) async-start(bf16[4,2,32,16,512]{4,3,1,0,2:T(8,128)(2,1)} %copy.26), calls=%async_computation | async-start | bytes 8388608 | tf_op jit(solution)/shard_map/all_to_all | solution.py:472
  (69 other events, 555.1 us)

commit v4 on v2

--- a/solution.py
+++ b/solution.py
@@ -25,44 +25,63 @@
     return (block.astype(jnp.float32) * gamma).astype(jnp.bfloat16)
 
 
-def lesser_kernel(chunk, half, green, gamma, out):
-    rows = out.shape[2]
-    span = slice(chunk * rows, (chunk + 1) * rows)
+def lesser_kernel(place, green, gamma, *outs):
+    norb = green.shape[-1]
+    rows = norb // CHUNKS
     gam = gamma[0, 0]
-    wide_re = green[0, 0, 0].astype(jnp.float32)
-    wide_im = green[0, 0, 1].astype(jnp.float32)
+    g_re, g_im = green[0, 0, 0], green[0, 0, 1]
+    wide_re = g_re.astype(jnp.float32)
+    wide_im = g_im.astype(jnp.float32)
     less = (wide_re - wide_im).astype(jnp.bfloat16)
     more = (wide_re + wide_im).astype(jnp.bfloat16)
-    total = dot_nt(scale(green[0, 0, 0, span], gam), less) + dot_nt(
-        scale(green[0, 0, 1, span], gam), more
-    )
-    out[0, 0] = total.astype(jnp.bfloat16)
-
-
-def packed_lesser(half, green, gamma, chunk):
+    total = dot_nt(scale(g_re, gam), less) + dot_nt(scale(g_im, gam), more)
+    total = total.astype(jnp.bfloat16)
+    for side in range(2):
+
+        @pl.when(pl.program_id(0) // 2 == side)
+        def _():
+            for c in range(CHUNKS):
+                outs[side * CHUNKS + c][0, 0] = total[c * rows : (c + 1) * rows]
+
+
+def packed_lesser(place, green, gamma):
     energies, norb = green.shape[1], green.shape[-1]
-    count = green.shape[0] // 2
+    half = green.shape[0] // 2
     rows = norb // CHUNKS
-    return pl.pallas_call(
-        functools.partial(lesser_kernel, chunk),
+
+    def which(k, p):
+        return ((p[0] + 1 + k // half) % 2) * half + k % half
+
+    def block_of(side):
+        def index(k, e, p):
+            if side == 0:
+                return (jnp.minimum(k, half - 1), jnp.where(k < half, e, energies - 1), 0, 0)
+            return (jnp.maximum(k - half, 0), jnp.where(k < half, 0, e), 0, 0)
+
+        return pl.BlockSpec((1, 1, rows, norb), index)
+
+    out = jax.ShapeDtypeStruct((half, energies, rows, norb), jnp.bfloat16)
+    outs = pl.pallas_call(
+        lesser_kernel,
         grid_spec=pltpu.PrefetchScalarGridSpec(
             num_scalar_prefetch=1,
-            grid=(count, energies),
+            grid=(2 * half, energies),
             in_specs=[
-                pl.BlockSpec((1, 1, 2, norb, norb), lambda k, e, h: (h[0] * count + k, e, 0, 0, 0)),
-                pl.BlockSpec((1, 1, 1, norb), lambda k, e, h: (h[0] * count + k, e, 0, 0)),
+                pl.BlockSpec((1, 1, 2, norb, norb), lambda k, e, p: (which(k, p), e, 0, 0, 0)),
+                pl.BlockSpec((1, 1, 1, norb), lambda k, e, p: (which(k, p), e, 0, 0)),
             ],
-            out_specs=pl.BlockSpec((1, 1, rows, norb), lambda k, e, h: (k, e, 0, 0)),
-        ),
-        out_shape=jax.ShapeDtypeStruct((count, energies, rows, norb), jnp.bfloat16),
-        compiler_params=pltpu.CompilerParams(vmem_limit_bytes=32 * MIB),
+            out_specs=[block_of(0)] * CHUNKS + [block_of(1)] * CHUNKS,
+        ),
+        out_shape=[out] * (2 * CHUNKS),
+        compiler_params=pltpu.CompilerParams(vmem_limit_bytes=60 * MIB),
         cost_estimate=pl.CostEstimate(
-            flops=4 * count * energies * rows * norb**2,
-            bytes_accessed=6 * count * energies * norb**2,
+            flops=8 * half * energies * norb**3,
+            bytes_accessed=12 * half * energies * norb**2,
             transcendentals=0,
         ),
         name="lesser",
-    )(half, green, gamma)
+    )(place, green, gamma)
+    return outs[:CHUNKS], outs[CHUNKS:]
 
 
 def shift_kernel(place, weights, own, got, own_halo, got_halo, early, out_own, out_other):
@@ -116,6 +135,18 @@
         ),
         name="shifted",
     )(place, weights, own, got, own_halo, got_halo, early)
+
+
+def held_back(arrays, waited):
+    return pl.pallas_call(
+        lambda *refs: None,
+        in_specs=[pl.BlockSpec(memory_space=pltpu.HBM)] * (len(arrays) + len(waited)),
+        out_specs=[pl.BlockSpec(memory_space=pltpu.HBM)] * len(arrays),
+        out_shape=[jax.ShapeDtypeStruct(x.shape, x.dtype) for x in arrays],
+        input_output_aliases={i: i for i in range(len(arrays))},
+        compiler_params=pltpu.CompilerParams(vmem_limit_bytes=60 * MIB),
+        name="held_back",
+    )(*arrays, *waited)
 
 
 def identity(n):
@@ -156,7 +187,7 @@
             ],
         ),
         out_shape=[whole, whole],
-        compiler_params=pltpu.CompilerParams(vmem_limit_bytes=48 * MIB),
+        compiler_params=pltpu.CompilerParams(vmem_limit_bytes=60 * MIB),
         cost_estimate=pl.CostEstimate(
             flops=4 * points * norb**3 // 2, bytes_accessed=14 * points * norb**2, transcendentals=0
         ),
@@ -164,22 +195,25 @@
     )(tiles, *parts)
 
 
-def add_products(targets, picks, sources, factor, at, store):
-    acc = [[None, None] for _ in range(targets)]
+def add_products(targets, streams, picks, donor, factor, at, store):
+    acc = [[None] * streams for _ in range(targets)]
+    kept = {}
     for quad in range(4):
-        donors = [(s, kk) for s in (2 * quad, 2 * quad + 1) for kk in range(2)]
-        held = [[sources[s][kk, e, at[0], at[1]] for e in range(2)] for s, kk in donors]
+        held = [[donor(4 * quad + d, n, at) for n in range(streams)] for d in range(4)]
         for t in range(targets):
             c = [factor[picks(t, 4 * quad + d), at[0], at[1]] for d in range(4)]
-            for e in range(2):
-                part = (c[0] * held[0][e] + c[1] * held[1][e]) + (
-                    c[2] * held[2][e] + c[3] * held[3][e]
+            for n in range(streams):
+                part = (c[0] * held[0][n] + c[1] * held[1][n]) + (
+                    c[2] * held[2][n] + c[3] * held[3][n]
                 )
-                part = part.astype(jnp.float32)
-                acc[t][e] = part if acc[t][e] is None else acc[t][e] + part
+                if quad % 2 == 0:
+                    kept[t, n] = part
+                    continue
+                part = (kept.pop((t, n)) + part).astype(jnp.float32)
+                acc[t][n] = part if acc[t][n] is None else acc[t][n] + part
     for t in range(targets):
-        for e in range(2):
-            store[t, e, at[0], at[1]] = acc[t][e].astype(store.dtype)
+        for n in range(streams):
+            store(t, n, at, acc[t][n])
 
 
 def home_kernel(table, *refs):
@@ -188,14 +222,23 @@
 
     def picks(t, d):
         return table[t * 16 + d]
+
+    def donor(d, n, at):
+        return sources[d // 2][d % 2, n, at[0], at[1]]
+
+    def into(ref):
+        def store(t, n, at, value):
+            ref[t, n, at[0], at[1]] = value.astype(jnp.bfloat16)
+
+        return store
 
     def slab(i, carry):
         at = (
             pl.ds(pl.multiple_of(i // 2 * 16, 16), 16),
             pl.ds(pl.multiple_of(i % 2 * (norb // 2), norb // 2), norb // 2),
         )
-        add_products(targets, picks, sources, coup, at, out)
-        add_products(targets, picks, sources, coup_t, at, out_t)
+        add_products(targets, 2, picks, donor, coup, at, into(out))
+        add_products(targets, 2, picks, donor, coup_t, at, into(out_t))
         return carry
 
     lax.fori_loop(0, height // 16 * 2, slab, 0)
@@ -204,7 +247,7 @@
 def home_sums(table, sources, coup, coup_t, chunk, targets):
     _, _, rows, norb = sources[0].shape
     points = coup.shape[0]
-    height = 128
+    height = 64
     steps = rows // height
     given = pl.BlockSpec((2, 2, height, norb), lambda i, q: (0, 0, i, 0))
     factor = pl.BlockSpec((points, height, norb), lambda i, q: (0, chunk * steps + i, 0))
@@ -219,10 +262,10 @@
             out_specs=[result] * 2,
         ),
         out_shape=[out, out],
-        compiler_params=pltpu.CompilerParams(vmem_limit_bytes=48 * MIB),
+        compiler_params=pltpu.CompilerParams(vmem_limit_bytes=60 * MIB),
         cost_estimate=pl.CostEstimate(
-            flops=40 * targets * points * rows * norb,
-            bytes_accessed=10 * MIB * steps,
+            flops=20 * targets * points * rows * norb,
+            bytes_accessed=12 * MIB,
             transcendentals=0,
         ),
         name="home",
@@ -231,91 +274,78 @@
 
 def rows_kernel(tile, table, *refs):
     rows_of, cols_of = refs[:16], refs[16:32]
-    coup, coup_t, out, picked, along, across = refs[32:]
+    coup, out, source = refs[32], refs[-2], refs[-1]
     targets, _, _, height, norb = out.shape
-    group = pl.program_id(0) * targets
+    group = pl.program_id(1) * targets
     part = norb // CHUNKS
 
     for c in range(CHUNKS):
 
-        @pl.when((pl.program_id(0) == 0) & (tile[0] // CHUNKS == c))
+        @pl.when((pl.program_id(1) == 0) & (tile[0] // CHUNKS == c))
         def _(held=rows_of[8 * c : 8 * c + 8]):
-            for s in range(8):
-                picked[s] = held[s][...]
+            turn = identity(height)
+
+            for d in range(16):
+                for b in range(CHUNKS):
+                    span = slice(b * part, (b + 1) * part)
+                    straight = held[d // 2][d % 2, 0, :, span].astype(jnp.float32)
+                    turned = turn_over(turn, cols_of[8 * b + d // 2][d % 2, 0])
+                    source[d, 0, :, span] = (straight + turned).astype(jnp.bfloat16)
+                    source[d, 1, :, span] = (straight - turned).astype(jnp.bfloat16)
 
     def picks(t, d):
         return table[(group + t) * 16 + d]
 
-    def over_rows(i, carry):
+    def donor(d, n, at):
+        return source[d, n, at[0], at[1]]
+
+    def store(t, n, at, value):
+        out[t, 0, n, at[0], at[1]] = value.astype(jnp.bfloat16)
+
+    def slab(i, carry):
         at = (
             pl.ds(pl.multiple_of(i // 2 * 16, 16), 16),
             pl.ds(pl.multiple_of(i % 2 * (norb // 2), norb // 2), norb // 2),
         )
-        add_products(targets, picks, [picked.at[s] for s in range(8)], coup, at, along)
+        add_products(targets, 2, picks, donor, coup, at, store)
         return carry
 
-    lax.fori_loop(0, height // 16 * 2, over_rows, 0)
-    for c in range(CHUNKS):
-
-        def over_cols(i, carry, c=c):
-            at = (pl.ds(pl.multiple_of(i * 32, 32), 32), slice(None))
-            add_products(
-                targets,
-                picks,
-                cols_of[8 * c : 8 * c + 8],
-                coup_t.at[:, c * part : (c + 1) * part],
-                at,
-                across.at[:, :, c * part : (c + 1) * part],
-            )
-            return carry
-
-        lax.fori_loop(0, part // 32, over_cols, 0)
-
-    turn = identity(height)
-    for t in range(targets):
-        for e in range(2):
-            u = along[t, e]
-            v = dot_nt(turn, across[t, e])
-            out[t, e, 0] = (u + v).astype(jnp.bfloat16)
-            out[t, e, 1] = (u - v).astype(jnp.bfloat16)
-
-
-def row_sums(tile, table, chunks, coup, coup_t, targets):
-    _, _, part, norb = chunks[0][0].shape
-    points = coup.shape[0]
-    height = 128
+    lax.fori_loop(0, height // 16 * 2, slab, 0)
+
+
+def turn_over(turn, block):
+    return dot_nt(turn, block)
+
+
+def row_sums(tile, table, chunks, coupling, targets):
+    _, energies, part, norb = chunks[0][0].shape
+    points, height, _ = coupling.shape
     steps = part // height
-    groups = points // targets
-    row_block = pl.BlockSpec((2, 2, height, norb), lambda g, t, q: (0, 0, t[0] % steps, 0))
-    col_block = pl.BlockSpec((2, 2, part, height), lambda g, t, q: (0, 0, 0, t[0]))
+    row_block = pl.BlockSpec((2, 1, height, norb), lambda e, g, t, q: (0, e, t[0] % steps, 0))
+    col_block = pl.BlockSpec((2, 1, part, height), lambda e, g, t, q: (0, e, 0, t[0]))
     sources = [x for chunk in chunks for x in chunk]
     return pl.pallas_call(
         rows_kernel,
         grid_spec=pltpu.PrefetchScalarGridSpec(
             num_scalar_prefetch=2,
-            grid=(groups,),
+            grid=(energies, points // targets),
             in_specs=[row_block] * 16
             + [col_block] * 16
-            + [
-                pl.BlockSpec((points, height, norb), lambda g, t, q: (0, t[0], 0)),
-                pl.BlockSpec((points, norb, height), lambda g, t, q: (0, 0, t[0])),
-            ],
-            out_specs=pl.BlockSpec((targets, 2, 2, height, norb), lambda g, t, q: (g, 0, 0, 0, 0)),
-            scratch_shapes=[
-                pltpu.VMEM((8, 2, 2, height, norb), jnp.bfloat16),
-                pltpu.VMEM((targets, 2, height, norb), jnp.float32),
-                pltpu.VMEM((targets, 2, norb, height), jnp.bfloat16),
-            ],
-        ),
-        out_shape=jax.ShapeDtypeStruct((points, 2, 2, height, norb), jnp.bfloat16),
-        compiler_params=pltpu.CompilerParams(vmem_limit_bytes=56 * MIB),
+            + [pl.BlockSpec((points, height, norb), lambda e, g, t, q: (0, 0, 0))],
+            out_specs=pl.BlockSpec(
+                (targets, 1, 2, height, norb), lambda e, g, t, q: (g, e, 0, 0, 0)
+            ),
+            scratch_shapes=[pltpu.VMEM((16, 2, height, norb), jnp.bfloat16)],
+        ),
+        out_shape=jax.ShapeDtypeStruct((points, energies, 2, height, norb), jnp.bfloat16),
+        compiler_params=pltpu.CompilerParams(vmem_limit_bytes=60 * MIB),
         cost_estimate=pl.CostEstimate(
             flops=40 * points * points * height * norb,
             bytes_accessed=24 * MIB,
             transcendentals=0,
         ),
         name="rows",
-    )(tile, table, *sources, *sources, coup, coup_t)
+    )(tile, table, *sources, *sources, coupling)
 
 
 def density_kernel(inverse, green, gamma, *refs):
@@ -355,7 +385,7 @@
         + [part] * (2 * CHUNKS),
         out_specs=pl.BlockSpec((1, 2, norb, norb), lambda k: (k, 0, 0, 0)),
         out_shape=jax.ShapeDtypeStruct((count, 2, norb, norb), jnp.bfloat16),
-        compiler_params=pltpu.CompilerParams(vmem_limit_bytes=48 * MIB),
+        compiler_params=pltpu.CompilerParams(vmem_limit_bytes=60 * MIB),
         cost_estimate=pl.CostEstimate(
             flops=16 * count * energies * norb**3,
             bytes_accessed=(8 * energies + 4) * count * norb**2,
@@ -404,27 +434,29 @@
 
     coup_b = flip(coupling, 1, 2)
     coup_c = flip(coupling, 0, 1)
-    coup_bc = flip(coup_b, 0, 1)
-    early = (coup_b, coup_bc)
-
-    sent = [packed_lesser(1 - place, green, gamma, c) for c in range(CHUNKS)]
+
+    sent, own = packed_lesser(place, green, gamma)
     got = [flip(x, 1, 0) for x in sent]
-    own = [packed_lesser(place, green, gamma, c) for c in range(CHUNKS)]
     own_halo = [along_pairs(x, -1) for x in own]
     got_halo = [along_pairs(x, 1) for x in got]
-
+    (coup_o,) = held_back([coup_b], [got[1], got_halo[0]])
+    coup_bc = flip(coup_o, 0, 1)
+
+    tile = mom.astype(jnp.int32)
+    coup, coup_t = folded(
+        jnp.arange(4, dtype=jnp.int32) ^ tile, [coupling, coup_c, coup_o, coup_bc]
+    )
+    early = (coup_b, coup_t)
     moves = [(0, 0), (1, 0), (1, 2), (0, 2)]
     moves = moves + [(lo, mo ^ 1) for lo, mo in moves]
-    chunks = []
+    near = []
     for c in range(CHUNKS):
         mine, other = shifted(place, weights, own[c], got[c], own_halo[c], got_halo[c], early[c])
-        near = [mine, flip(other, 1, 0), flip(other, 1, 2), flip(mine, 0, 2)]
-        chunks.append(near + [flip(x, 0, 1) for x in near])
-
-    tile = mom.astype(jnp.int32)
-    coup, coup_t = folded(
-        jnp.arange(4, dtype=jnp.int32) ^ tile, [coupling, coup_c, coup_b, coup_bc]
-    )
+        near.append([mine, flip(other, 1, 0), flip(other, 1, 2), flip(mine, 0, 2)])
+
+    def with_other_core(block, waited):
+        block = block[:1] + list(held_back(block[1:], waited))
+        return block + [flip(x, 0, 1) for x in block]
 
     donors = jnp.stack(
         [(mom ^ mo) * local_k + (x_lo ^ lo) * half + kk for lo, mo in moves for kk in range(half)]
@@ -439,7 +471,11 @@
     ).astype(jnp.int32)
     table_home = lax.dynamic_slice_in_dim(table, mom * local_k, local_k, 0).reshape(-1)
 
-    sums = [home_sums(table_home, chunks[c], coup, coup_t, c, local_k) for c in range(CHUNKS)]
+    sums, chunks, waited = [], [], mine
+    for c in range(CHUNKS):
+        chunks.append(with_other_core(near[c], [waited]))
+        sums.append(home_sums(table_home, chunks[c], coup, coup_t, c, local_k))
+        waited = sums[c][0]
     us, vs = [s[0] for s in sums], [s[1] for s in sums]
     inverse = 1.0 / (green.shape[1] * n_energy)
     received = []
@@ -447,7 +483,7 @@
         part = partial_density(green, gamma, us, vs, inverse, first, half)
         part = part.reshape(half, 2, n_energy, norb // n_energy, norb)
         received.append(lax.all_to_all(part, "energy", split_axis=2, concat_axis=2, tiled=True))
-    self_energy = row_sums(tile[None], table.reshape(-1), chunks, coup, coup_t, local_k)
+    self_energy = row_sums(tile[None], table.reshape(-1), chunks, coupling, local_k)
     summed = jnp.concatenate(
         [jnp.sum(x.astype(jnp.float32), axis=2) for x in received], axis=0
     )

time: 320 us -> 297 us (0.928)
  waiting for transfers between devices: 132 us -> 103 us
  local copies, waits for them, and re-layouts: 17.4 us -> 23.2 us
    ppermute x19, waiting for transfers between devices: 97.9 us -> 73.8 us  [flip(): return lax.ppermute(x, BOTH, perm)]
    pallas_call x1, Pallas kernels: 36.3 us -> 28.5 us  [row_sums(): pl.pallas_call(rows_kernel, grid_spec=pltpu.PrefetchScalarGridSpec(num_sc...]
    reshape x2, local copies, waits for them, and re-layouts: 3.13 us -> 6.35 us  [on_device(): part = part.reshape(half, 2, n_energy, norb // n_energy, norb)]
    unnamed x41 -> x39, local copies, waits for them, and re-layouts: 12.7 us -> 14.2 us
  transfers between devices with their start and end apart: 25 -> 25, of which waited for: 10 -> 11; matrix products, arithmetic and copies ran while one was open for 2% -> 3% of each run, Pallas kernels for 31% -> 33%
where the time goes in v4:
time: 297 us; the launch traced here: 295 us
  Pallas kernels  122 us (41%)
  waiting for transfers between devices  103 us (35%)
  starting transfers between devices  40.4 us (14%)
  local copies, waits for them, and re-layouts  23.2 us (8%)
  other arithmetic  3.77 us (1%)
  between operations  3.29 us (1%)
    ppermute x19, waiting for transfers between devices, flip(): return lax.ppermute(x, BOTH, perm)  73.8 us
    pallas_call x1, Pallas kernels, row_sums(): pl.pallas_call(rows_kernel, grid_spec=pltpu.PrefetchScalarGridSpec(num_sc...  28.5 us
    pallas_call x2, Pallas kernels, partial_density(): pl.pallas_call(functools.partial(density_kernel, inverse), grid=(count,),...  24.9 us
    pallas_call x2, Pallas kernels, home_sums(): pl.pallas_call(home_kernel, grid_spec=pltpu.PrefetchScalarGridSpec(num_sc...  24.7 us
    pallas_call x1, Pallas kernels, folded(): pl.pallas_call(fold_kernel, grid_spec=pltpu.PrefetchScalarGridSpec(num_sc...  24 us
    all_to_all x2, starting transfers between devices, on_device(): lax.all_to_all(part, 'energy', split_axis=2, concat_axis=2, tiled=True)  15.1 us
    ppermute x4, waiting for transfers between devices, along_pairs(): return lax.ppermute(x, 'energy', moves)  14.9 us
    unnamed x39, local copies, waits for them, and re-layouts  14.2 us
  transfers between devices with their start and end apart: 25, of which 11 were waited for; matrix products, arithmetic and copies ran while one was open for 3% of the time, Pallas kernels for 33%

profile of v4, /device:TPU:0, one launch (start us, length us, event | category | flops | bytes accessed | tf_op | source)
XLA Modules:
  0.0 295.4 jit_solution(6834395769800480503)
XLA Ops:
  4.9 10.8 %lesser.1 = (bf16[2,2,256,512]{3,2,1,0:T(8,128)(2,1)}, bf16[2,2,256,512]{3,2,1,0:T(8,128)(2,1)}, bf16[2,2,256,512]{3,2,1,0:T(8,128)(2,1)}, bf16[2,2,256,512]{3,2,1,0:T(8,128)(2,1)}) custom-call(s32[1]{0:T(128)} %bitcast.17.place, bf16[4,2,2,512,512]{4,3,2,1,0:T(8,128)(2,1)} %green.5, f32[4,2,1,512]{3,2,1,0:T(1,128)} %broadcast_in_dim.36.gamma), custom_call_target="tpu_custom_call" | custom-call | flops 4294967296 | bytes 12582912 | tf_op jit(solution)/shard_map/lesser/pallas_call | solution.py:64
  17.2 23.4 %collective-permute-done.got = bf16[2,2,256,512]{3,2,1,0:T(8,128)(2,1)} collective-permute-done((bf16[2,2,256,512]{3,2,1,0:T(8,128)(2,1)}, bf16[2,2,256,512]{3,2,1,0:T(8,128)(2,1)}, u32[]{:S(2)}, u32[]{:S(2)}) %collective-permute-start) | collective-permute-done | bytes 1048608 | tf_op jit(solution)/shard_map/ppermute | solution.py:414
  40.6 4.5 %collective-permute-start.2 = (bf16[2,2,256,512]{3,2,1,0:T(8,128)(2,1)}, bf16[2,2,256,512]{3,2,1,0:T(8,128)(2,1)}, u32[]{:S(2)}, u32[]{:S(2)}) collective-permute-start(bf16[2,2,256,512]{3,2,1,0:T(8,128)(2,1)} %collective-permute-done.got), channel_id=1, source_target_pairs={{0,8},{8,16},{12,4},{16,24},{20,12},{24,32},{28,20},{32,40},{36,28... | collective-permute-start | bytes 3145736 | tf_op jit(solution)/shard_map/ppermute | solution.py:423
  50.7 14.9 %collective-permute-done.2.got_halo.refs_2_ = bf16[2,2,256,512]{3,2,1,0:T(8,128)(2,1)} collective-permute-done((bf16[2,2,256,512]{3,2,1,0:T(8,128)(2,1)}, bf16[2,2,256,512]{3,2,1,0:T(8,128)(2,1)}, u32[]{:S(2)}, u32[]{:S(2)}) %collective-permute-start.2) | collective-permute-done | bytes 1048608 | tf_op jit(solution)/shard_map/ppermute | solution.py:423
  68.4 5.1 %shifted.2 = (bf16[2,2,256,512]{3,2,1,0:T(8,128)(2,1)S(1)}, bf16[2,2,256,512]{3,2,1,0:T(8,128)(2,1)}) custom-call(s32[1]{0:T(128)} %bitcast.17.place, f32[4]{0:T(128)S(1)} %pad_maximum_fusion.weights, bf16[2,2,256,512]{3,2,1,0:T(8,128)(2,1)S(1)} %copy-done.8, bf16[2,2,256,512]{3,2,1,0:T(8,128)(2,1)} %collective-permute-done.got, ...), custom_call_target="tpu_custom_call" | custom-call | flops 8388608 | bytes 6291456 | tf_op jit(solution)/shard_map/shifted/pallas_call | solution.py:121
  75.9 6.0 %collective-permute-start.9 = (bf16[2,2,256,512]{3,2,1,0:T(8,128)(2,1)}, bf16[2,2,256,512]{3,2,1,0:T(8,128)(2,1)}, u32[]{:S(2)}, u32[]{:S(2)}) collective-permute-start(bf16[2,2,256,512]{3,2,1,0:T(8,128)(2,1)} %copy-done.6), channel_id=1, source_target_pairs={{0,8},{8,16},{12,4},{16,24},{20,12},{24,32},{28,20},{32,40},{36,28... | collective-permute-start | bytes 3145736 | tf_op jit(solution)/shard_map/ppermute | solution.py:423
  83.9 3.9 %collective-permute-start.6 = (bf16[2,2,256,512]{3,2,1,0:T(8,128)(2,1)S(1)}, bf16[2,2,256,512]{3,2,1,0:T(8,128)(2,1)}, u32[]{:S(2)}, u32[]{:S(2)}) collective-permute-start(bf16[2,2,256,512]{3,2,1,0:T(8,128)(2,1)S(1)} %get-tuple-element.24.refs_0_.refs_16_), channel_id=1, source_target_pairs={{0,2},{1,3},{2,0},{3,1},{4,6},{5,7},{6,4},{7,5},{8,10},{9,11},{10,... | collective-permute-start | bytes 3145736 | tf_op jit(solution)/shard_map/ppermute | solution.py:414
  88.5 24.0 %fold.1 = (bf16[16,512,512]{2,1,0:T(8,128)(2,1)}, bf16[16,512,512]{2,1,0:T(8,128)(2,1)}) custom-call(s32[4]{0:T(128)} %iota_xor_fusion.tiles, bf16[16,128,512]{2,1,0:T(8,128)(2,1)} %refs_32_.1, bf16[16,128,512]{2,1,0:T(8,128)(2,1)} %collective-permute-done.10.refs_1_, bf16[16,128,512]{2,1,0:T(8,128)(2,1)} %held_back.3.refs_2_, bf16[16,128,512]{2,1,0:T(8,128)(2,1)} %copy-done.18), custom_call_target="tpu_custom_call" | custom-call | flops 4294967296 | bytes 58720256 | tf_op jit(solution)/shard_map/fold/pallas_call | solution.py:178
  112.6 3.4 %copy-done = bf16[16,512,512]{2,1,0:T(8,128)(2,1)S(1)} copy-done((bf16[16,512,512]{2,1,0:T(8,128)(2,1)S(1)}, bf16[16,512,512]{2,1,0:T(8,128)(2,1)}, u32[]{:S(2)}) %copy-start) | copy-done | bytes 8388632
  116.0 4.1 %shifted.3 = (bf16[2,2,256,512]{3,2,1,0:T(8,128)(2,1)S(1)}, bf16[2,2,256,512]{3,2,1,0:T(8,128)(2,1)S(1)}) custom-call(s32[1]{0:T(128)} %bitcast.17.place, f32[4]{0:T(128)S(1)} %pad_maximum_fusion.weights, bf16[2,2,256,512]{3,2,1,0:T(8,128)(2,1)} %get-tuple-element.26.own, bf16[2,2,256,512]{3,2,1,0:T(8,128)(2,1)S(1)} %copy-done.7, ...), custom_call_target="tpu_custom_call" | custom-call | flops 8388608 | bytes 6291456 | tf_op jit(solution)/shard_map/shifted/pallas_call | solution.py:121
  122.1 10.3 %collective-permute-done.6.refs_2_ = bf16[2,2,256,512]{3,2,1,0:T(8,128)(2,1)} collective-permute-done((bf16[2,2,256,512]{3,2,1,0:T(8,128)(2,1)S(1)}, bf16[2,2,256,512]{3,2,1,0:T(8,128)(2,1)}, u32[]{:S(2)}, u32[]{:S(2)}) %collective-permute-start.6) | collective-permute-done | bytes 1048608 | tf_op jit(solution)/shard_map/ppermute | solution.py:414
  139.2 12.4 %home.2 = (bf16[4,2,256,512]{3,2,1,0:T(8,128)(2,1)}, bf16[4,2,256,512]{3,2,1,0:T(8,128)(2,1)}) custom-call(s32[64]{0:T(128)} %reshape.19.table, bf16[2,2,256,512]{3,2,1,0:T(8,128)(2,1)} %copy-done.3, bf16[2,2,256,512]{3,2,1,0:T(8,128)(2,1)} %get-tuple-element.30.refs_1_.refs_17_, bf16[2,2,256,512]{3,2,1,0:T(8,128)(2,1)} %get-tuple-element.31.refs_2_.refs_18_, ...), custom_call_target="tpu_custom_call" | custom-call | flops 167772160 | bytes 12582912 | tf_op jit(solution)/shard_map/home/pallas_call | solution.py:256
  151.5 8.5 %collective-permute-done.17.refs_1_ = bf16[2,2,256,512]{3,2,1,0:T(8,128)(2,1)} collective-permute-done((bf16[2,2,256,512]{3,2,1,0:T(8,128)(2,1)S(1)}, bf16[2,2,256,512]{3,2,1,0:T(8,128)(2,1)}, u32[]{:S(2)}, u32[]{:S(2)}) %collective-permute-start.17) | collective-permute-done | bytes 1048608 | tf_op jit(solution)/shard_map/ppermute | solution.py:414
  160.1 23.4 %collective-permute-done.18.refs_2_ = bf16[2,2,256,512]{3,2,1,0:T(8,128)(2,1)} collective-permute-done((bf16[2,2,256,512]{3,2,1,0:T(8,128)(2,1)S(1)}, bf16[2,2,256,512]{3,2,1,0:T(8,128)(2,1)}, u32[]{:S(2)}, u32[]{:S(2)}) %collective-permute-start.18) | collective-permute-done | bytes 1048608 | tf_op jit(solution)/shard_map/ppermute | solution.py:414
  186.4 3.0 %collective-permute-done.21.refs_14_.refs_30_.refs_6_ = bf16[2,2,256,512]{3,2,1,0:T(8,128)(2,1)S(1)} collective-permute-done((bf16[2,2,256,512]{3,2,1,0:T(8,128)(2,1)}, bf16[2,2,256,512]{3,2,1,0:T(8,128)(2,1)S(1)}, u32[]{:S(2)}, u32[]{:S(2)}) %collective-permute-start.21) | collective-permute-done | bytes 1048608 | tf_op jit(solution)/shard_map/ppermute | solution.py:414
  190.3 12.4 %home.3 = (bf16[4,2,256,512]{3,2,1,0:T(8,128)(2,1)}, bf16[4,2,256,512]{3,2,1,0:T(8,128)(2,1)}) custom-call(s32[64]{0:T(128)} %reshape.19.table, bf16[2,2,256,512]{3,2,1,0:T(8,128)(2,1)} %copy-done.1, bf16[2,2,256,512]{3,2,1,0:T(8,128)(2,1)} %get-tuple-element.36.refs_9_.refs_25_.refs_1_, ...), custom_call_target="tpu_custom_call" | custom-call | flops 167772160 | bytes 12582912 | tf_op jit(solution)/shard_map/home/pallas_call | solution.py:256
  202.7 12.4 %density.3 = bf16[2,2,512,512]{3,2,1,0:T(8,128)(2,1)} custom-call(bf16[4,2,2,512,512]{4,3,2,1,0:T(8,128)(2,1)} %green.5, f32[4,2,1,512]{3,2,1,0:T(1,128)} %broadcast_in_dim.36.gamma, bf16[4,2,256,512]{3,2,1,0:T(8,128)(2,1)} %get-tuple-element.35.refs_3_.refs_0_, bf16[4,2,256,512]{3,2,1,0:T(8,128)(2,1)} %get-tuple-element.39.refs_1_, ...), custom_call_target="tpu_custom_call" | custom-call | flops 8589934592 | bytes 10485760 | tf_op jit(solution)/shard_map/density/pallas_call | solution.py:378
  215.2 3.2 %copy.23 = bf16[2,2,32,16,512]{4,3,1,0,2:T(8,128)(2,1)} copy(bf16[2,2,32,16,512]{4,3,2,1,0:T(8,128)(2,1)} %bitcast.27) | data formatting | bytes 4194304 | tf_op jit(solution)/shard_map/reshape | solution.py:484
  218.3 9.4 %all-to-all-start.1 = ((bf16[2,2,32,16,512]{4,3,1,0,2:T(8,128)(2,1)}), bf16[2,2,32,16,512]{4,3,1,0,2:T(8,128)(2,1)S(1)}, u32[]{:S(2)}, u32[]{:S(2)}) async-start(bf16[2,2,32,16,512]{4,3,1,0,2:T(8,128)(2,1)} %copy.23), calls=%async_computation.1 | async-start | bytes 4194304 | tf_op jit(solution)/shard_map/all_to_all | solution.py:485
  227.7 12.4 %density.2 = bf16[2,2,512,512]{3,2,1,0:T(8,128)(2,1)} custom-call(bf16[4,2,2,512,512]{4,3,2,1,0:T(8,128)(2,1)} %green.5, f32[4,2,1,512]{3,2,1,0:T(1,128)} %broadcast_in_dim.36.gamma, bf16[4,2,256,512]{3,2,1,0:T(8,128)(2,1)} %get-tuple-element.35.refs_3_.refs_0_, bf16[4,2,256,512]{3,2,1,0:T(8,128)(2,1)} %get-tuple-element.39.refs_1_, ...), custom_call_target="tpu_custom_call" | custom-call | flops 8589934592 | bytes 10485760 | tf_op jit(solution)/shard_map/density/pallas_call | solution.py:378
  240.1 3.2 %copy.21 = bf16[2,2,32,16,512]{4,3,1,0,2:T(8,128)(2,1)} copy(bf16[2,2,32,16,512]{4,3,2,1,0:T(8,128)(2,1)} %bitcast.26) | data formatting | bytes 4194304 | tf_op jit(solution)/shard_map/reshape | solution.py:484
  243.3 13.9 %all-to-all-done.1 = bf16[2,2,32,16,512]{4,3,1,0,2:T(8,128)(2,1)S(1)} async-done(((bf16[2,2,32,16,512]{4,3,1,0,2:T(8,128)(2,1)}), bf16[2,2,32,16,512]{4,3,1,0,2:T(8,128)(2,1)S(1)}, u32[]{:S(2)}, u32[]{:S(2)}) %all-to-all-start.1) | async-done | bytes 2097184 | tf_op jit(solution)/shard_map/all_to_all | solution.py:485
  257.3 5.7 %all-to-all-start = ((bf16[2,2,32,16,512]{4,3,1,0,2:T(8,128)(2,1)}), bf16[2,2,32,16,512]{4,3,1,0,2:T(8,128)(2,1)}, u32[]{:S(2)}, u32[]{:S(2)}) async-start(bf16[2,2,32,16,512]{4,3,1,0,2:T(8,128)(2,1)} %copy.21), calls=%async_computation | async-start | bytes 4194304 | tf_op jit(solution)/shard_map/all_to_all | solution.py:485
  263.6 28.5 %rows.1 = bf16[16,2,2,128,512]{4,3,2,1,0:T(8,128)(2,1)} custom-call(s32[1]{0:T(128)} %bitcast.tile, s32[256]{0:T(256)} %reshape.18.table, bf16[2,2,256,512]{3,2,1,0:T(8,128)(2,1)} %copy-done.3, bf16[2,2,256,512]{3,2,1,0:T(8,128)(2,1)} %get-tuple-element.30.refs_1_.refs_17_, bf16[2,2,256,512]{3,2,1,0:T(8,128)(2,1)} %get-tuple-element.31.refs_2_.refs_18_, ...), custom_call_target="tpu_custom_call" | custom-call | flops 671088640 | bytes 25165824 | tf_op jit(solution)/shard_map/rows/pallas_call | solution.py:327
  (91 shorter events, 33.4 us)
Async XLA Ops:
  0.6 48.8 %collective-permute-start.3 = (bf16[16,128,512]{2,1,0:T(8,128)(2,1)}, bf16[16,128,512]{2,1,0:T(8,128)(2,1)S(1)}, u32[]{:S(2)}, u32[]{:S(2)}) collective-permute-start(bf16[16,128,512]{2,1,0:T(8,128)(2,1)} %refs_32_.1), channel_id=1, source_target_pairs={{0,6},{1,7},{2,4},{3,5},{4,2},{5,3},{6,0},{7,1},{8,14},{9,15},{10,... | collective-permute-start | bytes 6291464 | tf_op jit(solution)/shard_map/ppermute | solution.py:414
  15.7 24.9 %collective-permute-start = (bf16[2,2,256,512]{3,2,1,0:T(8,128)(2,1)}, bf16[2,2,256,512]{3,2,1,0:T(8,128)(2,1)}, u32[]{:S(2)}, u32[]{:S(2)}) collective-permute-start(bf16[2,2,256,512]{3,2,1,0:T(8,128)(2,1)} %get-tuple-element.23), channel_id=1, source_target_pairs={{0,4},{1,5},{2,6},{3,7},{4,0},{5,1},{6,2},{7,3},{8,12},{9,13},{10,... | collective-permute-start | bytes 3145736 | tf_op jit(solution)/shard_map/ppermute | solution.py:414
  15.9 32.4 %collective-permute-start.1 = (bf16[2,2,256,512]{3,2,1,0:T(8,128)(2,1)}, bf16[2,2,256,512]{3,2,1,0:T(8,128)(2,1)}, u32[]{:S(2)}, u32[]{:S(2)}) collective-permute-start(bf16[2,2,256,512]{3,2,1,0:T(8,128)(2,1)} %get-tuple-element.22.own), channel_id=1, source_target_pairs={{4,12},{8,0},{12,20},{16,8},{20,28},{24,16},{28,36},{32,24},{36,44... | collective-permute-start | bytes 3145736 | tf_op jit(solution)/shard_map/ppermute | solution.py:423
  40.6 25.0 %collective-permute-start.2 = (bf16[2,2,256,512]{3,2,1,0:T(8,128)(2,1)}, bf16[2,2,256,512]{3,2,1,0:T(8,128)(2,1)}, u32[]{:S(2)}, u32[]{:S(2)}) collective-permute-start(bf16[2,2,256,512]{3,2,1,0:T(8,128)(2,1)} %collective-permute-done.got), channel_id=1, source_target_pairs={{0,8},{8,16},{12,4},{16,24},{20,12},{24,32},{28,20},{32,40},{36,28... | collective-permute-start | bytes 3145736 | tf_op jit(solution)/shard_map/ppermute | solution.py:423
  45.1 28.5 %collective-permute-start.7 = (bf16[2,2,256,512]{3,2,1,0:T(8,128)(2,1)}, bf16[2,2,256,512]{3,2,1,0:T(8,128)(2,1)S(1)}, u32[]{:S(2)}, u32[]{:S(2)}) collective-permute-start(bf16[2,2,256,512]{3,2,1,0:T(8,128)(2,1)} %get-tuple-element.27), channel_id=1, source_target_pairs={{0,4},{1,5},{2,6},{3,7},{4,0},{5,1},{6,2},{7,3},{8,12},{9,13},{10,... | collective-permute-start | bytes 3145736 | tf_op jit(solution)/shard_map/ppermute | solution.py:414
  45.1 36.8 %collective-permute-start.10 = (bf16[16,128,512]{2,1,0:T(8,128)(2,1)}, bf16[16,128,512]{2,1,0:T(8,128)(2,1)}, u32[]{:S(2)}, u32[]{:S(2)}) collective-permute-start(bf16[16,128,512]{2,1,0:T(8,128)(2,1)} %refs_32_.1), channel_id=1, source_target_pairs={{0,1},{1,0},{2,3},{3,2},{4,5},{5,4},{6,7},{7,6},{8,9},{9,8},{10,11... | collective-permute-start | bytes 6291464 | tf_op jit(solution)/shard_map/ppermute | solution.py:414
  74.6 8.1 %collective-permute-start.11 = (bf16[16,128,512]{2,1,0:T(8,128)(2,1)}, bf16[16,128,512]{2,1,0:T(8,128)(2,1)S(1)}, u32[]{:S(2)}, u32[]{:S(2)}) collective-permute-start(bf16[16,128,512]{2,1,0:T(8,128)(2,1)} %held_back.3.refs_2_), channel_id=1, source_target_pairs={{0,1},{1,0},{2,3},{3,2},{4,5},{5,4},{6,7},{7,6},{8,9},{9,8},{10,11... | collective-permute-start | bytes 6291464 | tf_op jit(solution)/shard_map/ppermute | solution.py:414
  74.6 37.9 %collective-permute-start.8 = (bf16[2,2,256,512]{3,2,1,0:T(8,128)(2,1)}, bf16[2,2,256,512]{3,2,1,0:T(8,128)(2,1)S(1)}, u32[]{:S(2)}, u32[]{:S(2)}) collective-permute-start(bf16[2,2,256,512]{3,2,1,0:T(8,128)(2,1)} %get-tuple-element.26.own), channel_id=1, source_target_pairs={{4,12},{8,0},{12,20},{16,8},{20,28},{24,16},{28,36},{32,24},{36,44... | collective-permute-start | bytes 3145736 | tf_op jit(solution)/shard_map/ppermute | solution.py:423
  75.9 36.7 %collective-permute-start.9 = (bf16[2,2,256,512]{3,2,1,0:T(8,128)(2,1)}, bf16[2,2,256,512]{3,2,1,0:T(8,128)(2,1)}, u32[]{:S(2)}, u32[]{:S(2)}) collective-permute-start(bf16[2,2,256,512]{3,2,1,0:T(8,128)(2,1)} %copy-done.6), channel_id=1, source_target_pairs={{0,8},{8,16},{12,4},{16,24},{20,12},{24,32},{28,20},{32,40},{36,28... | collective-permute-start | bytes 3145736 | tf_op jit(solution)/shard_map/ppermute | solution.py:423
  81.9 40.2 %collective-permute-start.5 = (bf16[2,2,256,512]{3,2,1,0:T(8,128)(2,1)}, bf16[2,2,256,512]{3,2,1,0:T(8,128)(2,1)}, u32[]{:S(2)}, u32[]{:S(2)}) collective-permute-start(bf16[2,2,256,512]{3,2,1,0:T(8,128)(2,1)} %get-tuple-element.25), channel_id=1, source_target_pairs={{0,6},{1,7},{2,4},{3,5},{4,2},{5,3},{6,0},{7,1},{8,14},{9,15},{10,... | collective-permute-start | bytes 3145736 | tf_op jit(solution)/shard_map/ppermute | solution.py:414
  81.9 40.2 %collective-permute-start.4 = (bf16[2,2,256,512]{3,2,1,0:T(8,128)(2,1)}, bf16[2,2,256,512]{3,2,1,0:T(8,128)(2,1)}, u32[]{:S(2)}, u32[]{:S(2)}) collective-permute-start(bf16[2,2,256,512]{3,2,1,0:T(8,128)(2,1)} %get-tuple-element.25), channel_id=1, source_target_pairs={{0,4},{1,5},{2,6},{3,7},{4,0},{5,1},{6,2},{7,3},{8,12},{9,13},{10,... | collective-permute-start | bytes 3145736 | tf_op jit(solution)/shard_map/ppermute | solution.py:414
  83.9 48.4 %collective-permute-start.6 = (bf16[2,2,256,512]{3,2,1,0:T(8,128)(2,1)S(1)}, bf16[2,2,256,512]{3,2,1,0:T(8,128)(2,1)}, u32[]{:S(2)}, u32[]{:S(2)}) collective-permute-start(bf16[2,2,256,512]{3,2,1,0:T(8,128)(2,1)S(1)} %get-tuple-element.24.refs_0_.refs_16_), channel_id=1, source_target_pairs={{0,2},{1,3},{2,0},{3,1},{4,6},{5,7},{6,4},{7,5},{8,10},{9,11},{10,... | collective-permute-start | bytes 3145736 | tf_op jit(solution)/shard_map/ppermute | solution.py:414
  112.5 21.3 %collective-permute-start.12 = (bf16[2,2,256,512]{3,2,1,0:T(8,128)(2,1)S(1)}, bf16[2,2,256,512]{3,2,1,0:T(8,128)(2,1)}, u32[]{:S(2)}, u32[]{:S(2)}) collective-permute-start(bf16[2,2,256,512]{3,2,1,0:T(8,128)(2,1)S(1)} %get-tuple-element.24.refs_0_.refs_16_), channel_id=1, source_target_pairs={{0,1},{1,0},{2,3},{3,2},{4,5},{5,4},{6,7},{7,6},{8,9},{9,8},{10,11... | collective-permute-start | bytes 3145736 | tf_op jit(solution)/shard_map/ppermute | solution.py:414
  132.3 3.1 %collective-permute-start.13 = (bf16[2,2,256,512]{3,2,1,0:T(8,128)(2,1)}, bf16[2,2,256,512]{3,2,1,0:T(8,128)(2,1)}, u32[]{:S(2)}, u32[]{:S(2)}) collective-permute-start(bf16[2,2,256,512]{3,2,1,0:T(8,128)(2,1)} %get-tuple-element.30.refs_1_.refs_17_), channel_id=1, source_target_pairs={{0,1},{1,0},{2,3},{3,2},{4,5},{5,4},{6,7},{7,6},{8,9},{9,8},{10,11... | collective-permute-start | bytes 3145736 | tf_op jit(solution)/shard_map/ppermute | solution.py:414
  132.4 6.7 %collective-permute-start.14 = (bf16[2,2,256,512]{3,2,1,0:T(8,128)(2,1)}, bf16[2,2,256,512]{3,2,1,0:T(8,128)(2,1)}, u32[]{:S(2)}, u32[]{:S(2)}) collective-permute-start(bf16[2,2,256,512]{3,2,1,0:T(8,128)(2,1)} %get-tuple-element.31.refs_2_.refs_18_), channel_id=1, source_target_pairs={{0,1},{1,0},{2,3},{3,2},{4,5},{5,4},{6,7},{7,6},{8,9},{9,8},{10,11... | collective-permute-start | bytes 3145736 | tf_op jit(solution)/shard_map/ppermute | solution.py:414
  132.9 6.2 %collective-permute-start.15 = (bf16[2,2,256,512]{3,2,1,0:T(8,128)(2,1)}, bf16[2,2,256,512]{3,2,1,0:T(8,128)(2,1)}, u32[]{:S(2)}, u32[]{:S(2)}) collective-permute-start(bf16[2,2,256,512]{3,2,1,0:T(8,128)(2,1)} %get-tuple-element.32.refs_3_.refs_19_), channel_id=1, source_target_pairs={{0,1},{1,0},{2,3},{3,2},{4,5},{5,4},{6,7},{7,6},{8,9},{9,8},{10,11... | collective-permute-start | bytes 3145736 | tf_op jit(solution)/shard_map/ppermute | solution.py:414
  133.6 26.5 %collective-permute-start.17 = (bf16[2,2,256,512]{3,2,1,0:T(8,128)(2,1)S(1)}, bf16[2,2,256,512]{3,2,1,0:T(8,128)(2,1)}, u32[]{:S(2)}, u32[]{:S(2)}) collective-permute-start(bf16[2,2,256,512]{3,2,1,0:T(8,128)(2,1)S(1)} %copy-done.10), channel_id=1, source_target_pairs={{0,6},{1,7},{2,4},{3,5},{4,2},{5,3},{6,0},{7,1},{8,14},{9,15},{10,... | collective-permute-start | bytes 3145736 | tf_op jit(solution)/shard_map/ppermute | solution.py:414
  133.8 26.2 %collective-permute-start.16 = (bf16[2,2,256,512]{3,2,1,0:T(8,128)(2,1)S(1)}, bf16[2,2,256,512]{3,2,1,0:T(8,128)(2,1)S(1)}, u32[]{:S(2)}, u32[]{:S(2)}) collective-permute-start(bf16[2,2,256,512]{3,2,1,0:T(8,128)(2,1)S(1)} %copy-done.10), channel_id=1, source_target_pairs={{0,4},{1,5},{2,6},{3,7},{4,0},{5,1},{6,2},{7,3},{8,12},{9,13},{10,... | collective-permute-start | bytes 3145736 | tf_op jit(solution)/shard_map/ppermute | solution.py:414
  135.4 48.1 %collective-permute-start.18 = (bf16[2,2,256,512]{3,2,1,0:T(8,128)(2,1)S(1)}, bf16[2,2,256,512]{3,2,1,0:T(8,128)(2,1)}, u32[]{:S(2)}, u32[]{:S(2)}) collective-permute-start(bf16[2,2,256,512]{3,2,1,0:T(8,128)(2,1)S(1)} %copy-done.2), channel_id=1, source_target_pairs={{0,2},{1,3},{2,0},{3,1},{4,6},{5,7},{6,4},{7,5},{8,10},{9,11},{10,... | collective-permute-start | bytes 3145736 | tf_op jit(solution)/shard_map/ppermute | solution.py:414
  139.2 44.8 %collective-permute-start.19 = (bf16[2,2,256,512]{3,2,1,0:T(8,128)(2,1)S(1)}, bf16[2,2,256,512]{3,2,1,0:T(8,128)(2,1)}, u32[]{:S(2)}, u32[]{:S(2)}) collective-permute-start(bf16[2,2,256,512]{3,2,1,0:T(8,128)(2,1)S(1)} %copy-done.2), channel_id=1, source_target_pairs={{0,1},{1,0},{2,3},{3,2},{4,5},{5,4},{6,7},{7,6},{8,9},{9,8},{10,11... | collective-permute-start | bytes 3145736 | tf_op jit(solution)/shard_map/ppermute | solution.py:414
  183.5 5.9 %collective-permute-start.21 = (bf16[2,2,256,512]{3,2,1,0:T(8,128)(2,1)}, bf16[2,2,256,512]{3,2,1,0:T(8,128)(2,1)S(1)}, u32[]{:S(2)}, u32[]{:S(2)}) collective-permute-start(bf16[2,2,256,512]{3,2,1,0:T(8,128)(2,1)} %get-tuple-element.37.refs_10_.refs_26_.refs_2_), channel_id=1, source_target_pairs={{0,1},{1,0},{2,3},{3,2},{4,5},{5,4},{6,7},{7,6},{8,9},{9,8},{10,11... | collective-permute-start | bytes 3145736 | tf_op jit(solution)/shard_map/ppermute | solution.py:414
  184.0 5.5 %collective-permute-start.22 = (bf16[2,2,256,512]{3,2,1,0:T(8,128)(2,1)}, bf16[2,2,256,512]{3,2,1,0:T(8,128)(2,1)}, u32[]{:S(2)}, u32[]{:S(2)}) collective-permute-start(bf16[2,2,256,512]{3,2,1,0:T(8,128)(2,1)} %get-tuple-element.38.refs_11_.refs_27_.refs_3_), channel_id=1, source_target_pairs={{0,1},{1,0},{2,3},{3,2},{4,5},{5,4},{6,7},{7,6},{8,9},{9,8},{10,11... | collective-permute-start | bytes 3145736 | tf_op jit(solution)/shard_map/ppermute | solution.py:414
  218.3 38.9 %all-to-all-start.1 = ((bf16[2,2,32,16,512]{4,3,1,0,2:T(8,128)(2,1)}), bf16[2,2,32,16,512]{4,3,1,0,2:T(8,128)(2,1)S(1)}, u32[]{:S(2)}, u32[]{:S(2)}) async-start(bf16[2,2,32,16,512]{4,3,1,0,2:T(8,128)(2,1)} %copy.23), calls=%async_computation.1 | async-start | bytes 4194304 | tf_op jit(solution)/shard_map/all_to_all | solution.py:485
  257.3 35.2 %all-to-all-start = ((bf16[2,2,32,16,512]{4,3,1,0,2:T(8,128)(2,1)}), bf16[2,2,32,16,512]{4,3,1,0,2:T(8,128)(2,1)}, u32[]{:S(2)}, u32[]{:S(2)}) async-start(bf16[2,2,32,16,512]{4,3,1,0,2:T(8,128)(2,1)} %copy.21), calls=%async_computation | async-start | bytes 4194304 | tf_op jit(solution)/shard_map/all_to_all | solution.py:485
  (20 other events, 236.3 us)

commit v5 on v4

v5 whole, which is shorter than its diff:
```python
import functools

import jax
import jax.numpy as jnp
from jax import lax
from jax.experimental import pallas as pl
from jax.experimental.pallas import tpu as pltpu
from jax.sharding import PartitionSpec as P

MIB = 1 << 20
NT = (((1,), (1,)), ((), ()))


def dot_nt(left, right):
    return lax.dot_general(left, right, NT, preferred_element_type=jnp.float32)


def dot_nn(left, right):
    return jnp.dot(left, right, preferred_element_type=jnp.float32)


def scale(block, gamma):
    return (block.astype(jnp.float32) * gamma).astype(jnp.bfloat16)


def lesser_kernel(place, green, gamma, *outs):
    norb = green.shape[-1]
    rows = outs[0].shape[3]
    gam = gamma[0, 0]
    g_re, g_im = green[0, 0, 0], green[0, 0, 1]
    wide_re = g_re.astype(jnp.float32)
    wide_im = g_im.astype(jnp.float32)
    less = (wide_re - wide_im).astype(jnp.bfloat16)
    more = (wide_re + wide_im).astype(jnp.bfloat16)
    total = dot_nt(scale(g_re, gam), less) + dot_nt(scale(g_im, gam), more)
    total = total.astype(jnp.bfloat16)
    for side in range(2):

        @pl.when(pl.program_id(0) // 2 == side)
        def _():
            for c in range(norb // rows):
                outs[side][c, 0, 0] = total[c * rows : (c + 1) * rows]


def packed_lesser(place, green, gamma, chunks):
    energies, norb = green.shape[1], green.shape[-1]
    half = green.shape[0] // 2
    rows = norb // chunks

    def which(k, p):
        return ((p[0] + 1 + k // half) % 2) * half + k % half

    def block_of(side):
        def index(k, e, p):
            if side == 0:
                return (0, jnp.minimum(k, half - 1), jnp.where(k < half, e, energies - 1), 0, 0)
            return (0, jnp.maximum(k - half, 0), jnp.where(k < half, 0, e), 0, 0)

        return pl.BlockSpec((chunks, 1, 1, rows, norb), index)

    out = jax.ShapeDtypeStruct((chunks, half, energies, rows, norb), jnp.bfloat16)
    outs = pl.pallas_call(
        lesser_kernel,
        grid_spec=pltpu.PrefetchScalarGridSpec(
            num_scalar_prefetch=1,
            grid=(2 * half, energies),
            in_specs=[
                pl.BlockSpec((1, 1, 2, norb, norb), lambda k, e, p: (which(k, p), e, 0, 0, 0)),
                pl.BlockSpec((1, 1, 1, norb), lambda k, e, p: (which(k, p), e, 0, 0)),
            ],
            out_specs=[block_of(0), block_of(1)],
        ),
        out_shape=[out] * 2,
        compiler_params=pltpu.CompilerParams(vmem_limit_bytes=60 * MIB),
        cost_estimate=pl.CostEstimate(
            flops=8 * half * energies * norb**3,
            bytes_accessed=12 * half * energies * norb**2,
            transcendentals=0,
        ),
        name="lesser",
    )(place, green, gamma)
    return outs


def identity(n):
    rows = lax.broadcasted_iota(jnp.int32, (n, n), 0)
    cols = lax.broadcasted_iota(jnp.int32, (n, n), 1)
    return (rows == cols).astype(jnp.float32).astype(jnp.bfloat16)


def exchange_kernel(
    weights, sent, own, coupling, src, coup, coup_t,
    got, own_halo, got_halo, mine, other, tiles, turned, send, recv, local,
):
    energy, mom = lax.axis_index("energy"), lax.axis_index("mom")
    pairs = lax.axis_size("energy") // 2
    x_lo, pair = energy % 2, energy // 2
    chunks, half, _, rows, norb = sent.shape
    points, height, _ = coupling.shape
    energy_a = energy + 1 - 2 * x_lo
    mom_core = mom + 1 - 2 * (mom % 2)
    mom_hi = mom + 2 - 4 * (mom // 2)
    mom_both = 3 - mom
    place = [mom, mom_core, mom_hi, mom_both]
    ring_a, ring_b, ring_ab = (energy_a, mom), (energy_a, mom_hi), (energy, mom_hi)
    core = (energy, mom_core)
    own_to = (energy - 2 + 4 * x_lo, mom)
    got_to = (energy + 2 - 4 * x_lo, mom)
    low, high = pair > 0, pair < pairs - 1
    first = x_lo == 0
    has_own_to = jnp.logical_or(
        jnp.logical_and(first, low), jnp.logical_and(jnp.logical_not(first), high)
    )
    has_got_to = jnp.logical_or(
        jnp.logical_and(first, high), jnp.logical_and(jnp.logical_not(first), low)
    )

    def remote(kind, c, source, target, device):
        return pltpu.make_async_remote_copy(
            src_ref=source,
            dst_ref=target,
            send_sem=send.at[kind, c],
            recv_sem=recv.at[kind, c],
            device_id=device,
            device_id_type=pl.DeviceIdType.MESH,
        )

    swap = [remote(0, c, sent.at[c], got.at[c], ring_a) for c in range(chunks)]
    to_own = [remote(1, c, own.at[c], own_halo.at[c], own_to) for c in range(chunks)]
    to_got = [remote(2, c, got.at[c], got_halo.at[c], got_to) for c in range(chunks)]
    near = [
        [
            remote(3, c, other.at[c], src.at[c, 1], ring_a),
            remote(4, c, other.at[c], src.at[c, 2], ring_b),
            remote(5, c, mine.at[c], src.at[c, 3], ring_ab),
        ]
        for c in range(chunks)
    ]
    far = [
        [remote(6, c, mine.at[c], src.at[c, 4], core)]
        + [remote(6 + s, c, src.at[c, s], src.at[c, 4 + s], core) for s in (1, 2, 3)]
        for c in range(chunks)
    ]
    stay = [pltpu.make_async_copy(mine.at[c], src.at[c, 0], local.at[c]) for c in range(chunks)]
    tile_core = remote(10, 0, coupling, tiles.at[1], core)
    tile_b = remote(10, 1, coupling, tiles.at[2], ring_b)
    tile_bc = remote(10, 2, tiles.at[2], tiles.at[3], core)
    tile_own = pltpu.make_async_copy(coupling, tiles.at[0], local.at[chunks])
    placed = [
        (
            pltpu.make_async_copy(
                tiles.at[s],
                coup.at[:, pl.ds(pl.multiple_of(place[s] * height, height), height), :],
                local.at[chunks + 1 + 2 * s],
            ),
            pltpu.make_async_copy(
                turned.at[s],
                coup_t.at[:, :, pl.ds(pl.multiple_of(place[s] * height, height), height)],
                local.at[chunks + 2 + 2 * s],
            ),
        )
        for s in range(4)
    ]

    barrier = pltpu.get_barrier_semaphore()

    def greet(device):
        pl.semaphore_signal(
            barrier, inc=1, device_id=device, device_id_type=pl.DeviceIdType.MESH
        )

    for device in (ring_a, ring_b, ring_ab, core):
        greet(device)

    @pl.when(has_own_to)
    def _():
        greet(own_to)

    @pl.when(has_got_to)
    def _():
        greet(got_to)

    pl.semaphore_wait(barrier, 4 + jnp.where(low, 1, 0) + jnp.where(high, 1, 0))

    swap[0].start()
    swap[1].start()

    @pl.when(has_own_to)
    def _():
        for c in range(chunks):
            to_own[c].start()

    tile_b.start()
    tile_core.start()
    tile_own.start()

    step = 16
    slabs = rows // step

    def clear(halo):
        def one(i, carry):
            c, r = i // slabs, i % slabs
            at = pl.ds(pl.multiple_of(r * step, step), step)
            for k in range(half):
                for e in range(2):
                    halo[c, k, e, at, :] = jnp.zeros((step, norb), halo.dtype)
            return carry

        lax.fori_loop(0, chunks * slabs, one, 0)

    @pl.when(jnp.logical_not(has_got_to))
    def _():
        clear(own_halo)

    @pl.when(jnp.logical_not(has_own_to))
    def _():
        clear(got_halo)

    turn = identity(norb // 2)

    def fold(s):
        def one(q, carry):
            for b in range(2):
                span = slice(b * (norb // 2), (b + 1) * (norb // 2))
                turned[s, q, span, :] = dot_nt(turn, tiles[s, q, :, span]).astype(turned.dtype)
            return carry

        lax.fori_loop(0, points, one, 0)
        for copy in placed[s]:
            copy.start()

    def shift(c, parts, outs):
        def one(i, carry):
            k, r = i // slabs, i % slabs
            at = pl.ds(pl.multiple_of(r * step, step), step)
            levels = [ref[c, k, e, at, :].astype(jnp.float32) for ref in parts for e in range(2)]
            for o in range(4):
                total = weights[0] * levels[o + 3] + weights[1] * levels[o + 4]
                total = total + weights[2] * levels[o + 1] + weights[3] * levels[o]
                outs[o // 2][c, k, o % 2, at, :] = total.astype(mine.dtype)
            return carry

        lax.fori_loop(0, half * slabs, one, 0)

    for c in range(chunks + 1):
        if c < chunks:
            swap[c].wait_recv()

            @pl.when(has_got_to)
            def _(copy=to_got[c]):
                copy.start()

            if c + 2 < chunks:
                swap[c + 2].start()
        if c == 0:
            tile_own.wait()
            fold(0)
        else:
            d = c - 1

            @pl.when(has_got_to)
            def _(copy=to_own[d]):
                copy.wait_recv()

            @pl.when(has_own_to)
            def _(copy=to_got[d]):
                copy.wait_recv()

            @pl.when(first)
            def _(d=d):
                shift(d, (got_halo, own, got, own_halo), (mine, other))

            @pl.when(jnp.logical_not(first))
            def _(d=d):
                shift(d, (own_halo, got, own, got_halo), (other, mine))

            for copy in near[d]:
                copy.start()
            far[d][0].start()
            stay[d].start()
        if c == 1:
            tile_core.wait_recv()
            fold(1)

    tile_b.wait_recv()
    tile_bc.start()
    fold(2)
    for c in range(chunks):
        for s in (1, 2, 3):
            near[c][s - 1].wait_recv()
            far[c][s].start()
        if c == 0:
            tile_bc.wait_recv()
            fold(3)
    for c in range(chunks):
        for copy in far[c]:
            copy.wait_recv()
        for copy in [swap[c]] + near[c] + far[c]:
            copy.wait_send()
        stay[c].wait()

        @pl.when(has_own_to)
        def _(copy=to_own[c]):
            copy.wait_send()

        @pl.when(has_got_to)
        def _(copy=to_got[c]):
            copy.wait_send()

    for copy in (tile_core, tile_b, tile_bc):
        copy.wait_send()
    for pair_of in placed:
        for copy in pair_of:
            copy.wait()


def exchanged(weights, sent, own, coupling):
    chunks, half, energies, rows, norb = sent.shape
    points, height, _ = coupling.shape
    whole = jax.ShapeDtypeStruct((points, norb, norb), jnp.bfloat16)
    vmem = pl.BlockSpec(memory_space=pltpu.VMEM)
    hbm = pl.BlockSpec(memory_space=pl.ANY)
    part = pltpu.VMEM(sent.shape, jnp.bfloat16)
    return pl.pallas_call(
        exchange_kernel,
        in_specs=[pl.BlockSpec(memory_space=pltpu.SMEM), vmem, vmem, hbm],
        out_specs=[hbm] * 3,
        out_shape=[
            jax.ShapeDtypeStruct((chunks, 8, half, energies, rows, norb), jnp.bfloat16),
            whole,
            whole,
        ],
        scratch_shapes=[part] * 5
        + [
            pltpu.VMEM((4, points, height, norb), jnp.bfloat16),
            pltpu.VMEM((4, points, norb, height), jnp.bfloat16),
            pltpu.SemaphoreType.DMA((11, chunks)),
            pltpu.SemaphoreType.DMA((11, chunks)),
            pltpu.SemaphoreType.DMA((chunks + 9,)),
        ],
        compiler_params=pltpu.CompilerParams(
            collective_id=0, has_side_effects=True, vmem_limit_bytes=60 * MIB
        ),
        name="exchange",
    )(weights, sent, own, coupling)


def add_products(targets, streams, picks, donor, factor, at, store):
    acc = [[None] * streams for _ in range(targets)]
    kept = {}
    for quad in range(4):
        held = [[donor(4 * quad + d, n, at) for n in range(streams)] for d in range(4)]
        for t in range(targets):
            c = [factor[picks(t, 4 * quad + d), at[0], at[1]] for d in range(4)]
            for n in range(streams):
                part = (c[0] * held[0][n] + c[1] * held[1][n]) + (
                    c[2] * held[2][n] + c[3] * held[3][n]
                )
                if quad % 2 == 0:
                    kept[t, n] = part
                    continue
                part = (kept.pop((t, n)) + part).astype(jnp.float32)
                acc[t][n] = part if acc[t][n] is None else acc[t][n] + part
    for t in range(targets):
        for n in range(streams):
            store(t, n, at, acc[t][n])


def home_kernel(table, *refs):
    sources, coup, coup_t, out, out_t = refs
    targets, _, height, norb = out.shape

    def picks(t, d):
        return table[t * 16 + d]

    def donor(d, n, at):
        return sources[0, d // 2, d % 2, n, at[0], at[1]]

    def into(ref):
        def store(t, n, at, value):
            ref[t, n, at[0], at[1]] = value.astype(jnp.bfloat16)

        return store

    def slab(i, carry):
        at = (
            pl.ds(pl.multiple_of(i // 2 * 16, 16), 16),
            pl.ds(pl.multiple_of(i % 2 * (norb // 2), norb // 2), norb // 2),
        )
        add_products(targets, 2, picks, donor, coup, at, into(out))
        add_products(targets, 2, picks, donor, coup_t, at, into(out_t))
        return carry

    lax.fori_loop(0, height // 16 * 2, slab, 0)


def home_sums(table, src, coup, coup_t, targets):
    chunks, _, half, energies, rows, norb = src.shape
    points = coup.shape[0]
    height = rows // 2
    steps = rows // height
    given = pl.BlockSpec(
        (1, 8, half, energies, height, norb), lambda i, q: (i // steps, 0, 0, 0, i % steps, 0)
    )
    factor = pl.BlockSpec((points, height, norb), lambda i, q: (0, i, 0))
    result = pl.BlockSpec((targets, energies, height, norb), lambda i, q: (0, 0, i, 0))
    out = jax.ShapeDtypeStruct((targets, energies, chunks * rows, norb), jnp.bfloat16)
    return pl.pallas_call(
        home_kernel,
        grid_spec=pltpu.PrefetchScalarGridSpec(
            num_scalar_prefetch=1,
            grid=(chunks * steps,),
            in_specs=[given] + [factor] * 2,
            out_specs=[result] * 2,
        ),
        out_shape=[out, out],
        compiler_params=pltpu.CompilerParams(vmem_limit_bytes=60 * MIB),
        name="home",
    )(table, src, coup, coup_t)


def rows_kernel(tile, table, rows_of, cols_of, coup, out, source):
    targets, _, _, height, norb = out.shape
    group = pl.program_id(1) * targets

    @pl.when(pl.program_id(1) == 0)
    def _():
        turn = identity(height)
        for d in range(16):
            for b in range(norb // height):
                span = slice(b * height, (b + 1) * height)
                straight = rows_of[0, d // 2, d % 2, 0, :, span].astype(jnp.float32)
                turned = dot_nt(turn, cols_of[b, d // 2, d % 2, 0])
                source[d, 0, :, span] = (straight + turned).astype(jnp.bfloat16)
                source[d, 1, :, span] = (straight - turned).astype(jnp.bfloat16)

    def picks(t, d):
        return table[(group + t) * 16 + d]

    def donor(d, n, at):
        return source[d, n, at[0], at[1]]

    def store(t, n, at, value):
        out[t, 0, n, at[0], at[1]] = value.astype(jnp.bfloat16)

    def slab(i, carry):
        at = (
            pl.ds(pl.multiple_of(i // 2 * 16, 16), 16),
            pl.ds(pl.multiple_of(i % 2 * (norb // 2), norb // 2), norb // 2),
        )
        add_products(targets, 2, picks, donor, coup, at, store)
        return carry

    lax.fori_loop(0, height // 16 * 2, slab, 0)


def row_sums(tile, table, src, coupling, targets):
    chunks, _, half, energies, rows, norb = src.shape
    points, height, _ = coupling.shape
    row_block = pl.BlockSpec(
        (1, 8, half, 1, rows, norb), lambda e, g, t, q: (t[0], 0, 0, e, 0, 0)
    )
    col_block = pl.BlockSpec(
        (chunks, 8, half, 1, rows, height), lambda e, g, t, q: (0, 0, 0, e, 0, t[0])
    )
    return pl.pallas_call(
        rows_kernel,
        grid_spec=pltpu.PrefetchScalarGridSpec(
            num_scalar_prefetch=2,
            grid=(energies, points // targets),
            in_specs=[
                row_block,
                col_block,
                pl.BlockSpec((points, height, norb), lambda e, g, t, q: (0, 0, 0)),
            ],
            out_specs=pl.BlockSpec(
                (targets, 1, 2, height, norb), lambda e, g, t, q: (g, e, 0, 0, 0)
            ),
            scratch_shapes=[pltpu.VMEM((16, 2, height, norb), jnp.bfloat16)],
        ),
        out_shape=jax.ShapeDtypeStruct((points, energies, 2, height, norb), jnp.bfloat16),
        compiler_params=pltpu.CompilerParams(vmem_limit_bytes=60 * MIB),
        name="rows",
    )(tile, table, src, src, coupling)


def density_kernel(inverse, green, gamma, us, vs, out):
    d_re = d_im = None
    for e in range(green.shape[1]):
        g_re, g_im = green[0, e, 0], green[0, e, 1]
        gam = gamma[0, e]
        wide_re, wide_im = g_re.astype(jnp.float32), g_im.astype(jnp.float32)
        less = (wide_re - wide_im).astype(jnp.bfloat16)
        more = (wide_re + wide_im).astype(jnp.bfloat16)
        u, v = us[0, e], vs[0, e]
        m_re = dot_nn(less, u) + dot_nt(more, v) + scale(g_re, gam).astype(jnp.float32)
        m_im = dot_nn(more, u) - dot_nt(less, v) + scale(g_im, gam).astype(jnp.float32)
        m_re, m_im = m_re.astype(jnp.bfloat16), m_im.astype(jnp.bfloat16)
        one = dot_nt(m_re, g_re) + dot_nt(m_im, g_im)
        two = dot_nt(m_im, g_re) - dot_nt(m_re, g_im)
        d_re = one if d_re is None else d_re + one
        d_im = two if d_im is None else d_im + two
    shape = out.shape[2:]
    out[0, 0] = (d_re * inverse).astype(jnp.bfloat16).reshape(shape)
    out[0, 1] = (d_im * inverse).astype(jnp.bfloat16).reshape(shape)


def partial_density(green, gamma, us, vs, inverse, owners):
    count, energies, _, norb, _ = green.shape
    rows = norb // owners
    part = pl.BlockSpec((1, energies, norb, norb), lambda k: (k, 0, 0, 0))
    return pl.pallas_call(
        functools.partial(density_kernel, inverse),
        grid=(count,),
        in_specs=[
            pl.BlockSpec((1, energies, 2, norb, norb), lambda k: (k, 0, 0, 0, 0)),
            pl.BlockSpec((1, energies, 1, norb), lambda k: (k, 0, 0, 0)),
            part,
            part,
        ],
        out_specs=pl.BlockSpec((1, 2, owners, rows, norb), lambda k: (k, 0, 0, 0, 0)),
        out_shape=jax.ShapeDtypeStruct((count, 2, owners, rows, norb), jnp.bfloat16),
        compiler_params=pltpu.CompilerParams(vmem_limit_bytes=60 * MIB),
        name="density",
    )(green, gamma, us, vs)


def on_device(green, broadening, coupling, shift_steps, mode_weight, occupation, momentum_map):
    n_energy, n_mom = lax.axis_size("energy"), lax.axis_size("mom")
    local_k, local_e = green.shape[:2]
    half = local_k // 2
    points = momentum_map.shape[1]
    energy, mom = lax.axis_index("energy"), lax.axis_index("mom")
    x_lo = energy % 2

    def weight_of(step, factor):
        return 0.5 * jnp.sum(jnp.where(shift_steps == step, mode_weight * factor, 0.0))

    weights = jnp.stack(
        [weight_of(s, occupation + 1.0) for s in (1, 2)] + [weight_of(s, occupation) for s in (1, 2)]
    ).astype(jnp.float32)

    gamma = broadening[:, :, None, :]
    sent, own = packed_lesser(x_lo.astype(jnp.int32)[None], green, gamma, n_mom)
    src, coup, coup_t = exchanged(weights, sent, own, coupling)

    moves = [(0, 0), (1, 0), (1, 2), (0, 2)]
    moves = moves + [(lo, mo ^ 1) for lo, mo in moves]
    donors = jnp.stack(
        [(mom ^ mo) * local_k + (x_lo ^ lo) * half + kk for lo, mo in moves for kk in range(half)]
    ).astype(jnp.int32)
    table = jnp.sum(
        jnp.where(
            momentum_map[:, :, None] == donors[None, None, :],
            jnp.arange(points, dtype=jnp.int32)[None, :, None],
            0,
        ),
        axis=1,
    ).astype(jnp.int32)
    table_home = lax.dynamic_slice_in_dim(table, mom * local_k, local_k, 0).reshape(-1)

    us, vs = home_sums(table_home, src, coup, coup_t, local_k)
    part = partial_density(green, gamma, us, vs, 1.0 / (local_e * n_energy), n_energy)
    parts = lax.all_to_all(part, "energy", split_axis=2, concat_axis=2, tiled=True)
    self_energy = row_sums(
        mom.astype(jnp.int32)[None], table.reshape(-1), src, coupling, local_k
    )
    density = jnp.transpose(jnp.sum(parts.astype(jnp.float32), axis=2), (2, 0, 1, 3))
    return (self_energy, density)


def solution(mesh):
    return jax.shard_map(
        on_device,
        mesh=mesh,
        in_specs=(
            P("mom", "energy", None, None, None),
            P("mom", "energy", None),
            P(None, "mom", None),
            P(),
            P(),
            P(),
            P(),
        ),
        out_specs=(P(None, "energy", None, "mom", None), P("energy", "mom", None, None)),
        check_vma=False,
    )
```

time: 297 us -> 287 us (0.966); the launches traced: 295 us -> 282 us
  Pallas kernels: 122 us -> 223 us
  waiting for transfers between devices: 103 us -> 33.1 us
  starting transfers between devices: 40.4 us -> 8.32 us
  local copies, waits for them, and re-layouts: 23.2 us -> 8.34 us
    pallas_call x6 -> x1, Pallas kernels: 33.2 us -> 145 us  [exchanged(): pl.pallas_call(exchange_kernel, in_specs=[pl.BlockSpec(memory_space=pltpu...]
    ppermute x23 -> x0, waiting for transfers between devices: 88.7 us -> none  [the longest x19 73.8 us: flip(): return lax.ppermute(x, BOTH, perm)]
    ppermute x23 -> x0, starting transfers between devices: 25.3 us -> none  [the longest x4 13 us: along_pairs(): return lax.ppermute(x, 'energy', moves)]
    all_to_all x2 -> x1, waiting for transfers between devices: 13.9 us -> 33.1 us  [on_device(): lax.all_to_all(part, 'energy', split_axis=2, concat_axis=2, tiled=True)]
    unnamed x39 -> x1, local copies, waits for them, and re-layouts: 14.2 us -> 0.91 us
    all_to_all x2 -> x1, starting transfers between devices: 15.1 us -> 8.32 us  [on_device(): lax.all_to_all(part, 'energy', split_axis=2, concat_axis=2, tiled=True)]
    reshape x2 -> x0, local copies, waits for them, and re-layouts: 6.35 us -> none  [on_device(): part = part.reshape(half, 2, n_energy, norb // n_energy, norb)]
    pallas_call x0 -> x1, local copies, waits for them, and re-layouts: none -> 4.76 us  [partial_density(): pl.pallas_call(functools.partial(density_kernel, inverse), grid=(count,),...]
  transfers between devices with their start and end apart: 25 -> 1, of which waited for: 11 -> 1; matrix products, arithmetic and copies ran while one was open for 3% -> 0% of each run, Pallas kernels for 33% -> 9%
where the time goes in v5:
time: 287 us; the launch traced here: 282 us
  Pallas kernels  223 us (78%)
  waiting for transfers between devices  33.1 us (12%)
  local copies, waits for them, and re-layouts  8.34 us (3%)
  starting transfers between devices  8.32 us (3%)
  other arithmetic  5.91 us (2%)
  between operations  3.17 us (1%)
    pallas_call x1, Pallas kernels, exchanged(): pl.pallas_call(exchange_kernel, in_specs=[pl.BlockSpec(memory_space=pltpu...  145 us
    all_to_all x1, waiting for transfers between devices, on_device(): lax.all_to_all(part, 'energy', split_axis=2, concat_axis=2, tiled=True)  33.1 us
    pallas_call x1, Pallas kernels, row_sums(): pl.pallas_call(rows_kernel, grid_spec=pltpu.PrefetchScalarGridSpec(num_sc...  24.6 us
    pallas_call x1, Pallas kernels, partial_density(): pl.pallas_call(functools.partial(density_kernel, inverse), grid=(count,),...  21.8 us
    pallas_call x1, Pallas kernels, home_sums(): pl.pallas_call(home_kernel, grid_spec=pltpu.PrefetchScalarGridSpec(num_sc...  20.4 us
    pallas_call x1, Pallas kernels, packed_lesser(): pl.pallas_call(lesser_kernel, grid_spec=pltpu.PrefetchScalarGridSpec(num_...  10.8 us
    all_to_all x1, starting transfers between devices, on_device(): lax.all_to_all(part, 'energy', split_axis=2, concat_axis=2, tiled=True)  8.32 us
  transfers between devices with their start and end apart: 1, of which 1 were waited for; matrix products, arithmetic and copies ran while one was open for 0% of the time, Pallas kernels for 9%

profile of v5, /device:TPU:0, one launch (start us, length us, event | category | flops | bytes accessed | tf_op | source)
XLA Modules:
  0.0 281.6 jit_solution(513941763551672846)
XLA Ops:
  0.7 1.4 fusion
  4.5 0.1 stack.82
  4.6 0.8 select_reduce_fusion
  5.4 0.6 reshape.13.table
  6.0 1.3 broadcast_in_dim.36.gamma
  7.3 10.8 %lesser.1 = (bf16[4,2,2,128,512]{4,3,2,1,0:T(8,128)(2,1)}, bf16[4,2,2,128,512]{4,3,2,1,0:T(8,128)(2,1)}) custom-call(s32[1]{0:T(128)} %bitcast.21.place, bf16[4,2,2,512,512]{4,3,2,1,0:T(8,128)(2,1)} %green.3, f32[4,2,1,512]{3,2,1,0:T(1,128)} %broadcast_in_dim.36.gamma), custom_call_target="tpu_custom_call" | custom-call | flops 4294967296 | bytes 12582912 | tf_op jit(solution)/shard_map/lesser/pallas_call | solution.py:62
  18.1 0.6 pad_maximum_fusion.weights
  18.7 145.2 %exchange.1 = (bf16[4,8,2,2,128,512]{5,4,3,2,1,0:T(8,128)(2,1)}, bf16[16,512,512]{2,1,0:T(8,128)(2,1)}, bf16[16,512,512]{2,1,0:T(8,128)(2,1)}) custom-call(f32[4]{0:T(128)} %pad_maximum_fusion.weights, bf16[4,2,2,128,512]{4,3,2,1,0:T(8,128)(2,1)} %get-tuple-element.9.sent, bf16[4,2,2,128,512]{4,3,2,1,0:T(8,128)(2,1)} %get-tuple-element.10.own, ...), custom_call_target="tpu_custom_call" | custom-call | tf_op jit(solution)/shard_map/exchange/pallas_call | solution.py:324
  164.0 20.4 %home.1 = (bf16[4,2,512,512]{3,2,1,0:T(8,128)(2,1)}, bf16[4,2,512,512]{3,2,1,0:T(8,128)(2,1)}) custom-call(s32[64]{0:T(128)} %reshape.13.table, bf16[4,8,2,2,128,512]{5,4,3,2,1,0:T(8,128)(2,1)} %get-tuple-element.11.rows_of.cols_of.refs_0_, bf16[16,512,512]{2,1,0:T(8,128)(2,1)} %get-tuple-element.12.refs_1_, bf16[16,512,512]{2,1,0:T(8,128)(2,1)} %get-tuple-element.13.refs_2_), custom_call_target="tpu_custom_call" | custom-call | tf_op jit(solution)/shard_map/home/pallas_call | solution.py:408
  184.3 21.8 %density.1 = bf16[4,2,32,16,512]{4,3,2,1,0:T(8,128)(2,1)} custom-call(bf16[4,2,2,512,512]{4,3,2,1,0:T(8,128)(2,1)} %green.3, f32[4,2,1,512]{3,2,1,0:T(1,128)} %broadcast_in_dim.36.gamma, bf16[4,2,512,512]{3,2,1,0:T(8,128)(2,1)} %get-tuple-element.14.us, bf16[4,2,512,512]{3,2,1,0:T(8,128)(2,1)} %get-tuple-element.15.vs), custom_call_target="tpu_custom_call" | custom-call | tf_op jit(solution)/shard_map/density/pallas_call | solution.py:512
  206.1 4.8 %copy.12 = bf16[4,2,32,16,512]{4,3,1,0,2:T(8,128)(2,1)} copy(bf16[4,2,32,16,512]{4,3,2,1,0:T(8,128)(2,1)} %density.1) | data formatting | bytes 8388608 | tf_op jit(solution)/shard_map/density/pallas_call | solution.py:512
  210.9 8.3 %all-to-all-start = ((bf16[4,2,32,16,512]{4,3,1,0,2:T(8,128)(2,1)}), bf16[4,2,32,16,512]{4,3,1,0,2:T(8,128)(2,1)}, u32[]{:S(2)}, u32[]{:S(2)}) async-start(bf16[4,2,32,16,512]{4,3,1,0,2:T(8,128)(2,1)} %copy.12), calls=%async_computation | async-start | bytes 8388608 | tf_op jit(solution)/shard_map/all_to_all | solution.py:564
  219.2 0.6 reshape.12.table
  219.8 24.6 %rows.1 = bf16[16,2,2,128,512]{4,3,2,1,0:T(8,128)(2,1)} custom-call(s32[1]{0:T(128)} %bitcast.tile, s32[256]{0:T(256)} %reshape.12.table, bf16[4,8,2,2,128,512]{5,4,3,2,1,0:T(8,128)(2,1)} %get-tuple-element.11.rows_of.cols_of.refs_0_, bf16[4,8,2,2,128,512]{5,4,3,2,1,0:T(8,128)(2,1)} %get-tuple-element.11.rows_of.cols_of.refs_0_, bf16[16,128,512]{2,1,0:T(8,128)(2,1)} %coup.1), custom_call_target="tpu_custom_call" | custom-call | tf_op jit(solution)/shard_map/rows/pallas_call | solution.py:466
  244.4 33.1 %all-to-all-done = bf16[4,2,32,16,512]{4,3,1,0,2:T(8,128)(2,1)} async-done(((bf16[4,2,32,16,512]{4,3,1,0,2:T(8,128)(2,1)}), bf16[4,2,32,16,512]{4,3,1,0,2:T(8,128)(2,1)}, u32[]{:S(2)}, u32[]{:S(2)}) %all-to-all-start) | async-done | bytes 4194336 | tf_op jit(solution)/shard_map/all_to_all | solution.py:564
  277.5 3.1 %convert_reduce_fusion = f32[4,2,16,512]{3,2,1,0:T(8,128)S(1)} fusion(bf16[4,2,32,16,512]{4,3,1,0,2:T(8,128)(2,1)} %all-to-all-done), kind=kLoop, calls=%fused_computation | loop fusion | flops 4128768 | bytes 4456448 | tf_op jit(solution)/shard_map/reduce_sum | solution.py:568
  280.7 0.9 copy.14
  (1 shorter events, 0.0 us)
Async XLA Ops:
  210.9 66.7 %all-to-all-start = ((bf16[4,2,32,16,512]{4,3,1,0,2:T(8,128)(2,1)}), bf16[4,2,32,16,512]{4,3,1,0,2:T(8,128)(2,1)}, u32[]{:S(2)}, u32[]{:S(2)}) async-start(bf16[4,2,32,16,512]{4,3,1,0,2:T(8,128)(2,1)} %copy.12), calls=%async_computation | async-start | bytes 8388608 | tf_op jit(solution)/shard_map/all_to_all | solution.py:564

commit v6 on v5

--- a/solution.py
+++ b/solution.py
@@ -419,11 +419,72 @@
     )(table, src, coup, coup_t)
 
 
-def rows_kernel(tile, table, rows_of, cols_of, coup, out, source):
+def finish_kernel(
+    inverse, table, green, gamma, us, vs, rows_of, cols_of, coup, out, density,
+    source, part, came, send, recv,
+):
+    energy, mom = lax.axis_index("energy"), lax.axis_index("mom")
+    owners = lax.axis_size("energy")
+    count = part.shape[0]
     targets, _, _, height, norb = out.shape
-    group = pl.program_id(1) * targets
-
-    @pl.when(pl.program_id(1) == 0)
+    index = pl.program_id(0)
+
+    @pl.when(index == 0)
+    def _():
+        barrier = pltpu.get_barrier_semaphore()
+
+        def greet(n, carry):
+            pl.semaphore_signal(
+                barrier,
+                inc=1,
+                device_id=((energy + n) % owners, mom),
+                device_id_type=pl.DeviceIdType.MESH,
+            )
+            return carry
+
+        lax.fori_loop(1, owners, greet, 0)
+        pl.semaphore_wait(barrier, owners - 1)
+
+    @pl.when(index < count)
+    def _():
+        d_re = d_im = None
+        for e in range(green.shape[1]):
+            g_re, g_im = green[0, e, 0], green[0, e, 1]
+            gam = gamma[0, e]
+            wide_re, wide_im = g_re.astype(jnp.float32), g_im.astype(jnp.float32)
+            less = (wide_re - wide_im).astype(jnp.bfloat16)
+            more = (wide_re + wide_im).astype(jnp.bfloat16)
+            u, v = us[0, e], vs[0, e]
+            m_re = dot_nn(less, u) + dot_nt(more, v) + scale(g_re, gam).astype(jnp.float32)
+            m_im = dot_nn(more, u) - dot_nt(less, v) + scale(g_im, gam).astype(jnp.float32)
+            m_re, m_im = m_re.astype(jnp.bfloat16), m_im.astype(jnp.bfloat16)
+            one = dot_nt(m_re, g_re) + dot_nt(m_im, g_im)
+            two = dot_nt(m_im, g_re) - dot_nt(m_re, g_im)
+            d_re = one if d_re is None else d_re + one
+            d_im = two if d_im is None else d_im + two
+        shape = (owners, norb // owners, norb)
+        part[index, :, 0] = (d_re * inverse).astype(jnp.bfloat16).reshape(shape)
+        part[index, :, 1] = (d_im * inverse).astype(jnp.bfloat16).reshape(shape)
+        came[index, energy] = part[index, energy]
+
+        def post(n, carry):
+            peer = (energy + n) % owners
+            pltpu.make_async_remote_copy(
+                src_ref=part.at[index, peer],
+                dst_ref=came.at[index, energy],
+                send_sem=send.at[index],
+                recv_sem=recv.at[index],
+                device_id=(peer, mom),
+                device_id_type=pl.DeviceIdType.MESH,
+            ).start()
+            return carry
+
+        lax.fori_loop(1, owners, post, 0)
+
+    place = index - count
+    group = place % 4 * targets
+
+    @pl.when(jnp.logical_and(index >= count, place % 4 == 0))
     def _():
         turn = identity(height)
         for d in range(16):
@@ -443,91 +504,101 @@
     def store(t, n, at, value):
         out[t, 0, n, at[0], at[1]] = value.astype(jnp.bfloat16)
 
-    def slab(i, carry):
-        at = (
-            pl.ds(pl.multiple_of(i // 2 * 16, 16), 16),
-            pl.ds(pl.multiple_of(i % 2 * (norb // 2), norb // 2), norb // 2),
-        )
-        add_products(targets, 2, picks, donor, coup, at, store)
-        return carry
-
-    lax.fori_loop(0, height // 16 * 2, slab, 0)
-
-
-def row_sums(tile, table, src, coupling, targets):
+    @pl.when(index >= count)
+    def _():
+        def slab(i, carry):
+            at = (
+                pl.ds(pl.multiple_of(i // 2 * 16, 16), 16),
+                pl.ds(pl.multiple_of(i % 2 * (norb // 2), norb // 2), norb // 2),
+            )
+            add_products(targets, 2, picks, donor, coup, at, store)
+            return carry
+
+        lax.fori_loop(0, height // 16 * 2, slab, 0)
+
+    @pl.when(index == pl.num_programs(0) - 1)
+    def _():
+        for k in range(count):
+            every = pltpu.make_async_remote_copy(
+                src_ref=part.at[k, pl.ds(0, owners - 1)],
+                dst_ref=came.at[k, pl.ds(0, owners - 1)],
+                send_sem=send.at[k],
+                recv_sem=recv.at[k],
+                device_id=((energy + 1) % owners, mom),
+                device_id_type=pl.DeviceIdType.MESH,
+            )
+            every.wait_recv()
+            every.wait_send()
+
+            def add(n, total):
+                return total + came[k, n].astype(jnp.float32)
+
+            total = lax.fori_loop(1, owners, add, came[k, 0].astype(jnp.float32))
+            for c in range(2):
+                density[:, k, c, :] = total[c]
+
+
+def finished(table, green, gamma, us, vs, src, coupling, owners, targets):
     chunks, _, half, energies, rows, norb = src.shape
     points, height, _ = coupling.shape
-    row_block = pl.BlockSpec(
-        (1, 8, half, 1, rows, norb), lambda e, g, t, q: (t[0], 0, 0, e, 0, 0)
-    )
-    col_block = pl.BlockSpec(
-        (chunks, 8, half, 1, rows, height), lambda e, g, t, q: (0, 0, 0, e, 0, t[0])
-    )
+    count = green.shape[0]
+    own_rows = norb // owners
+    groups = points // targets
+
+    def of_k(i):
+        return jnp.minimum(i, count - 1)
+
+    def of_e(i):
+        return jnp.maximum(i - count, 0) // groups
+
+    def of_g(i):
+        return jnp.maximum(i - count, 0) % groups
+
+    part = pl.BlockSpec((1, energies, norb, norb), lambda i: (of_k(i), 0, 0, 0))
     return pl.pallas_call(
-        rows_kernel,
-        grid_spec=pltpu.PrefetchScalarGridSpec(
-            num_scalar_prefetch=2,
-            grid=(energies, points // targets),
-            in_specs=[
-                row_block,
-                col_block,
-                pl.BlockSpec((points, height, norb), lambda e, g, t, q: (0, 0, 0)),
-            ],
-            out_specs=pl.BlockSpec(
-                (targets, 1, 2, height, norb), lambda e, g, t, q: (g, e, 0, 0, 0)
-            ),
-            scratch_shapes=[pltpu.VMEM((16, 2, height, norb), jnp.bfloat16)],
-        ),
-        out_shape=jax.ShapeDtypeStruct((points, energies, 2, height, norb), jnp.bfloat16),
-        compiler_params=pltpu.CompilerParams(vmem_limit_bytes=60 * MIB),
-        name="rows",
-    )(tile, table, src, src, coupling)
-
-
-def density_kernel(inverse, green, gamma, us, vs, out):
-    d_re = d_im = None
-    for e in range(green.shape[1]):
-        g_re, g_im = green[0, e, 0], green[0, e, 1]
-        gam = gamma[0, e]
-        wide_re, wide_im = g_re.astype(jnp.float32), g_im.astype(jnp.float32)
-        less = (wide_re - wide_im).astype(jnp.bfloat16)
-        more = (wide_re + wide_im).astype(jnp.bfloat16)
-        u, v = us[0, e], vs[0, e]
-        m_re = dot_nn(less, u) + dot_nt(more, v) + scale(g_re, gam).astype(jnp.float32)
-        m_im = dot_nn(more, u) - dot_nt(less, v) + scale(g_im, gam).astype(jnp.float32)
-        m_re, m_im = m_re.astype(jnp.bfloat16), m_im.astype(jnp.bfloat16)
-        one = dot_nt(m_re, g_re) + dot_nt(m_im, g_im)
-        two = dot_nt(m_im, g_re) - dot_nt(m_re, g_im)
-        d_re = one if d_re is None else d_re + one
-        d_im = two if d_im is None else d_im + two
-    shape = out.shape[2:]
-    out[0, 0] = (d_re * inverse).astype(jnp.bfloat16).reshape(shape)
-    out[0, 1] = (d_im * inverse).astype(jnp.bfloat16).reshape(shape)
-
-
-def partial_density(green, gamma, us, vs, inverse, owners):
-    count, energies, _, norb, _ = green.shape
-    rows = norb // owners
-    part = pl.BlockSpec((1, energies, norb, norb), lambda k: (k, 0, 0, 0))
-    return pl.pallas_call(
-        functools.partial(density_kernel, inverse),
-        grid=(count,),
+        functools.partial(finish_kernel, 1.0 / (energies * owners)),
+        grid=(count + energies * groups,),
         in_specs=[
-            pl.BlockSpec((1, energies, 2, norb, norb), lambda k: (k, 0, 0, 0, 0)),
-            pl.BlockSpec((1, energies, 1, norb), lambda k: (k, 0, 0, 0)),
+            pl.BlockSpec(memory_space=pltpu.SMEM),
+            pl.BlockSpec((1, energies, 2, norb, norb), lambda i: (of_k(i), 0, 0, 0, 0)),
+            pl.BlockSpec((1, energies, 1, norb), lambda i: (of_k(i), 0, 0, 0)),
             part,
             part,
+            pl.BlockSpec(
+                (1, 8, half, 1, rows, norb),
+                lambda i: (lax.axis_index("mom"), 0, 0, of_e(i), 0, 0),
+            ),
+            pl.BlockSpec(
+                (chunks, 8, half, 1, rows, height),
+                lambda i: (0, 0, 0, of_e(i), 0, lax.axis_index("mom")),
+            ),
+            pl.BlockSpec((points, height, norb), lambda i: (0, 0, 0)),
         ],
-        out_specs=pl.BlockSpec((1, 2, owners, rows, norb), lambda k: (k, 0, 0, 0, 0)),
-        out_shape=jax.ShapeDtypeStruct((count, 2, owners, rows, norb), jnp.bfloat16),
-        compiler_params=pltpu.CompilerParams(vmem_limit_bytes=60 * MIB),
-        name="density",
-    )(green, gamma, us, vs)
+        out_specs=[
+            pl.BlockSpec((targets, 1, 2, height, norb), lambda i: (of_g(i), of_e(i), 0, 0, 0)),
+            pl.BlockSpec((own_rows, count, 2, norb), lambda i: (0, 0, 0, 0)),
+        ],
+        out_shape=[
+            jax.ShapeDtypeStruct((points, energies, 2, height, norb), jnp.bfloat16),
+            jax.ShapeDtypeStruct((own_rows, count, 2, norb), jnp.float32),
+        ],
+        scratch_shapes=[
+            pltpu.VMEM((16, 2, height, norb), jnp.bfloat16),
+            pltpu.VMEM((count, owners, 2, own_rows, norb), jnp.bfloat16),
+            pltpu.VMEM((count, owners, 2, own_rows, norb), jnp.bfloat16),
+            pltpu.SemaphoreType.DMA((count,)),
+            pltpu.SemaphoreType.DMA((count,)),
+        ],
+        compiler_params=pltpu.CompilerParams(
+            collective_id=1, has_side_effects=True, vmem_limit_bytes=60 * MIB
+        ),
+        name="finish",
+    )(table, green, gamma, us, vs, src, src, coupling)
 
 
 def on_device(green, broadening, coupling, shift_steps, mode_weight, occupation, momentum_map):
     n_energy, n_mom = lax.axis_size("energy"), lax.axis_size("mom")
-    local_k, local_e = green.shape[:2]
+    local_k = green.shape[0]
     half = local_k // 2
     points = momentum_map.shape[1]
     energy, mom = lax.axis_index("energy"), lax.axis_index("mom")
@@ -560,13 +631,9 @@
     table_home = lax.dynamic_slice_in_dim(table, mom * local_k, local_k, 0).reshape(-1)
 
     us, vs = home_sums(table_home, src, coup, coup_t, local_k)
-    part = partial_density(green, gamma, us, vs, 1.0 / (local_e * n_energy), n_energy)
-    parts = lax.all_to_all(part, "energy", split_axis=2, concat_axis=2, tiled=True)
-    self_energy = row_sums(
-        mom.astype(jnp.int32)[None], table.reshape(-1), src, coupling, local_k
+    return tuple(
+        finished(table.reshape(-1), green, gamma, us, vs, src, coupling, n_energy, local_k)
     )
-    density = jnp.transpose(jnp.sum(parts.astype(jnp.float32), axis=2), (2, 0, 1, 3))
-    return (self_energy, density)
 
 
 def solution(mesh):

time: 287 us -> 262 us (0.913); the launches traced: 282 us -> 262 us
  waiting for transfers between devices: 33.1 us -> 0 us
  Pallas kernels: 223 us -> 245 us
  starting transfers between devices: 8.32 us -> 0 us
  other arithmetic: 5.91 us -> 2.82 us
    all_to_all x1 -> x0, waiting for transfers between devices: 33.1 us -> none  [on_device(): lax.all_to_all(part, 'energy', split_axis=2, concat_axis=2, tiled=True)]
    pallas_call x2 -> x1, Pallas kernels: 46.3 us -> 68.2 us  [finished(): pl.pallas_call(functools.partial(finish_kernel, 1.0 / (energies * owners)...]
    all_to_all x1 -> x0, starting transfers between devices: 8.32 us -> none  [on_device(): lax.all_to_all(part, 'energy', split_axis=2, concat_axis=2, tiled=True)]
    unnamed x1 -> x4, local copies, waits for them, and re-layouts: 0.91 us -> 8.52 us
    pallas_call x1 -> x0, local copies, waits for them, and re-layouts: 4.76 us -> none  [partial_density(): pl.pallas_call(functools.partial(density_kernel, inverse), grid=(count,),...]
    reduce_sum x1 -> x0, other arithmetic: 3.15 us -> none  [on_device(): jnp.sum(parts.astype(jnp.float32), axis=2)]
  transfers between devices with their start and end apart: 1 -> 0, of which waited for: 1 -> 0; matrix products, arithmetic and copies ran while one was open for 0% -> 0% of each run, Pallas kernels for 9% -> 0%
where the time goes in v6:
time: 262 us
  Pallas kernels  245 us (94%)
  local copies, waits for them, and re-layouts  11.1 us (4%)
  between operations  3.19 us (1%)
  other arithmetic  2.82 us (1%)
    pallas_call x1, Pallas kernels, exchanged(): pl.pallas_call(exchange_kernel, in_specs=[pl.BlockSpec(memory_space=pltpu...  145 us
    pallas_call x1, Pallas kernels, finished(): pl.pallas_call(functools.partial(finish_kernel, 1.0 / (energies * owners)...  68.2 us
    pallas_call x1, Pallas kernels, home_sums(): pl.pallas_call(home_kernel, grid_spec=pltpu.PrefetchScalarGridSpec(num_sc...  20.4 us
    pallas_call x1, Pallas kernels, packed_lesser(): pl.pallas_call(lesser_kernel, grid_spec=pltpu.PrefetchScalarGridSpec(num_...  10.8 us
    unnamed x4, local copies, waits for them, and re-layouts  8.52 us

profile of v6, /device:TPU:0, one launch (start us, length us, event | category | flops | bytes accessed | tf_op | source)
XLA Modules:
  0.0 261.8 jit_solution(2174138174435349138)
XLA Ops:
  0.7 0.1 stack.82
  0.8 1.3 fusion
  4.6 0.7 pad_maximum_fusion.weights
  5.3 0.8 select_reduce_fusion
  6.1 0.6 reshape.12.table
  6.7 0.6 reshape.13.table
  7.3 1.3 broadcast_in_dim.30.gamma
  8.6 10.8 %lesser.1 = (bf16[4,2,2,128,512]{4,3,2,1,0:T(8,128)(2,1)}, bf16[4,2,2,128,512]{4,3,2,1,0:T(8,128)(2,1)}) custom-call(s32[1]{0:T(128)} %bitcast.20.place, bf16[4,2,2,512,512]{4,3,2,1,0:T(8,128)(2,1)} %green.3, f32[4,2,1,512]{3,2,1,0:T(1,128)} %broadcast_in_dim.30.gamma), custom_call_target="tpu_custom_call" | custom-call | flops 4294967296 | bytes 12582912 | tf_op jit(solution)/shard_map/lesser/pallas_call | solution.py:62
  19.4 145.2 %exchange.1 = (bf16[4,8,2,2,128,512]{5,4,3,2,1,0:T(8,128)(2,1)}, bf16[16,512,512]{2,1,0:T(8,128)(2,1)}, bf16[16,512,512]{2,1,0:T(8,128)(2,1)}) custom-call(f32[4]{0:T(128)} %pad_maximum_fusion.weights, bf16[4,2,2,128,512]{4,3,2,1,0:T(8,128)(2,1)} %get-tuple-element.9.sent, bf16[4,2,2,128,512]{4,3,2,1,0:T(8,128)(2,1)} %get-tuple-element.10.own, ...), custom_call_target="tpu_custom_call" | custom-call | tf_op jit(solution)/shard_map/exchange/pallas_call | solution.py:324
  164.6 20.4 %home.1 = (bf16[4,2,512,512]{3,2,1,0:T(8,128)(2,1)}, bf16[4,2,512,512]{3,2,1,0:T(8,128)(2,1)}) custom-call(s32[64]{0:T(128)} %reshape.13.table, bf16[4,8,2,2,128,512]{5,4,3,2,1,0:T(8,128)(2,1)} %get-tuple-element.11.refs_0_.rows_of.cols_of, bf16[16,512,512]{2,1,0:T(8,128)(2,1)} %get-tuple-element.12.refs_1_, bf16[16,512,512]{2,1,0:T(8,128)(2,1)} %get-tuple-element.13.refs_2_), custom_call_target="tpu_custom_call" | custom-call | tf_op jit(solution)/shard_map/home/pallas_call | solution.py:408
  185.0 68.2 %finish.1 = (bf16[16,2,2,128,512]{4,3,2,1,0:T(8,128)(2,1)}, f32[16,4,2,512]{3,2,1,0:T(2,128)}) custom-call(s32[256]{0:T(256)} %reshape.12.table, bf16[4,2,2,512,512]{4,3,2,1,0:T(8,128)(2,1)} %green.3, f32[4,2,1,512]{3,2,1,0:T(1,128)} %broadcast_in_dim.30.gamma, bf16[4,2,512,512]{3,2,1,0:T(8,128)(2,1)} %get-tuple-element.14.us, ...), custom_call_target="tpu_custom_call" | custom-call | tf_op jit(solution)/shard_map/finish/pallas_call | solution.py:558
  253.2 0.0 copy-start
  253.2 7.8 %copy.11 = bf16[16,2,2,128,512]{4,3,2,1,0:T(8,128)(2,1)} copy(bf16[16,2,2,128,512]{4,3,2,1,0:T(8,128)(2,1)} %get-tuple-element.22) | data formatting | bytes 16777216
  261.0 0.0 copy-done
  261.1 0.7 copy.12
  (1 shorter events, 0.0 us)
Async XLA Ops:
  253.2 7.8 %copy-start = (f32[16,4,2,512]{3,2,1,0:T(2,128)S(1)}, f32[16,4,2,512]{3,2,1,0:T(2,128)}, u32[]{:S(2)}) copy-start(f32[16,4,2,512]{3,2,1,0:T(2,128)} %get-tuple-element.23) | copy-start | bytes 786436

commit v7 on v6

--- a/solution.py
+++ b/solution.py
@@ -26,7 +26,9 @@
 def lesser_kernel(place, green, gamma, *outs):
     norb = green.shape[-1]
     rows = outs[0].shape[3]
-    gam = gamma[0, 0]
+    half = gamma.shape[0] // 2
+    step = pl.program_id(0)
+    gam = gamma[(place[0] + 1 + step // half) % 2 * half + step % half, pl.ds(pl.program_id(1), 1), :]
     g_re, g_im = green[0, 0, 0], green[0, 0, 1]
     wide_re = g_re.astype(jnp.float32)
     wide_im = g_im.astype(jnp.float32)
@@ -66,7 +68,7 @@
             grid=(2 * half, energies),
             in_specs=[
                 pl.BlockSpec((1, 1, 2, norb, norb), lambda k, e, p: (which(k, p), e, 0, 0, 0)),
-                pl.BlockSpec((1, 1, 1, norb), lambda k, e, p: (which(k, p), e, 0, 0)),
+                pl.BlockSpec(gamma.shape, lambda k, e, p: (0, 0, 0)),
             ],
             out_specs=[block_of(0), block_of(1)],
         ),
@@ -89,7 +91,7 @@
 
 
 def exchange_kernel(
-    weights, sent, own, coupling, src, coup, coup_t,
+    shift_steps, mode_weight, occupation, sent, own, coupling, src, coup, coup_t,
     got, own_halo, got_halo, mine, other, tiles, turned, send, recv, local,
 ):
     energy, mom = lax.axis_index("energy"), lax.axis_index("mom")
@@ -114,6 +116,16 @@
     has_got_to = jnp.logical_or(
         jnp.logical_and(first, high), jnp.logical_and(jnp.logical_not(first), low)
     )
+
+    weights = [0.0] * 4
+    for m in range(shift_steps.shape[0]):
+        two = shift_steps[m].astype(jnp.float32) - 1.0
+        up = 0.5 * mode_weight[m] * (occupation[m] + 1.0)
+        down = 0.5 * mode_weight[m] * occupation[m]
+        weights[0] += (1.0 - two) * up
+        weights[1] += two * up
+        weights[2] += (1.0 - two) * down
+        weights[3] += two * down
 
     def remote(kind, c, source, target, device):
         return pltpu.make_async_remote_copy(
@@ -314,7 +326,7 @@
             copy.wait()
 
 
-def exchanged(weights, sent, own, coupling):
+def exchanged(shift_steps, mode_weight, occupation, sent, own, coupling):
     chunks, half, energies, rows, norb = sent.shape
     points, height, _ = coupling.shape
     whole = jax.ShapeDtypeStruct((points, norb, norb), jnp.bfloat16)
@@ -323,7 +335,7 @@
     part = pltpu.VMEM(sent.shape, jnp.bfloat16)
     return pl.pallas_call(
         exchange_kernel,
-        in_specs=[pl.BlockSpec(memory_space=pltpu.SMEM), vmem, vmem, hbm],
+        in_specs=[pl.BlockSpec(memory_space=pltpu.SMEM)] * 3 + [vmem, vmem, hbm],
         out_specs=[hbm] * 3,
         out_shape=[
             jax.ShapeDtypeStruct((chunks, 8, half, energies, rows, norb), jnp.bfloat16),
@@ -342,7 +354,7 @@
             collective_id=0, has_side_effects=True, vmem_limit_bytes=60 * MIB
         ),
         name="exchange",
-    )(weights, sent, own, coupling)
+    )(shift_steps, mode_weight, occupation, sent, own, coupling)
 
 
 def add_products(targets, streams, picks, donor, factor, at, store):
@@ -369,9 +381,10 @@
 def home_kernel(table, *refs):
     sources, coup, coup_t, out, out_t = refs
     targets, _, height, norb = out.shape
+    home = lax.axis_index("mom") * targets
 
     def picks(t, d):
-        return table[t * 16 + d]
+        return table[home + t, d]
 
     def donor(d, n, at):
         return sources[0, d // 2, d % 2, n, at[0], at[1]]
@@ -425,9 +438,11 @@
 ):
     energy, mom = lax.axis_index("energy"), lax.axis_index("mom")
     owners = lax.axis_size("energy")
-    count = part.shape[0]
+    packs = part.shape[0]
+    count = packs * 2
     targets, _, _, height, norb = out.shape
     index = pl.program_id(0)
+    pack = jnp.minimum(index, count - 1) // 2
 
     @pl.when(index == 0)
     def _():
@@ -450,7 +465,7 @@
         d_re = d_im = None
         for e in range(green.shape[1]):
             g_re, g_im = green[0, e, 0], green[0, e, 1]
-            gam = gamma[0, e]
+            gam = gamma[index, e : e + 1, :]
             wide_re, wide_im = g_re.astype(jnp.float32), g_im.astype(jnp.float32)
             less = (wide_re - wide_im).astype(jnp.bfloat16)
             more = (wide_re + wide_im).astype(jnp.bfloat16)
@@ -463,17 +478,20 @@
             d_re = one if d_re is None else d_re + one
             d_im = two if d_im is None else d_im + two
         shape = (owners, norb // owners, norb)
-        part[index, :, 0] = (d_re * inverse).astype(jnp.bfloat16).reshape(shape)
-        part[index, :, 1] = (d_im * inverse).astype(jnp.bfloat16).reshape(shape)
-        came[index, energy] = part[index, energy]
+        part[pack, :, index % 2, 0] = (d_re * inverse).astype(jnp.bfloat16).reshape(shape)
+        part[pack, :, index % 2, 1] = (d_im * inverse).astype(jnp.bfloat16).reshape(shape)
+
+    @pl.when(jnp.logical_and(index < count, index % 2 == 1))
+    def _():
+        came[pack, energy] = part[pack, energy]
 
         def post(n, carry):
             peer = (energy + n) % owners
             pltpu.make_async_remote_copy(
-                src_ref=part.at[index, peer],
-                dst_ref=came.at[index, energy],
-                send_sem=send.at[index],
-                recv_sem=recv.at[index],
+                src_ref=part.at[pack, peer],
+                dst_ref=came.at[pack, energy],
+                send_sem=send.at[pack],
+                recv_sem=recv.at[pack],
                 device_id=(peer, mom),
                 device_id_type=pl.DeviceIdType.MESH,
             ).start()
@@ -496,7 +514,7 @@
                 source[d, 1, :, span] = (straight - turned).astype(jnp.bfloat16)
 
     def picks(t, d):
-        return table[(group + t) * 16 + d]
+        return table[group + t, d]
 
     def donor(d, n, at):
         return source[d, n, at[0], at[1]]
@@ -518,7 +536,7 @@
 
     @pl.when(index == pl.num_programs(0) - 1)
     def _():
-        for k in range(count):
+        for k in range(packs):
             every = pltpu.make_async_remote_copy(
                 src_ref=part.at[k, pl.ds(0, owners - 1)],
                 dst_ref=came.at[k, pl.ds(0, owners - 1)],
@@ -534,8 +552,9 @@
                 return total + came[k, n].astype(jnp.float32)
 
             total = lax.fori_loop(1, owners, add, came[k, 0].astype(jnp.float32))
-            for c in range(2):
-                density[:, k, c, :] = total[c]
+            for kk in range(2):
+                for c in range(2):
+                    density[:, 2 * k + kk, c, :] = total[kk, c]
 
 
 def finished(table, green, gamma, us, vs, src, coupling, owners, targets):
@@ -561,7 +580,7 @@
         in_specs=[
             pl.BlockSpec(memory_space=pltpu.SMEM),
             pl.BlockSpec((1, energies, 2, norb, norb), lambda i: (of_k(i), 0, 0, 0, 0)),
-            pl.BlockSpec((1, energies, 1, norb), lambda i: (of_k(i), 0, 0, 0)),
+            pl.BlockSpec(gamma.shape, lambda i: (0, 0, 0)),
             part,
             part,
             pl.BlockSpec(
@@ -584,10 +603,10 @@
         ],
         scratch_shapes=[
             pltpu.VMEM((16, 2, height, norb), jnp.bfloat16),
-            pltpu.VMEM((count, owners, 2, own_rows, norb), jnp.bfloat16),
-            pltpu.VMEM((count, owners, 2, own_rows, norb), jnp.bfloat16),
-            pltpu.SemaphoreType.DMA((count,)),
-            pltpu.SemaphoreType.DMA((count,)),
+            pltpu.VMEM((count // 2, owners, 2, 2, own_rows, norb), jnp.bfloat16),
+            pltpu.VMEM((count // 2, owners, 2, 2, own_rows, norb), jnp.bfloat16),
+            pltpu.SemaphoreType.DMA((count // 2,)),
+            pltpu.SemaphoreType.DMA((count // 2,)),
         ],
         compiler_params=pltpu.CompilerParams(
             collective_id=1, has_side_effects=True, vmem_limit_bytes=60 * MIB
@@ -604,16 +623,10 @@
     energy, mom = lax.axis_index("energy"), lax.axis_index("mom")
     x_lo = energy % 2
 
-    def weight_of(step, factor):
-        return 0.5 * jnp.sum(jnp.where(shift_steps == step, mode_weight * factor, 0.0))
-
-    weights = jnp.stack(
-        [weight_of(s, occupation + 1.0) for s in (1, 2)] + [weight_of(s, occupation) for s in (1, 2)]
-    ).astype(jnp.float32)
-
-    gamma = broadening[:, :, None, :]
-    sent, own = packed_lesser(x_lo.astype(jnp.int32)[None], green, gamma, n_mom)
-    src, coup, coup_t = exchanged(weights, sent, own, coupling)
+    sent, own = packed_lesser(x_lo.astype(jnp.int32)[None], green, broadening, n_mom)
+    src, coup, coup_t = exchanged(
+        shift_steps, mode_weight, occupation, sent, own, coupling
+    )
 
     moves = [(0, 0), (1, 0), (1, 2), (0, 2)]
     moves = moves + [(lo, mo ^ 1) for lo, mo in moves]
@@ -628,11 +641,9 @@
         ),
         axis=1,
     ).astype(jnp.int32)
-    table_home = lax.dynamic_slice_in_dim(table, mom * local_k, local_k, 0).reshape(-1)
-
-    us, vs = home_sums(table_home, src, coup, coup_t, local_k)
+    us, vs = home_sums(table, src, coup, coup_t, local_k)
     return tuple(
-        finished(table.reshape(-1), green, gamma, us, vs, src, coupling, n_energy, local_k)
+        finished(table, green, broadening, us, vs, src, coupling, n_energy, local_k)
     )
 
 

time: 262 us -> 270 us (1.031)
  Pallas kernels: 245 us -> 258 us
    pallas_call x1, Pallas kernels: 68.2 us -> 80.9 us  [finished(): pl.pallas_call(functools.partial(finish_kernel, 1.0 / (energies * owners)...]
where the time goes in v7:
time: 270 us; the launch traced here: 269 us
  Pallas kernels  258 us (96%)
  local copies, waits for them, and re-layouts  8.61 us (3%)
    pallas_call x1, Pallas kernels, exchanged(): pl.pallas_call(exchange_kernel, in_specs=[pl.BlockSpec(memory_space=pltpu...  145 us
    pallas_call x1, Pallas kernels, finished(): pl.pallas_call(functools.partial(finish_kernel, 1.0 / (energies * owners)...  80.9 us
    pallas_call x1, Pallas kernels, home_sums(): pl.pallas_call(home_kernel, grid_spec=pltpu.PrefetchScalarGridSpec(num_sc...  21.1 us
    pallas_call x1, Pallas kernels, packed_lesser(): pl.pallas_call(lesser_kernel, grid_spec=pltpu.PrefetchScalarGridSpec(num_...  10.7 us
    unnamed x4, local copies, waits for them, and re-layouts  8.52 us

profile of v7, /device:TPU:0, one launch (start us, length us, event | category | flops | bytes accessed | tf_op | source)
XLA Modules:
  0.0 268.7 jit_solution(15363516726306199402)
XLA Ops:
  0.7 0.1 stack.67
  0.8 1.4 select_reduce_fusion.table
  2.2 10.7 %lesser.1 = (bf16[4,2,2,128,512]{4,3,2,1,0:T(8,128)(2,1)}, bf16[4,2,2,128,512]{4,3,2,1,0:T(8,128)(2,1)}) custom-call(s32[1]{0:T(128)} %bitcast.16.place, bf16[4,2,2,512,512]{4,3,2,1,0:T(8,128)(2,1)} %green.3, f32[4,2,512]{2,1,0:T(2,128)} %gamma.3), custom_call_target="tpu_custom_call" | custom-call | flops 4294967296 | bytes 12582912 | tf_op jit(solution)/shard_map/lesser/pallas_call | solution.py:64
  12.9 145.3 %exchange.1 = (bf16[4,8,2,2,128,512]{5,4,3,2,1,0:T(8,128)(2,1)}, bf16[16,512,512]{2,1,0:T(8,128)(2,1)}, bf16[16,512,512]{2,1,0:T(8,128)(2,1)}) custom-call(s32[4]{0:T(128)} %shift_steps.1, f32[4]{0:T(128)} %mode_weight.1, f32[4]{0:T(128)} %occupation.1, bf16[4,2,2,128,512]{4,3,2,1,0:T(8,128)(2,1)} %get-tuple-element.9.sent, ...), custom_call_target="tpu_custom_call" | custom-call | tf_op jit(solution)/shard_map/exchange/pallas_call | solution.py:336
  158.2 21.1 %home.1 = (bf16[4,2,512,512]{3,2,1,0:T(8,128)(2,1)}, bf16[4,2,512,512]{3,2,1,0:T(8,128)(2,1)}) custom-call(s32[16,16]{1,0:T(8,128)} %select_reduce_fusion.table, bf16[4,8,2,2,128,512]{5,4,3,2,1,0:T(8,128)(2,1)} %get-tuple-element.11.refs_0_.rows_of.cols_of, bf16[16,512,512]{2,1,0:T(8,128)(2,1)} %get-tuple-element.12.refs_1_, ...), custom_call_target="tpu_custom_call" | custom-call | tf_op jit(solution)/shard_map/home/pallas_call | solution.py:421
  179.2 80.9 %finish.1 = (bf16[16,2,2,128,512]{4,3,2,1,0:T(8,128)(2,1)}, f32[16,4,2,512]{3,2,1,0:T(2,128)}) custom-call(s32[16,16]{1,0:T(8,128)} %select_reduce_fusion.table, bf16[4,2,2,512,512]{4,3,2,1,0:T(8,128)(2,1)} %green.3, f32[4,2,512]{2,1,0:T(2,128)} %gamma.3, bf16[4,2,512,512]{3,2,1,0:T(8,128)(2,1)} %get-tuple-element.14.us, ...), custom_call_target="tpu_custom_call" | custom-call | tf_op jit(solution)/shard_map/finish/pallas_call | solution.py:577
  260.1 0.0 copy-start
  260.1 7.8 %copy.11 = bf16[16,2,2,128,512]{4,3,2,1,0:T(8,128)(2,1)} copy(bf16[16,2,2,128,512]{4,3,2,1,0:T(8,128)(2,1)} %get-tuple-element.18) | data formatting | bytes 16777216
  268.0 0.0 copy-done
  268.0 0.7 copy.12
Async XLA Ops:
  260.1 7.8 %copy-start = (f32[16,4,2,512]{3,2,1,0:T(2,128)S(1)}, f32[16,4,2,512]{3,2,1,0:T(2,128)}, u32[]{:S(2)}) copy-start(f32[16,4,2,512]{3,2,1,0:T(2,128)} %get-tuple-element.19) | copy-start | bytes 786436

commit v8 on v7

--- a/solution.py
+++ b/solution.py
@@ -438,11 +438,9 @@
 ):
     energy, mom = lax.axis_index("energy"), lax.axis_index("mom")
     owners = lax.axis_size("energy")
-    packs = part.shape[0]
-    count = packs * 2
+    count = part.shape[0]
     targets, _, _, height, norb = out.shape
     index = pl.program_id(0)
-    pack = jnp.minimum(index, count - 1) // 2
 
     @pl.when(index == 0)
     def _():
@@ -478,20 +476,17 @@
             d_re = one if d_re is None else d_re + one
             d_im = two if d_im is None else d_im + two
         shape = (owners, norb // owners, norb)
-        part[pack, :, index % 2, 0] = (d_re * inverse).astype(jnp.bfloat16).reshape(shape)
-        part[pack, :, index % 2, 1] = (d_im * inverse).astype(jnp.bfloat16).reshape(shape)
-
-    @pl.when(jnp.logical_and(index < count, index % 2 == 1))
-    def _():
-        came[pack, energy] = part[pack, energy]
+        part[index, :, 0] = (d_re * inverse).astype(jnp.bfloat16).reshape(shape)
+        part[index, :, 1] = (d_im * inverse).astype(jnp.bfloat16).reshape(shape)
+        came[index, energy] = part[index, energy]
 
         def post(n, carry):
-            peer = (energy + n) % owners
+            peer = (energy + n * 13) % owners
             pltpu.make_async_remote_copy(
-                src_ref=part.at[pack, peer],
-                dst_ref=came.at[pack, energy],
-                send_sem=send.at[pack],
-                recv_sem=recv.at[pack],
+                src_ref=part.at[index, peer],
+                dst_ref=came.at[index, energy],
+                send_sem=send.at[index],
+                recv_sem=recv.at[index],
                 device_id=(peer, mom),
                 device_id_type=pl.DeviceIdType.MESH,
             ).start()
@@ -536,7 +531,7 @@
 
     @pl.when(index == pl.num_programs(0) - 1)
     def _():
-        for k in range(packs):
+        for k in range(count):
             every = pltpu.make_async_remote_copy(
                 src_ref=part.at[k, pl.ds(0, owners - 1)],
                 dst_ref=came.at[k, pl.ds(0, owners - 1)],
@@ -552,9 +547,8 @@
                 return total + came[k, n].astype(jnp.float32)
 
             total = lax.fori_loop(1, owners, add, came[k, 0].astype(jnp.float32))
-            for kk in range(2):
-                for c in range(2):
-                    density[:, 2 * k + kk, c, :] = total[kk, c]
+            for c in range(2):
+                density[:, k, c, :] = total[c]
 
 
 def finished(table, green, gamma, us, vs, src, coupling, owners, targets):
@@ -603,10 +597,10 @@
         ],
         scratch_shapes=[
             pltpu.VMEM((16, 2, height, norb), jnp.bfloat16),
-            pltpu.VMEM((count // 2, owners, 2, 2, own_rows, norb), jnp.bfloat16),
-            pltpu.VMEM((count // 2, owners, 2, 2, own_rows, norb), jnp.bfloat16),
-            pltpu.SemaphoreType.DMA((count // 2,)),
-            pltpu.SemaphoreType.DMA((count // 2,)),
+            pltpu.VMEM((count, owners, 2, own_rows, norb), jnp.bfloat16),
+            pltpu.VMEM((count, owners, 2, own_rows, norb), jnp.bfloat16),
+            pltpu.SemaphoreType.DMA((count,)),
+            pltpu.SemaphoreType.DMA((count,)),
         ],
         compiler_params=pltpu.CompilerParams(
             collective_id=1, has_side_effects=True, vmem_limit_bytes=60 * MIB

time: 270 us -> 254 us (0.941)
  Pallas kernels: 258 us -> 243 us
    pallas_call x1, Pallas kernels: 80.9 us -> 66 us  [finished(): pl.pallas_call(functools.partial(finish_kernel, 1.0 / (energies * owners)...]
where the time goes in v8:
time: 254 us
  Pallas kernels  243 us (96%)
  local copies, waits for them, and re-layouts  8.61 us (3%)
    pallas_call x1, Pallas kernels, exchanged(): pl.pallas_call(exchange_kernel, in_specs=[pl.BlockSpec(memory_space=pltpu...  145 us
    pallas_call x1, Pallas kernels, finished(): pl.pallas_call(functools.partial(finish_kernel, 1.0 / (energies * owners)...  66 us
    pallas_call x1, Pallas kernels, home_sums(): pl.pallas_call(home_kernel, grid_spec=pltpu.PrefetchScalarGridSpec(num_sc...  21.1 us
    pallas_call x1, Pallas kernels, packed_lesser(): pl.pallas_call(lesser_kernel, grid_spec=pltpu.PrefetchScalarGridSpec(num_...  10.7 us
    unnamed x4, local copies, waits for them, and re-layouts  8.52 us

profile of v8, /device:TPU:0, one launch (start us, length us, event | category | flops | bytes accessed | tf_op | source)
XLA Modules:
  0.0 253.8 jit_solution(5424981395170639585)
XLA Ops:
  0.7 0.1 stack.67
  0.8 1.4 select_reduce_fusion.table
  2.2 10.7 %lesser.1 = (bf16[4,2,2,128,512]{4,3,2,1,0:T(8,128)(2,1)}, bf16[4,2,2,128,512]{4,3,2,1,0:T(8,128)(2,1)}) custom-call(s32[1]{0:T(128)} %bitcast.16.place, bf16[4,2,2,512,512]{4,3,2,1,0:T(8,128)(2,1)} %green.3, f32[4,2,512]{2,1,0:T(2,128)} %gamma.3), custom_call_target="tpu_custom_call" | custom-call | flops 4294967296 | bytes 12582912 | tf_op jit(solution)/shard_map/lesser/pallas_call | solution.py:64
  12.9 145.3 %exchange.1 = (bf16[4,8,2,2,128,512]{5,4,3,2,1,0:T(8,128)(2,1)}, bf16[16,512,512]{2,1,0:T(8,128)(2,1)}, bf16[16,512,512]{2,1,0:T(8,128)(2,1)}) custom-call(s32[4]{0:T(128)} %shift_steps.1, f32[4]{0:T(128)} %mode_weight.1, f32[4]{0:T(128)} %occupation.1, bf16[4,2,2,128,512]{4,3,2,1,0:T(8,128)(2,1)} %get-tuple-element.9.sent, ...), custom_call_target="tpu_custom_call" | custom-call | tf_op jit(solution)/shard_map/exchange/pallas_call | solution.py:336
  158.2 21.1 %home.1 = (bf16[4,2,512,512]{3,2,1,0:T(8,128)(2,1)}, bf16[4,2,512,512]{3,2,1,0:T(8,128)(2,1)}) custom-call(s32[16,16]{1,0:T(8,128)} %select_reduce_fusion.table, bf16[4,8,2,2,128,512]{5,4,3,2,1,0:T(8,128)(2,1)} %get-tuple-element.11.refs_0_.rows_of.cols_of, bf16[16,512,512]{2,1,0:T(8,128)(2,1)} %get-tuple-element.12.refs_1_, ...), custom_call_target="tpu_custom_call" | custom-call | tf_op jit(solution)/shard_map/home/pallas_call | solution.py:421
  179.2 66.0 %finish.1 = (bf16[16,2,2,128,512]{4,3,2,1,0:T(8,128)(2,1)}, f32[16,4,2,512]{3,2,1,0:T(2,128)}) custom-call(s32[16,16]{1,0:T(8,128)} %select_reduce_fusion.table, bf16[4,2,2,512,512]{4,3,2,1,0:T(8,128)(2,1)} %green.3, f32[4,2,512]{2,1,0:T(2,128)} %gamma.3, bf16[4,2,512,512]{3,2,1,0:T(8,128)(2,1)} %get-tuple-element.14.us, ...), custom_call_target="tpu_custom_call" | custom-call | tf_op jit(solution)/shard_map/finish/pallas_call | solution.py:571
  245.3 0.0 copy-start
  245.3 7.8 %copy.11 = bf16[16,2,2,128,512]{4,3,2,1,0:T(8,128)(2,1)} copy(bf16[16,2,2,128,512]{4,3,2,1,0:T(8,128)(2,1)} %get-tuple-element.18) | data formatting | bytes 16777216
  253.1 0.0 copy-done
  253.1 0.7 copy.12
Async XLA Ops:
  245.3 7.8 %copy-start = (f32[16,4,2,512]{3,2,1,0:T(2,128)S(1)}, f32[16,4,2,512]{3,2,1,0:T(2,128)}, u32[]{:S(2)}) copy-start(f32[16,4,2,512]{3,2,1,0:T(2,128)} %get-tuple-element.19) | copy-start | bytes 786436

commit v9 on v8

--- a/solution.py
+++ b/solution.py
@@ -91,8 +91,8 @@
 
 
 def exchange_kernel(
-    shift_steps, mode_weight, occupation, sent, own, coupling, src, coup, coup_t,
-    got, own_halo, got_halo, mine, other, tiles, turned, send, recv, local,
+    shift_steps, mode_weight, occupation, table, sent, own, coupling, src, us, vs,
+    got, own_halo, got_halo, mine, other, tiles, turned, held, sums, sums_t, send, recv, local,
 ):
     energy, mom = lax.axis_index("energy"), lax.axis_index("mom")
     pairs = lax.axis_size("energy") // 2
@@ -158,21 +158,61 @@
     tile_b = remote(10, 1, coupling, tiles.at[2], ring_b)
     tile_bc = remote(10, 2, tiles.at[2], tiles.at[3], core)
     tile_own = pltpu.make_async_copy(coupling, tiles.at[0], local.at[chunks])
-    placed = [
+    taken = [
+        pltpu.make_async_copy(src.at[c], held.at[c % 2], local.at[chunks + 1 + c])
+        for c in range(chunks)
+    ]
+    summed = [
         (
             pltpu.make_async_copy(
-                tiles.at[s],
-                coup.at[:, pl.ds(pl.multiple_of(place[s] * height, height), height), :],
-                local.at[chunks + 1 + 2 * s],
+                sums.at[c], us.at[:, :, c * rows : (c + 1) * rows, :], local.at[2 * chunks + 1 + c]
             ),
             pltpu.make_async_copy(
-                turned.at[s],
-                coup_t.at[:, :, pl.ds(pl.multiple_of(place[s] * height, height), height)],
-                local.at[chunks + 2 + 2 * s],
+                sums_t.at[c], vs.at[:, :, c * rows : (c + 1) * rows, :], local.at[3 * chunks + 1 + c]
             ),
         )
-        for s in range(4)
+        for c in range(chunks)
     ]
+    targets = us.shape[0]
+    home = mom * targets
+
+    def picks(t, d):
+        return table[home + t, d]
+
+    def convolve(c):
+        low_bit = (mom + c) % 2
+        slot = low_bit + 2 * ((mom // 2 + c // 2) % 2)
+
+        def donor(d, n, at):
+            return held[c % 2, d // 2, d % 2, n, at[0], at[1]]
+
+        def store(t, n, at, value):
+            sums[c, t, n, at[0], at[1]] = value.astype(sums.dtype)
+
+        def store_t(t, n, at, value):
+            sums_t[c, t, n, at[0], at[1]] = value.astype(sums.dtype)
+
+        def straight(i, carry):
+            at = (
+                pl.ds(pl.multiple_of(i // 2 * 16, 16), 16),
+                pl.ds(pl.multiple_of(i % 2 * (norb // 2), norb // 2), norb // 2),
+            )
+            add_products(targets, 2, picks, donor, tiles.at[slot], at, store)
+            return carry
+
+        lax.fori_loop(0, rows // 16 * 2, straight, 0)
+        for s in range(4):
+
+            def across(i, carry, s=s):
+                span = pl.ds(pl.multiple_of(place[s] * height, height), height)
+                at = (pl.ds(pl.multiple_of(i * 32, 32), 32), span)
+                inner = (pl.ds(pl.multiple_of(c * rows + i * 32, 32), 32), slice(None))
+                add_products(targets, 2, picks, donor, turned.at[s], at, store_t, inner)
+                return carry
+
+            lax.fori_loop(0, rows // 32, across, 0)
+        for copy in summed[c]:
+            copy.start()
 
     barrier = pltpu.get_barrier_semaphore()
 
@@ -238,8 +278,6 @@
             return carry
 
         lax.fori_loop(0, points, one, 0)
-        for copy in placed[s]:
-            copy.start()
 
     def shift(c, parts, outs):
         def one(i, carry):
@@ -297,6 +335,12 @@
     tile_b.wait_recv()
     tile_bc.start()
     fold(2)
+    def take(c):
+        for copy in far[c]:
+            copy.wait_recv()
+        stay[c].wait()
+        taken[c].start()
+
     for c in range(chunks):
         for s in (1, 2, 3):
             near[c][s - 1].wait_recv()
@@ -304,12 +348,16 @@
         if c == 0:
             tile_bc.wait_recv()
             fold(3)
+        else:
+            take(c - 1)
+            taken[c - 1].wait()
+            convolve(c - 1)
+    take(chunks - 1)
+    taken[chunks - 1].wait()
+    convolve(chunks - 1)
     for c in range(chunks):
-        for copy in far[c]:
-            copy.wait_recv()
         for copy in [swap[c]] + near[c] + far[c]:
             copy.wait_send()
-        stay[c].wait()
 
         @pl.when(has_own_to)
         def _(copy=to_own[c]):
@@ -321,21 +369,22 @@
 
     for copy in (tile_core, tile_b, tile_bc):
         copy.wait_send()
-    for pair_of in placed:
-        for copy in pair_of:
+    for two in summed:
+        for copy in two:
             copy.wait()
 
 
-def exchanged(shift_steps, mode_weight, occupation, sent, own, coupling):
+def exchanged(shift_steps, mode_weight, occupation, table, sent, own, coupling, targets):
     chunks, half, energies, rows, norb = sent.shape
     points, height, _ = coupling.shape
-    whole = jax.ShapeDtypeStruct((points, norb, norb), jnp.bfloat16)
+    whole = jax.ShapeDtypeStruct((targets, energies, norb, norb), jnp.bfloat16)
+    result = pltpu.VMEM((chunks, targets, energies, rows, norb), jnp.bfloat16)
     vmem = pl.BlockSpec(memory_space=pltpu.VMEM)
     hbm = pl.BlockSpec(memory_space=pl.ANY)
     part = pltpu.VMEM(sent.shape, jnp.bfloat16)
     return pl.pallas_call(
         exchange_kernel,
-        in_specs=[pl.BlockSpec(memory_space=pltpu.SMEM)] * 3 + [vmem, vmem, hbm],
+        in_specs=[pl.BlockSpec(memory_space=pltpu.SMEM)] * 4 + [vmem, vmem, hbm],
         out_specs=[hbm] * 3,
         out_shape=[
             jax.ShapeDtypeStruct((chunks, 8, half, energies, rows, norb), jnp.bfloat16),
@@ -346,24 +395,28 @@
         + [
             pltpu.VMEM((4, points, height, norb), jnp.bfloat16),
             pltpu.VMEM((4, points, norb, height), jnp.bfloat16),
+            pltpu.VMEM((2, 8, half, energies, rows, norb), jnp.bfloat16),
+            result,
+            result,
             pltpu.SemaphoreType.DMA((11, chunks)),
             pltpu.SemaphoreType.DMA((11, chunks)),
-            pltpu.SemaphoreType.DMA((chunks + 9,)),
+            pltpu.SemaphoreType.DMA((4 * chunks + 1,)),
         ],
         compiler_params=pltpu.CompilerParams(
             collective_id=0, has_side_effects=True, vmem_limit_bytes=60 * MIB
         ),
         name="exchange",
-    )(shift_steps, mode_weight, occupation, sent, own, coupling)
-
-
-def add_products(targets, streams, picks, donor, factor, at, store):
+    )(shift_steps, mode_weight, occupation, table, sent, own, coupling)
+
+
+def add_products(targets, streams, picks, donor, factor, at, store, inner=None):
+    inner = at if inner is None else inner
     acc = [[None] * streams for _ in range(targets)]
     kept = {}
     for quad in range(4):
         held = [[donor(4 * quad + d, n, at) for n in range(streams)] for d in range(4)]
         for t in range(targets):
-            c = [factor[picks(t, 4 * quad + d), at[0], at[1]] for d in range(4)]
+            c = [factor[picks(t, 4 * quad + d), inner[0], inner[1]] for d in range(4)]
             for n in range(streams):
                 part = (c[0] * held[0][n] + c[1] * held[1][n]) + (
                     c[2] * held[2][n] + c[3] * held[3][n]
@@ -376,60 +429,6 @@
     for t in range(targets):
         for n in range(streams):
             store(t, n, at, acc[t][n])
-
-
-def home_kernel(table, *refs):
-    sources, coup, coup_t, out, out_t = refs
-    targets, _, height, norb = out.shape
-    home = lax.axis_index("mom") * targets
-
-    def picks(t, d):
-        return table[home + t, d]
-
-    def donor(d, n, at):
-        return sources[0, d // 2, d % 2, n, at[0], at[1]]
-
-    def into(ref):
-        def store(t, n, at, value):
-            ref[t, n, at[0], at[1]] = value.astype(jnp.bfloat16)
-
-        return store
-
-    def slab(i, carry):
-        at = (
-            pl.ds(pl.multiple_of(i // 2 * 16, 16), 16),
-            pl.ds(pl.multiple_of(i % 2 * (norb // 2), norb // 2), norb // 2),
-        )
-        add_products(targets, 2, picks, donor, coup, at, into(out))
-        add_products(targets, 2, picks, donor, coup_t, at, into(out_t))
-        return carry
-
-    lax.fori_loop(0, height // 16 * 2, slab, 0)
-
-
-def home_sums(table, src, coup, coup_t, targets):
-    chunks, _, half, energies, rows, norb = src.shape
-    points = coup.shape[0]
-    height = rows // 2
-    steps = rows // height
-    given = pl.BlockSpec(
-        (1, 8, half, energies, height, norb), lambda i, q: (i // steps, 0, 0, 0, i % steps, 0)
-    )
-    factor = pl.BlockSpec((points, height, norb), lambda i, q: (0, i, 0))
-    result = pl.BlockSpec((targets, energies, height, norb), lambda i, q: (0, 0, i, 0))
-    out = jax.ShapeDtypeStruct((targets, energies, chunks * rows, norb), jnp.bfloat16)
-    return pl.pallas_call(
-        home_kernel,
-        grid_spec=pltpu.PrefetchScalarGridSpec(
-            num_scalar_prefetch=1,
-            grid=(chunks * steps,),
-            in_specs=[given] + [factor] * 2,
-            out_specs=[result] * 2,
-        ),
-        out_shape=[out, out],
-        compiler_params=pltpu.CompilerParams(vmem_limit_bytes=60 * MIB),
-        name="home",
-    )(table, src, coup, coup_t)
 
 
 def finish_kernel(
@@ -618,10 +617,6 @@
     x_lo = energy % 2
 
     sent, own = packed_lesser(x_lo.astype(jnp.int32)[None], green, broadening, n_mom)
-    src, coup, coup_t = exchanged(
-        shift_steps, mode_weight, occupation, sent, own, coupling
-    )
-
     moves = [(0, 0), (1, 0), (1, 2), (0, 2)]
     moves = moves + [(lo, mo ^ 1) for lo, mo in moves]
     donors = jnp.stack(
@@ -635,7 +630,9 @@
         ),
         axis=1,
     ).astype(jnp.int32)
-    us, vs = home_sums(table, src, coup, coup_t, local_k)
+    src, us, vs = exchanged(
+        shift_steps, mode_weight, occupation, table, sent, own, coupling, local_k
+    )
     return tuple(
         finished(table, green, broadening, us, vs, src, coupling, n_energy, local_k)
     )

time: 254 us -> 249 us (0.980)
  Pallas kernels: 243 us -> 238 us
    pallas_call x1 -> x0, Pallas kernels: 21.1 us -> none  [home_sums(): pl.pallas_call(home_kernel, grid_spec=pltpu.PrefetchScalarGridSpec(num_sc...]
    pallas_call x1, Pallas kernels: 145 us -> 162 us  [exchanged(): pl.pallas_call(exchange_kernel, in_specs=[pl.BlockSpec(memory_space=pltpu...]
where the time goes in v9:
time: 249 us; the launch traced here: 248 us
  Pallas kernels  238 us (96%)
  local copies, waits for them, and re-layouts  8.61 us (3%)
    pallas_call x1, Pallas kernels, exchanged(): pl.pallas_call(exchange_kernel, in_specs=[pl.BlockSpec(memory_space=pltpu...  162 us
    pallas_call x1, Pallas kernels, finished(): pl.pallas_call(functools.partial(finish_kernel, 1.0 / (energies * owners)...  64.7 us
    pallas_call x1, Pallas kernels, packed_lesser(): pl.pallas_call(lesser_kernel, grid_spec=pltpu.PrefetchScalarGridSpec(num_...  10.7 us
    unnamed x4, local copies, waits for them, and re-layouts  8.52 us

profile of v9, /device:TPU:0, one launch (start us, length us, event | category | flops | bytes accessed | tf_op | source)
XLA Modules:
  0.0 248.4 jit_solution(9100682286058695287)
XLA Ops:
  0.7 0.1 stack.67
  0.8 1.4 select_reduce_fusion.table
  2.2 10.7 %lesser.1 = (bf16[4,2,2,128,512]{4,3,2,1,0:T(8,128)(2,1)}, bf16[4,2,2,128,512]{4,3,2,1,0:T(8,128)(2,1)}) custom-call(s32[1]{0:T(128)} %bitcast.16.place, bf16[4,2,2,512,512]{4,3,2,1,0:T(8,128)(2,1)} %green.3, f32[4,2,512]{2,1,0:T(2,128)} %gamma.3), custom_call_target="tpu_custom_call" | custom-call | flops 4294967296 | bytes 12582912 | tf_op jit(solution)/shard_map/lesser/pallas_call | solution.py:64
  12.9 162.3 %exchange.1 = (bf16[4,8,2,2,128,512]{5,4,3,2,1,0:T(8,128)(2,1)}, bf16[4,2,512,512]{3,2,1,0:T(8,128)(2,1)}, bf16[4,2,512,512]{3,2,1,0:T(8,128)(2,1)}) custom-call(s32[4]{0:T(128)} %shift_steps.1, f32[4]{0:T(128)} %mode_weight.1, f32[4]{0:T(128)} %occupation.1, s32[16,16]{1,0:T(8,128)} %select_reduce_fusion.table, ...), custom_call_target="tpu_custom_call" | custom-call | tf_op jit(solution)/shard_map/exchange/pallas_call | solution.py:385
  175.2 64.7 %finish.1 = (bf16[16,2,2,128,512]{4,3,2,1,0:T(8,128)(2,1)}, f32[16,4,2,512]{3,2,1,0:T(2,128)}) custom-call(s32[16,16]{1,0:T(8,128)} %select_reduce_fusion.table, bf16[4,2,2,512,512]{4,3,2,1,0:T(8,128)(2,1)} %green.3, f32[4,2,512]{2,1,0:T(2,128)} %gamma.3, bf16[4,2,512,512]{3,2,1,0:T(8,128)(2,1)} %get-tuple-element.9.us, ...), custom_call_target="tpu_custom_call" | custom-call | tf_op jit(solution)/shard_map/finish/pallas_call | solution.py:570
  239.9 0.0 copy-start
  239.9 7.8 %copy.11 = bf16[16,2,2,128,512]{4,3,2,1,0:T(8,128)(2,1)} copy(bf16[16,2,2,128,512]{4,3,2,1,0:T(8,128)(2,1)} %get-tuple-element.14) | data formatting | bytes 16777216
  247.7 0.0 copy-done
  247.7 0.7 copy.12
Async XLA Ops:
  239.9 7.8 %copy-start = (f32[16,4,2,512]{3,2,1,0:T(2,128)S(1)}, f32[16,4,2,512]{3,2,1,0:T(2,128)}, u32[]{:S(2)}) copy-start(f32[16,4,2,512]{3,2,1,0:T(2,128)} %get-tuple-element.15) | copy-start | bytes 786436

commit v10 on v9

--- a/solution.py
+++ b/solution.py
@@ -342,16 +342,16 @@
         taken[c].start()
 
     for c in range(chunks):
+        if c > 0:
+            take(c - 1)
+            taken[c - 1].wait()
+            convolve(c - 1)
         for s in (1, 2, 3):
             near[c][s - 1].wait_recv()
             far[c][s].start()
         if c == 0:
             tile_bc.wait_recv()
             fold(3)
-        else:
-            take(c - 1)
-            taken[c - 1].wait()
-            convolve(c - 1)
     take(chunks - 1)
     taken[chunks - 1].wait()
     convolve(chunks - 1)

time: 249 us -> 243 us (0.976)
  Pallas kernels: 238 us -> 231 us
    pallas_call x1, Pallas kernels: 162 us -> 154 us  [exchanged(): pl.pallas_call(exchange_kernel, in_specs=[pl.BlockSpec(memory_space=pltpu...]
where the time goes in v10:
time: 243 us; the launch traced here: 241 us
  Pallas kernels  231 us (95%)
  local copies, waits for them, and re-layouts  8.61 us (4%)
    pallas_call x1, Pallas kernels, exchanged(): pl.pallas_call(exchange_kernel, in_specs=[pl.BlockSpec(memory_space=pltpu...  154 us
    pallas_call x1, Pallas kernels, finished(): pl.pallas_call(functools.partial(finish_kernel, 1.0 / (energies * owners)...  66.2 us
    pallas_call x1, Pallas kernels, packed_lesser(): pl.pallas_call(lesser_kernel, grid_spec=pltpu.PrefetchScalarGridSpec(num_...  10.7 us
    unnamed x4, local copies, waits for them, and re-layouts  8.52 us

profile of v10, /device:TPU:0, one launch (start us, length us, event | category | flops | bytes accessed | tf_op | source)
XLA Modules:
  0.0 241.5 jit_solution(621418372029975343)
XLA Ops:
  0.7 0.1 stack.67
  0.8 1.4 select_reduce_fusion.table
  2.2 10.7 %lesser.1 = (bf16[4,2,2,128,512]{4,3,2,1,0:T(8,128)(2,1)}, bf16[4,2,2,128,512]{4,3,2,1,0:T(8,128)(2,1)}) custom-call(s32[1]{0:T(128)} %bitcast.16.place, bf16[4,2,2,512,512]{4,3,2,1,0:T(8,128)(2,1)} %green.3, f32[4,2,512]{2,1,0:T(2,128)} %gamma.3), custom_call_target="tpu_custom_call" | custom-call | flops 4294967296 | bytes 12582912 | tf_op jit(solution)/shard_map/lesser/pallas_call | solution.py:64
  12.9 153.8 %exchange.1 = (bf16[4,8,2,2,128,512]{5,4,3,2,1,0:T(8,128)(2,1)}, bf16[4,2,512,512]{3,2,1,0:T(8,128)(2,1)}, bf16[4,2,512,512]{3,2,1,0:T(8,128)(2,1)}) custom-call(s32[4]{0:T(128)} %shift_steps.1, f32[4]{0:T(128)} %mode_weight.1, f32[4]{0:T(128)} %occupation.1, s32[16,16]{1,0:T(8,128)} %select_reduce_fusion.table, ...), custom_call_target="tpu_custom_call" | custom-call | tf_op jit(solution)/shard_map/exchange/pallas_call | solution.py:385
  166.7 66.2 %finish.1 = (bf16[16,2,2,128,512]{4,3,2,1,0:T(8,128)(2,1)}, f32[16,4,2,512]{3,2,1,0:T(2,128)}) custom-call(s32[16,16]{1,0:T(8,128)} %select_reduce_fusion.table, bf16[4,2,2,512,512]{4,3,2,1,0:T(8,128)(2,1)} %green.3, f32[4,2,512]{2,1,0:T(2,128)} %gamma.3, bf16[4,2,512,512]{3,2,1,0:T(8,128)(2,1)} %get-tuple-element.9.us, ...), custom_call_target="tpu_custom_call" | custom-call | tf_op jit(solution)/shard_map/finish/pallas_call | solution.py:570
  233.0 0.0 copy-start
  233.0 7.8 %copy.11 = bf16[16,2,2,128,512]{4,3,2,1,0:T(8,128)(2,1)} copy(bf16[16,2,2,128,512]{4,3,2,1,0:T(8,128)(2,1)} %get-tuple-element.14) | data formatting | bytes 16777216
  240.8 0.0 copy-done
  240.8 0.7 copy.12
Async XLA Ops:
  233.0 7.8 %copy-start = (f32[16,4,2,512]{3,2,1,0:T(2,128)S(1)}, f32[16,4,2,512]{3,2,1,0:T(2,128)}, u32[]{:S(2)}) copy-start(f32[16,4,2,512]{3,2,1,0:T(2,128)} %get-tuple-element.15) | copy-start | bytes 786436
